TPU v7x, 32 devices: a whole 2x2x4 slice. The times are simulated.
32 devices in a mesh: dp: 8 (over z, x), row: 2 (over core), col: 2 (over y).
Axes of the slice: x: 2, y: 2, z: 4, core: 2. Of those that a mesh axis runs over, the one named last changes fastest.
Arguments:
- tokens: bfloat16 [3136, 512], P(('dp', 'row'), 'col'), may hold values from -6 to 6
- cotangent: bfloat16 [3136, 512], P(('dp', 'row'), 'col'), may hold values from -12 to 12
- qkv_weight: bfloat16 [2, 512, 3, 512], P(None, 'col', None, 'row'), may hold values from -0.25 to 0.25
- qv_bias: bfloat16 [2, 2, 512], P(None, None, 'row'), may hold values from -3 to 3
- out_weight: bfloat16 [2, 512, 512], P(None, 'row', 'col'), may hold values from -1 to 1
- out_bias: bfloat16 [2, 512], P(None, 'col'), may hold values from -3 to 3
- up_weight: bfloat16 [2, 512, 2048], P(None, 'col', 'row'), may hold values from -0.25 to 0.25
- up_bias: bfloat16 [2, 2048], P(None, 'row'), may hold values from -3 to 3
- down_weight: bfloat16 [2, 2048, 512], P(None, 'row', 'col'), may hold values from -0.125 to 0.125
- down_bias: bfloat16 [2, 512], P(None, 'col'), may hold values from -3 to 3
- norm_gain: bfloat16 [2, 2, 512], P(None, None, 'col'), may hold values from 0.5 to 1.5
- norm_shift: bfloat16 [2, 2, 512], P(None, None, 'col'), may hold values from -3 to 3
- bias_table: bfloat16 [2, 169, 16], P(None, None, 'row'), may hold values from -4 to 4
- index_map: int32 [49, 49], replicated, may hold values from 0 to 168
- region_ids: int32 [196], replicated, may hold values from 0 to 3
Outputs:
- output: bfloat16 [3136, 512], P(('dp', 'row'), 'col')
- input_grad: bfloat16 [3136, 512], P(('dp', 'row'), 'col')
- grad_qkv_weight: float32 [2, 512, 3, 512], P(None, 'col', None, 'row')
- grad_qv_bias: float32 [2, 2, 512], P(None, None, 'row')
- grad_out_weight: float32 [2, 512, 512], P(None, 'row', 'col')
- grad_out_bias: float32 [2, 512], P(None, 'col')
- grad_up_weight: float32 [2, 512, 2048], P(None, 'col', 'row')
- grad_up_bias: float32 [2, 2048], P(None, 'row')
- grad_down_weight: float32 [2, 2048, 512], P(None, 'row', 'col')
- grad_down_bias: float32 [2, 512], P(None, 'col')
- grad_norm_gain: float32 [2, 2, 512], P(None, None, 'col')
- grad_norm_shift: float32 [2, 2, 512], P(None, None, 'col')
- grad_bias_table: float32 [2, 169, 16], P(None, None, 'row')
All inputs are finite; a program needn't handle non-finite values.
Results may differ from a plain program's by a relative error of at most 0.03.
Values may be sent and summed in bfloat16 or wider, within the bound.
No kernel may reach another device: no remote copies, remote signals or barrier semaphores. Data moves between devices by JAX's collectives and lax.ppermute only.
A program may use at most 128 MiB of HBM per device.

v0:
```python
import math

import jax
import jax.numpy as jnp
from jax import lax
from jax.sharding import PartitionSpec as P

D = 512
HEADS = 16
HEAD_DIM = 32
FF = 2048
GRID = 14
WINDOW = 7
SHIFT = 3
TABLE = 169
LAYERS = 2


EPS = 1e-05
NEG = -1000000000.0
HIGH = lax.Precision.HIGHEST


def contract(left, right, dims):
    return lax.dot_general(left, right, (dims, ((), ())), preferred_element_type=jnp.float32)


def row_gather(values):
    return lax.all_gather(values, "row", axis=0, tiled=True)


def col_sum(pieces):
    return lax.psum_scatter(
        pieces.astype(jnp.bfloat16), "col", scatter_dimension=0, tiled=True
    ).astype(jnp.float32)


def col_gather(values):
    return lax.all_gather(values, "col", axis=0, tiled=True)


def row_sum(pieces):
    return lax.psum_scatter(
        pieces.astype(jnp.bfloat16), "row", scatter_dimension=0, tiled=True
    ).astype(jnp.float32)


def back_row_gather(values):
    return lax.all_gather(values, "row", axis=0, tiled=True)


def back_col_sum(pieces):
    return lax.psum_scatter(
        pieces.astype(jnp.bfloat16), "col", scatter_dimension=0, tiled=True
    ).astype(jnp.float32)


def back_col_gather(values):
    return lax.all_gather(values, "col", axis=0, tiled=True)


def back_row_sum(pieces):
    return lax.psum_scatter(
        pieces.astype(jnp.bfloat16), "row", scatter_dimension=0, tiled=True
    ).astype(jnp.float32)


def norm_forward(residual, norm_scale, norm_offset):
    total_one, total_two = lax.psum((jnp.sum(residual, 1), jnp.sum(residual * residual, 1)), "col")
    average = total_one / D
    variance = total_two / D - average * average
    inverse = lax.rsqrt(variance + EPS)
    centred = (residual - average[:, None]) * inverse[:, None]
    return (centred * norm_scale + norm_offset, centred, inverse)


def norm_backward(grad_normed, centred, inverse, norm_scale):
    scaled = grad_normed * norm_scale
    total_one, total_two = lax.psum((jnp.sum(scaled, 1), jnp.sum(scaled * centred, 1)), "col")
    grad_input = inverse[:, None] * (
        scaled - total_one[:, None] / D - centred * (total_two[:, None] / D)
    )
    return (grad_input, jnp.sum(grad_normed * centred, 0), jnp.sum(grad_normed, 0))


def gelu_slope(values):
    return 0.5 * (1.0 + lax.erf(values / math.sqrt(2.0))) + values * jnp.exp(
        -0.5 * values * values
    ) / math.sqrt(2.0 * math.pi)


def to_windows(values, images, shifted):
    per_side = GRID // WINDOW
    channels = values.shape[-1]
    laid_out = values.reshape(images, GRID, GRID, channels)
    if shifted:
        laid_out = jnp.roll(laid_out, (-SHIFT, -SHIFT), (1, 2))
    laid_out = laid_out.reshape(images, per_side, WINDOW, per_side, WINDOW, channels).transpose(
        0, 1, 3, 2, 4, 5
    )
    return laid_out.reshape(images * per_side * per_side, WINDOW * WINDOW, channels)


def from_windows(values, images, shifted):
    per_side = GRID // WINDOW
    channels = values.shape[-1]
    laid_out = values.reshape(images, per_side, per_side, WINDOW, WINDOW, channels).transpose(
        0, 1, 3, 2, 4, 5
    )
    laid_out = laid_out.reshape(images, GRID, GRID, channels)
    if shifted:
        laid_out = jnp.roll(laid_out, (SHIFT, SHIFT), (1, 2))
    return laid_out.reshape(images * GRID * GRID, channels)


def region_windows(region_ids):
    per_side = GRID // WINDOW
    laid_out = region_ids.reshape(per_side, WINDOW, per_side, WINDOW).transpose(0, 2, 1, 3)
    return laid_out.reshape(per_side * per_side, WINDOW * WINDOW)


def window_setup(qkv, table_part, index_map, region_ids, shifted):
    images = qkv.shape[0] // (GRID * GRID)
    heads = qkv.shape[1] // (3 * HEAD_DIM)
    span = WINDOW * WINDOW
    windows = to_windows(qkv, images, shifted).reshape(-1, span, 3, heads, HEAD_DIM)
    query_win = windows[:, :, 0]
    key_win = windows[:, :, 1]
    value_win = windows[:, :, 2]
    one_hot = (
        index_map.reshape(-1)[:, None] == jnp.arange(TABLE, dtype=jnp.int32)[None, :]
    ).astype(jnp.float32)
    bias_heads = (
        jnp.dot(one_hot, table_part.astype(jnp.float32), precision=HIGH)
        .reshape(span, span, heads)
        .transpose(2, 0, 1)
    )
    scores = jnp.einsum(
        "bihd,bjhd->bhij", query_win, key_win, preferred_element_type=jnp.float32
    ) / math.sqrt(HEAD_DIM)
    scores = scores + bias_heads[None]
    if shifted:
        window_ids = region_windows(region_ids)
        allowed = window_ids[:, :, None] == window_ids[:, None, :]
        scores = scores.reshape(images, -1, heads, span, span)
        scores = jnp.where(allowed[None, :, None], scores, NEG)
        scores = scores.reshape(-1, heads, span, span)
    return (query_win, key_win, value_win, scores, one_hot, images)


def attend_forward(qkv, table_part, index_map, region_ids, shifted):
    query_win, key_win, value_win, scores, one_hot, images = window_setup(
        qkv, table_part, index_map, region_ids, shifted
    )
    peak = jnp.max(scores, -1, keepdims=True)
    expos = jnp.exp(scores - peak)
    totals = jnp.sum(expos, -1, keepdims=True)
    probs = expos / totals
    log_total = peak[..., 0] + jnp.log(totals[..., 0])
    output_win = jnp.einsum(
        "bhij,bjhd->bihd", probs.astype(jnp.bfloat16), value_win, preferred_element_type=jnp.float32
    )
    merged = from_windows(
        output_win.reshape(output_win.shape[0], output_win.shape[1], -1), images, shifted
    )
    return (merged, log_total)


def attend_backward(qkv, log_total, grad_out, table_part, index_map, region_ids, shifted):
    query_win, key_win, value_win, scores, one_hot, images = window_setup(
        qkv, table_part, index_map, region_ids, shifted
    )
    heads = query_win.shape[2]
    span = WINDOW * WINDOW
    grad_win = to_windows(grad_out.astype(jnp.bfloat16), images, shifted).reshape(
        -1, span, heads, HEAD_DIM
    )
    probs = jnp.exp(scores - log_total[..., None])
    grad_value = jnp.einsum(
        "bhij,bihd->bjhd", probs.astype(jnp.bfloat16), grad_win, preferred_element_type=jnp.float32
    )
    grad_probs = jnp.einsum(
        "bihd,bjhd->bhij", grad_win, value_win, preferred_element_type=jnp.float32
    )
    weighted = jnp.sum(probs * grad_probs, -1, keepdims=True)
    grad_scores = (probs * (grad_probs - weighted)).astype(jnp.bfloat16)
    grad_query = jnp.einsum(
        "bhij,bjhd->bihd", grad_scores, key_win, preferred_element_type=jnp.float32
    ) / math.sqrt(HEAD_DIM)
    grad_key = jnp.einsum(
        "bhij,bihd->bjhd", grad_scores, query_win, preferred_element_type=jnp.float32
    ) / math.sqrt(HEAD_DIM)
    stacked = (
        jnp.stack([grad_query, grad_key, grad_value], 2)
        .astype(jnp.bfloat16)
        .reshape(-1, span, 3 * heads * HEAD_DIM)
    )
    grads = from_windows(stacked, images, shifted)
    column_sums = jnp.sum(grads.astype(jnp.float32), 0).reshape(3, -1)
    qv_grad = jnp.stack([column_sums[0], column_sums[2]])
    summed = jnp.sum(grad_scores.astype(jnp.float32), 0).reshape(heads, span * span)
    table_grad = jnp.einsum("hk,kn->nh", summed, one_hot, precision=HIGH)
    return (grads, table_grad, qv_grad)


def embed_block(values, start, full_size, axis):
    holder = jnp.zeros(values.shape[:axis] + (full_size,) + values.shape[axis + 1 :], jnp.float32)
    return lax.dynamic_update_slice_in_dim(holder, values, start, axis)


def on_device(
    tokens,
    cotangent,
    qkv_weight,
    qv_bias,
    out_weight,
    out_bias,
    up_weight,
    up_bias,
    down_weight,
    down_bias,
    norm_gain,
    norm_shift,
    bias_table,
    index_map,
    region_ids,
):
    col_width = tokens.shape[1]
    row_width = qv_bias.shape[2]
    hidden_width = up_bias.shape[1]
    head_count = bias_table.shape[2]
    residual = tokens.astype(jnp.float32)
    saved = []
    for layer in range(LAYERS):
        shifted = layer % 2 == 1
        weight_qkv = qkv_weight[layer].reshape(col_width, -1)
        normed, centred_one, inverse_one = norm_forward(
            residual,
            norm_gain[layer, 0].astype(jnp.float32),
            norm_shift[layer, 0].astype(jnp.float32),
        )
        normed_one = row_gather(normed.astype(jnp.bfloat16))
        projected = col_sum(contract(normed_one, weight_qkv, ((1,), (0,))))
        bias_three = (
            jnp.stack([qv_bias[layer, 0], jnp.zeros_like(qv_bias[layer, 0]), qv_bias[layer, 1]])
            .astype(jnp.float32)
            .reshape(-1)
        )
        qkv = (projected + bias_three).astype(jnp.bfloat16)
        attended, log_total = attend_forward(qkv, bias_table[layer], index_map, region_ids, shifted)
        attended_all = col_gather(attended.astype(jnp.bfloat16))
        mixed = contract(attended_all, out_weight[layer], ((1,), (0,)))
        out_shift = out_bias[layer].astype(jnp.float32)
        gain_two = norm_gain[layer, 1].astype(jnp.float32)
        shift_two = norm_shift[layer, 1].astype(jnp.float32)
        middle = residual + row_sum(mixed) + out_shift
        normed_mid, centred_two, inverse_two = norm_forward(middle, gain_two, shift_two)
        normed_two = row_gather(normed_mid.astype(jnp.bfloat16))
        before = col_sum(contract(normed_two, up_weight[layer], ((1,), (0,)))) + up_bias[
            layer
        ].astype(jnp.float32)
        hidden_all = col_gather(jax.nn.gelu(before, approximate=False).astype(jnp.bfloat16))
        residual = (
            middle
            + row_sum(contract(hidden_all, down_weight[layer], ((1,), (0,))))
            + down_bias[layer].astype(jnp.float32)
        )
        saved.append(
            (
                centred_one,
                inverse_one,
                normed_one,
                qkv,
                log_total,
                attended_all,
                centred_two,
                inverse_two,
                normed_two,
                before,
                hidden_all,
            )
        )
    output = residual.astype(jnp.bfloat16)
    grad = cotangent.astype(jnp.float32)
    weight_records = [None] * LAYERS
    col_records = [None] * LAYERS
    row_records = [None] * LAYERS
    for layer in reversed(range(LAYERS)):
        shifted = layer % 2 == 1
        (
            centred_one,
            inverse_one,
            normed_one,
            qkv,
            log_total,
            attended_all,
            centred_two,
            inverse_two,
            normed_two,
            before,
            hidden_all,
        ) = saved[layer]
        weight_qkv = qkv_weight[layer].reshape(col_width, -1)
        grad_down = grad.astype(jnp.bfloat16)
        grad_down_bias = jnp.sum(grad_down.astype(jnp.float32), 0)
        grad_down_all = back_row_gather(grad_down)
        grad_down_weight = contract(hidden_all, grad_down_all, ((0,), (0,)))
        grad_hidden = back_col_sum(contract(grad_down_all, down_weight[layer], ((1,), (1,))))
        grad_pre = (grad_hidden * gelu_slope(before)).astype(jnp.bfloat16)
        grad_up_bias = jnp.sum(grad_pre.astype(jnp.float32), 0)
        grad_pre_all = back_col_gather(grad_pre)
        grad_up_weight = contract(normed_two, grad_pre_all, ((0,), (0,)))
        grad_normed = back_row_sum(contract(grad_pre_all, up_weight[layer], ((1,), (1,))))
        grad_mid, gain_grad_two, shift_grad_two = norm_backward(
            grad_normed, centred_two, inverse_two, norm_gain[layer, 1].astype(jnp.float32)
        )
        grad_mid = grad + grad_mid
        grad_att = grad_mid.astype(jnp.bfloat16)
        grad_out_bias = jnp.sum(grad_att.astype(jnp.float32), 0)
        grad_att_all = back_row_gather(grad_att)
        grad_out_weight = contract(attended_all, grad_att_all, ((0,), (0,)))
        grad_attended = back_col_sum(contract(grad_att_all, out_weight[layer], ((1,), (1,))))
        grad_qkv, grad_table, grad_qv = attend_backward(
            qkv, log_total, grad_attended, bias_table[layer], index_map, region_ids, shifted
        )
        grad_qkv_all = back_col_gather(grad_qkv)
        grad_qkv_weight = contract(normed_one, grad_qkv_all, ((0,), (0,))).reshape(
            qkv_weight.shape[1:]
        )
        grad_normed_one = back_row_sum(contract(grad_qkv_all, weight_qkv, ((1,), (1,))))
        grad_input, gain_grad_one, shift_grad_one = norm_backward(
            grad_normed_one, centred_one, inverse_one, norm_gain[layer, 0].astype(jnp.float32)
        )
        grad = grad_mid + grad_input
        weight_records[layer] = (grad_qkv_weight, grad_out_weight, grad_up_weight, grad_down_weight)
        col_records[layer] = jnp.stack(
            [
                gain_grad_one,
                gain_grad_two,
                shift_grad_one,
                shift_grad_two,
                grad_out_bias,
                grad_down_bias,
            ]
        )
        row_records[layer] = (grad_qv, grad_up_bias, grad_table)
    input_grad = grad.astype(jnp.bfloat16)
    qkv_stack = jnp.stack([record[0] for record in weight_records])
    out_stack = jnp.stack([record[1] for record in weight_records])
    up_stack = jnp.stack([record[2] for record in weight_records])
    down_stack = jnp.stack([record[3] for record in weight_records])
    grad_qkv_weight, grad_out_weight, grad_up_weight, grad_down_weight = lax.psum(
        (qkv_stack, out_stack, up_stack, down_stack), "dp"
    )
    col_feature_start = lax.axis_index("col") * col_width
    row_feature_start = lax.axis_index("row") * row_width
    col_full = embed_block(jnp.stack(col_records), col_feature_start, D, 2)
    qv_full = embed_block(jnp.stack([record[0] for record in row_records]), row_feature_start, D, 2)
    up_bias_full = embed_block(
        jnp.stack([record[1] for record in row_records]),
        lax.axis_index("row") * hidden_width,
        FF,
        1,
    )
    table_full = embed_block(
        jnp.stack([record[2] for record in row_records]),
        lax.axis_index("row") * head_count,
        HEADS,
        2,
    )
    col_total, qv_total, up_total, table_total = lax.psum(
        (col_full, qv_full, up_bias_full, table_full), ("dp", "row", "col")
    )
    col_part = lax.dynamic_slice_in_dim(col_total, col_feature_start, col_width, 2)
    grad_qv_bias = lax.dynamic_slice_in_dim(qv_total, row_feature_start, row_width, 2)
    grad_up_bias = lax.dynamic_slice_in_dim(
        up_total, lax.axis_index("row") * hidden_width, hidden_width, 1
    )
    grad_bias_table = lax.dynamic_slice_in_dim(
        table_total, lax.axis_index("row") * head_count, head_count, 2
    )
    grad_norm_gain = col_part[:, 0:2]
    grad_norm_shift = col_part[:, 2:4]
    grad_out_bias = col_part[:, 4]
    grad_down_bias = col_part[:, 5]
    return (
        output,
        input_grad,
        grad_qkv_weight,
        grad_qv_bias,
        grad_out_weight,
        grad_out_bias,
        grad_up_weight,
        grad_up_bias,
        grad_down_weight,
        grad_down_bias,
        grad_norm_gain,
        grad_norm_shift,
        grad_bias_table,
    )


def solution(mesh):
    in_specs = (
        P(("dp", "row"), "col"),
        P(("dp", "row"), "col"),
        P(None, "col", None, "row"),
        P(None, None, "row"),
        P(None, "row", "col"),
        P(None, "col"),
        P(None, "col", "row"),
        P(None, "row"),
        P(None, "row", "col"),
        P(None, "col"),
        P(None, None, "col"),
        P(None, None, "col"),
        P(None, None, "row"),
        P(),
        P(),
    )
    out_specs = (
        P(("dp", "row"), "col"),
        P(("dp", "row"), "col"),
        P(None, "col", None, "row"),
        P(None, None, "row"),
        P(None, "row", "col"),
        P(None, "col"),
        P(None, "col", "row"),
        P(None, "row"),
        P(None, "row", "col"),
        P(None, "col"),
        P(None, None, "col"),
        P(None, None, "col"),
        P(None, None, "row"),
    )
    return jax.shard_map(
        on_device, mesh=mesh, in_specs=in_specs, out_specs=out_specs, check_vma=False
    )
```

profile of v0, /device:TPU:0, one launch (start us, length us, event | category | flops | bytes accessed | tf_op | source)
XLA Modules:
  0.0 798.0 jit_solution(4987176507893806571)
XLA Ops:
  10.9 5.8 all-reduce.41
  23.0 13.0 %fusion = bf16[200,768]{1,0:T(8,128)(2,1)S(1)} fusion(bf16[392,768]{1,0:T(8,128)(2,1)S(1)} %convolution_convert_fusion.5), kind=kCustom, calls=%all-reduce-scatter | all-reduce-scatter fusion | flops 307201 | bytes 909824
  51.0 5.6 all-gather.1
  64.5 4.9 all-reduce.40
  72.0 13.3 %fusion.2 = bf16[200,1024]{1,0:T(8,128)(2,1)S(1)} fusion(bf16[392,1024]{1,0:T(8,128)(2,1)S(1)} %convolution_convert_fusion.3), kind=kCustom, calls=%all-reduce-scatter.2 | all-reduce-scatter fusion | flops 409601 | bytes 1212928
  92.9 10.6 %all-gather.3 = bf16[2,196,1024]{2,1,0:T(8,128)(2,1)S(1)} all-gather(bf16[1,196,1024]{2,1,0:T(8,128)(2,1)S(1)} %fusion.112), channel_id=1, replica_groups=mesh['dp'=8,'row'=2,'col'=2] {'col'}, dimensions={0}, use_global_device_ids=true | all-gather | bytes 1204224 | tf_op jit(solution)/shard_map/all_gather | solution.py:39
  112.3 4.9 all-reduce.39
  119.7 12.5 %fusion.4 = bf16[200,768]{1,0:T(8,128)(2,1)S(1)} fusion(bf16[392,768]{1,0:T(8,128)(2,1)S(1)} %convolution_convert_fusion.4), kind=kCustom, calls=%all-reduce-scatter.4 | all-reduce-scatter fusion | flops 307201 | bytes 909824
  152.7 5.4 all-gather.5
  160.0 3.7 fusion.5
  167.9 4.9 all-reduce.38
  179.1 24.0 %fusion.189 = (bf16[200,1024]{1,0:T(8,128)(2,1)}, bf16[200,1024]{1,0:T(8,128)(2,1)}) fusion(bf16[392,1024]{1,0:T(8,128)(2,1)} %convolution_convert_fusion.2, bf16[392,1024]{1,0:T(8,128)(2,1)} %convolution_convert_fusion.1), kind=kCustom, calls=%all-reduce-scatter.16 | all-reduce-scatter fusion | flops 819201 | bytes 2425344
  208.2 3.8 concatenate.57
  212.1 3.8 concatenate.55
  215.9 4.7 convert_reduce_fusion.2
  220.6 11.5 %all-gather.7 = bf16[2,196,1024]{2,1,0:T(8,128)(2,1)} all-gather(bf16[1,196,1024]{2,1,0:T(8,128)(2,1)S(1)} %get-tuple-element.134), channel_id=1, replica_groups=mesh['dp'=8,'row'=2,'col'=2] {'col'}, dimensions={0}, use_global_device_ids=true | all-gather | bytes 1204224 | tf_op jit(solution)/shard_map/all_gather | solution.py:39
  239.3 10.0 %all-gather.9 = bf16[2,196,1024]{2,1,0:T(8,128)(2,1)} all-gather(bf16[1,196,1024]{2,1,0:T(8,128)(2,1)S(1)} %bitcast.338), channel_id=1, replica_groups=mesh['dp'=8,'row'=2,'col'=2] {'col'}, dimensions={0}, use_global_device_ids=true | all-gather | bytes 1204224 | tf_op jit(solution)/shard_map/all_gather | solution.py:59
  254.0 3.7 fusion.9
  263.8 4.9 all-reduce.37
  276.1 7.8 fusion.10
  308.1 8.5 %all-gather.11 = bf16[2,196,768]{2,1,0:T(8,128)(2,1)S(1)} all-gather(bf16[1,196,768]{2,1,0:T(8,128)(2,1)} %reshape.323), channel_id=1, replica_groups=mesh['dp'=8,'row'=2,'col'=2] {'col'}, dimensions={0}, use_global_device_ids=true | all-gather | bytes 903168 | tf_op jit(solution)/shard_map/all_gather | solution.py:59
  326.7 4.9 all-reduce.36
  339.9 15.3 %fusion.12 = bf16[200,1024]{1,0:T(8,128)(2,1)} fusion(bf16[392,1024]{1,0:T(8,128)(2,1)} %convolution_convert_fusion), kind=kCustom, calls=%all-reduce-scatter.12 | all-reduce-scatter fusion | flops 409601 | bytes 1212928
  365.7 10.8 %all-gather.13 = bf16[2,196,1024]{2,1,0:T(8,128)(2,1)S(1)} all-gather(bf16[1,196,1024]{2,1,0:T(8,128)(2,1)S(1)} %bitcast.339), channel_id=1, replica_groups=mesh['dp'=8,'row'=2,'col'=2] {'col'}, dimensions={0}, use_global_device_ids=true | all-gather | bytes 1204224 | tf_op jit(solution)/shard_map/all_gather | solution.py:59
  381.5 3.7 fusion.13
  392.7 4.9 all-reduce.35
  401.9 6.7 fusion.14
  419.6 7.9 all-gather.15
  430.4 3.8 fusion.190
  443.1 4.9 all-reduce.34
  449.5 112.0 %all-reduce.47.cloned.1.call-done = (f32[2,2,512]{2,1,0:T(2,128)}, f32[2,6,512]{2,1,0:T(8,128)}, f32[2,2048]{1,0:T(2,128)}, f32[2,169,16]{1,2,0:T(8,128)}) async-done(((f32[2,2,512]{2,1,0:T(2,128)}, f32[2,6,512]{2,1,0:T(8,128)}, f32[2,2048]{1,0:T(2,128)}, f32[2,169,16]{1,2,0:T(8,128)}), (f32[2,2,512]{2,1,0:T(2,128)}, f32[2,6,512]{2,1,0:T(8,128)}, f32[2,2048]{1,0:T(2,128)}, ...) | async-done | bytes 70800 | tf_op jit(solution)/shard_map/psum | solution.py:371
  568.9 214.2 %all-reduce.49.cloned.1.call-done = (f32[2,256,3,256]{1,3,2,0:T(8,128)}, f32[2,256,256]{2,1,0:T(8,128)}, f32[2,256,1024]{2,1,0:T(8,128)}, f32[2,1024,256]{2,1,0:T(8,128)}) async-done(((f32[2,256,3,256]{1,3,2,0:T(8,128)}, f32[2,256,256]{2,1,0:T(8,128)}, f32[2,256,1024]{2,1,0:T(8,128)}, f32[2,1024,256]{2,1,0:T(8,128)}), (f32[2,256,3,256]{1,3,2,0:T(8,128)}, f32[2,256,256]{2,1,0:T(8,128)}, ...) | async-done | bytes 6291472 | tf_op jit(solution)/shard_map/psum | solution.py:352
  (497 shorter events, 223.2 us)
Async XLA Ops:
  7.2 554.3 %all-reduce.47.cloned.1.call-start = ((), (), s32[]{:S(2)}) async-start(), calls=%async_computation | async-start | bytes 180224 | tf_op jit(solution)/shard_map/psum | solution.py:371
  9.6 59.9 %copy-start.76 = (f32[1,1,256]{2,1,0:T(1,128)}, f32[1,1,256]{2,1,0:T(1,128)S(1)}, u32[]{:S(2)}) copy-start(f32[1,1,256]{2,1,0:T(1,128)S(1)} %get-tuple-element.147) | copy-start | bytes 3076
  9.6 107.6 %copy-start.77 = (f32[1,1,256]{2,1,0:T(1,128)}, f32[1,1,256]{2,1,0:T(1,128)S(1)}, u32[]{:S(2)}) copy-start(f32[1,1,256]{2,1,0:T(1,128)S(1)} %get-tuple-element.149) | copy-start | bytes 3076
  36.0 9.4 %collective-permute-start = (bf16[4,768]{1,0:T(4,128)(2,1)S(1)}, bf16[4,768]{1,0:T(4,128)(2,1)S(1)}, u32[]{:S(2)}, u32[]{:S(2)}) collective-permute-start(bf16[4,768]{1,0:T(4,128)(2,1)S(1)} %slice.308), channel_id=1, source_target_pairs={{0,1},{2,3},{4,5},{6,7},{8,9},{10,11},{12,13},{14,15},{16,17},{18,... | collective-permute-start | bytes 18440
  50.6 21.0 %copy-start.36 = (bf16[2,256,1024]{2,1,0:T(8,128)(2,1)S(1)}, bf16[2,256,1024]{2,1,0:T(8,128)(2,1)}, u32[]{:S(2)}) copy-start(bf16[2,256,1024]{2,1,0:T(8,128)(2,1)} %param.21) | copy-start | bytes 3145732
  59.9 4.1 collective-permute-start.1
  64.0 25.0 %copy-start.84 = (bf16[2,1024]{1,0:T(2,128)(2,1)S(1)}, bf16[2,1024]{1,0:T(2,128)(2,1)}, u32[]{:S(2)}) copy-start(bf16[2,1024]{1,0:T(2,128)(2,1)} %param.22) | copy-start | bytes 12292
  69.5 21.5 %copy-start.67 = (f32[196]{0:T(256)}, f32[196]{0:T(256)S(1)}, u32[]{:S(2)}) copy-start(f32[196]{0:T(256)S(1)} %get-tuple-element.164) | copy-start | bytes 2356
  69.5 21.5 %copy-start.69 = (f32[196]{0:T(256)}, f32[196]{0:T(256)S(1)}, u32[]{:S(2)}) copy-start(f32[196]{0:T(256)S(1)} %get-tuple-element.165) | copy-start | bytes 2356
  71.6 21.3 %copy-start.27 = (bf16[392,256]{1,0:T(8,128)(2,1)}, bf16[392,256]{1,0:T(8,128)(2,1)S(1)}, u32[]{:S(2)}) copy-start(bf16[392,256]{1,0:T(8,128)(2,1)S(1)} %reshape.306) | copy-start | bytes 602116
  85.4 5.0 collective-permute-start.2
  108.5 3.2 collective-permute-start.3
  132.3 5.4 collective-permute-start.4
  151.4 21.4 %copy-start.79 = (f32[1,1,256]{2,1,0:T(1,128)S(1)}, f32[1,1,256]{2,1,0:T(1,128)}, u32[]{:S(2)}) copy-start(f32[1,1,256]{2,1,0:T(1,128)} %get-tuple-element.146) | copy-start | bytes 3076
  163.7 3.1 collective-permute-start.5
  175.7 32.4 %copy-start.57 = (f32[4,8,49]{2,1,0:T(8,128)S(1)}, f32[4,8,49]{2,1,0:T(8,128)}, u32[]{:S(2)}) copy-start(f32[4,8,49]{2,1,0:T(8,128)} %copy-done.56) | copy-start | bytes 18820
  176.7 35.3 %copy-start.30 = (bf16[392,256]{1,0:T(8,128)(2,1)}, bf16[392,256]{1,0:T(8,128)(2,1)S(1)}, u32[]{:S(2)}) copy-start(bf16[392,256]{1,0:T(8,128)(2,1)S(1)} %reshape.314) | copy-start | bytes 602116
  179.1 36.8 %copy-start.81 = (f32[1,1024]{1,0:T(1,128)S(1)}, f32[1,1024]{1,0:T(1,128)}, u32[]{:S(2)}) copy-start(f32[1,1024]{1,0:T(1,128)} %get-tuple-element.144) | copy-start | bytes 12292
  204.6 3.7 collective-permute-start.8
  206.9 5.2 collective-permute-start.6
  257.7 4.9 collective-permute-start.9
  270.4 24.8 %copy-start.17 = (f32[196,256]{1,0:T(8,128)}, f32[196,256]{1,0:T(8,128)S(1)}, u32[]{:S(2)}) copy-start(f32[196,256]{1,0:T(8,128)S(1)} %get-tuple-element.121) | copy-start | bytes 602116
  283.9 5.1 collective-permute-start.10
  321.7 4.4 collective-permute-start.11
  335.8 23.7 %copy-start.2 = (f32[1,1024,256]{2,1,0:T(8,128)S(1)}, f32[1,1024,256]{2,1,0:T(8,128)}, u32[]{:S(2)}) copy-start(f32[1,1024,256]{2,1,0:T(8,128)} %convolution_bitcast_fusion) | copy-start | bytes 3145732
  355.9 5.6 collective-permute-start.12
  385.3 5.0 collective-permute-start.13
  389.5 22.7 %copy-start.43 = (f32[1,256,256]{2,1,0:T(8,128)S(1)}, f32[1,256,256]{2,1,0:T(8,128)}, u32[]{:S(2)}) copy-start(f32[1,256,256]{2,1,0:T(8,128)} %convolution_bitcast_fusion.5) | copy-start | bytes 786436
  408.6 4.9 collective-permute-start.14
  434.3 2.9 collective-permute-start.15
  438.4 344.7 %all-reduce.49.cloned.1.call-start = ((), (), s32[]{:S(2)}) async-start(), calls=%async_computation.1 | async-start | bytes 12582912 | tf_op jit(solution)/shard_map/psum | solution.py:352
  439.8 3.1 collective-permute-start.7
  (89 other events, 725.7 us)
Sparse Core Ops, SparseCore 0:
  438.5 122.9 all-reduce.46
  567.1 215.9 all-reduce.48
where the time goes:
time: 810 us; the launch traced here: 798 us
  waiting for transfers between devices  330 us (41%)
  blocking collectives  243 us (30%)
  local copies, waits for them, and re-layouts  84.5 us (10%)
  matrix products  45.1 us (6%)
  starting transfers between devices  40.4 us (5%)
  other arithmetic  37.2 us (5%)
  between operations  18 us (2%)
    psum x1, waiting for transfers between devices, on_device(): lax.psum((qkv_stack, out_stack, up_stack, down_stack), 'dp')  214 us
    unnamed x14, blocking collectives  116 us
    psum x1, waiting for transfers between devices, on_device(): lax.psum((col_full, qv_full, up_bias_full, table_full), ('dp', 'row', 'co...  112 us
    unnamed x276, local copies, waits for them, and re-layouts  51.5 us
    unnamed x16, starting transfers between devices  40.3 us
    all_gather x4, blocking collectives, back_col_gather(): return lax.all_gather(values, 'col', axis=0, tiled=True)  37.2 us
    dot_general x24, matrix products, contract(): lax.dot_general(left, right, (dims, ((), ())), preferred_element_type=jnp...  33.3 us
    all_gather x4, blocking collectives, col_gather(): return lax.all_gather(values, 'col', axis=0, tiled=True)  33.2 us
  transfers between devices with their start and end apart: 18, of which 7 were waited for; matrix products, arithmetic and copies ran while one was open for 4% of the time, Pallas kernels for 0%

commit v1 on v0

v1 whole, which is shorter than its diff:
```python
import math

import jax
import jax.numpy as jnp
import numpy as np
from jax import lax
from jax.experimental import pallas as pl
from jax.experimental.pallas import tpu as pltpu
from jax.sharding import PartitionSpec as P

D = 512
HEADS = 16
HEAD_DIM = 32
FF = 2048
GRID = 14
WINDOW = 7
SHIFT = 3
TABLE = 169
LAYERS = 2
SPAN = WINDOW * WINDOW
IMAGE = GRID * GRID

EPS = 1e-05
NEG = -1000000000.0
HIGH = lax.Precision.HIGHEST
SCALE = 1.0 / math.sqrt(HEAD_DIM)

HALF = IMAGE // 2
PAD = 128
ROWS = 2 * PAD
ROLL = SHIFT * GRID
GROUP = 128 // HEAD_DIM
GROUPS = HEADS // GROUP
STACK = GROUP * PAD
CHUNK = 512
BF = jnp.bfloat16
F32 = jnp.float32


def swap(values, axis):
    return lax.ppermute(values, axis, [(0, 1), (1, 0)])


def mm(left, right):
    return lax.dot_general(left, right, (((1,), (0,)), ((), ())), preferred_element_type=F32)


def mm_nt(left, right):
    return lax.dot_general(left, right, (((1,), (1,)), ((), ())), preferred_element_type=F32)


def mm_tn(left, right):
    return lax.dot_general(left, right, (((0,), (0,)), ((), ())), preferred_element_type=F32)


def token_positions(layer):
    token = np.arange(HALF)
    line, column = token // GRID, token % GRID
    if layer % 2 == 1:
        column = (column - SHIFT) % GRID
    return line * WINDOW + column % WINDOW, column // WINDOW, line * GRID + column


def position_one_hot(layer):
    position, _, _ = token_positions(layer)
    picks = np.zeros((PAD, PAD), np.float32)
    picks[np.arange(HALF), position] = 1.0
    return picks


def mask_of(layer, region_ids):
    _, window, place = token_positions(layer)
    same = np.zeros((PAD, PAD), bool)
    same[:HALF, :HALF] = window[:, None] == window[None, :]
    same[HALF:, :HALF] = True
    allowed = jnp.broadcast_to(jnp.asarray(same)[None], (2, PAD, PAD))
    if layer % 2 == 1:
        ids = jnp.roll(region_ids.reshape(2, WINDOW, GRID), SHIFT, 2).reshape(2, HALF)
        ids = jnp.pad(ids, ((0, 0), (0, PAD - HALF)), constant_values=-1)
        pad_row = jnp.asarray(np.arange(PAD) >= HALF)[None, :, None]
        allowed = allowed & ((ids[:, :, None] == ids[:, None, :]) | pad_row)
    return jnp.where(allowed, 0.0, NEG).astype(F32)


def head_mask():
    lane = lax.broadcasted_iota(jnp.int32, (STACK, PAD), 1) // HEAD_DIM
    row = lax.broadcasted_iota(jnp.int32, (STACK, PAD), 0) // PAD
    return lane == row


def stack_heads(values, mask):
    tiled = jnp.concatenate([values] * GROUP, axis=0)
    return jnp.where(mask, tiled, jnp.zeros_like(tiled))


def unstack_heads(values, mask):
    kept = jnp.where(mask, values, 0.0)
    total = kept[0:PAD]
    for head in range(1, GROUP):
        total = total + kept[head * PAD : (head + 1) * PAD]
    return total


def norm_parts(values):
    average = jnp.mean(values, -1, keepdims=True)
    centred = values - average
    variance = jnp.mean(centred * centred, -1, keepdims=True)
    inverse = lax.rsqrt(variance + EPS)
    return centred * inverse, inverse


def norm_back(grad_normed, values, gain):
    xhat, inverse = norm_parts(values)
    scaled = grad_normed * gain
    mean_one = jnp.mean(scaled, -1, keepdims=True)
    mean_two = jnp.mean(scaled * xhat, -1, keepdims=True)
    grad_input = inverse * (scaled - mean_one - xhat * mean_two)
    return grad_input, jnp.sum(grad_normed * xhat, 0, keepdims=True), jnp.sum(grad_normed, 0, keepdims=True)


def split_halves(values):
    return values[:, : D // 2], values[:, D // 2 :]


def gelu_slope(values):
    return 0.5 * (1.0 + lax.erf(values * (1.0 / math.sqrt(2.0)))) + values * jnp.exp(
        -0.5 * values * values
    ) * (1.0 / math.sqrt(2.0 * math.pi))


GAIN_ONE, GAIN_TWO, SHIFT_ONE, SHIFT_TWO, OUT_BIAS, DOWN_BIAS, Q_BIAS, V_BIAS, UP_BIAS = 0, 1, 2, 3, 4, 5, 6, 7, 8


def prep_kernel(table_ref, index_ref, picks_ref, bias_ref, pairs_ref):
    rows = table_ref.shape[1]
    for position in range(SPAN):
        wanted = index_ref[position : position + 1, :]
        hot = (lax.broadcasted_iota(jnp.int32, (rows, PAD), 0) == wanted).astype(F32).astype(BF)
        pairs_ref[position] = mm(table_ref[...], hot)
    for layer in range(LAYERS):
        picks = picks_ref[layer]
        for head in range(HEADS):
            bias = pairs_ref[:, layer * HEADS + head, :]
            spread = mm(picks[:, :64], bias.astype(BF)).astype(BF)
            bias_ref[layer, head] = mm_nt(spread, picks)


def attn_fwd_kernel(
    x_ref, small_ref, q00, q01, q10, q11, o00, o01, o10, o11, bias_ref, mask_ref,
    mid_ref, normed_ref, qkv_ref, probs_ref, att_ref,
):
    x = x_ref[...]
    xhat, _ = norm_parts(x)
    normed = (
        xhat * small_ref[GAIN_ONE : GAIN_ONE + 1] + small_ref[SHIFT_ONE : SHIFT_ONE + 1]
    ).astype(BF)
    normed_ref[...] = normed
    near, far = split_halves(normed)
    half = D // 2
    for part, (own, other) in enumerate(((q00, q01), (q10, q11))):
        projected = mm(near, own[...]) + mm(far, other[...])
        lanes = slice(part * half, (part + 1) * half)
        qkv_ref[part, :, 0:half] = (projected[:, 0:half] + small_ref[Q_BIAS : Q_BIAS + 1, lanes]).astype(BF)
        qkv_ref[part, :, half : 2 * half] = projected[:, half : 2 * half].astype(BF)
        qkv_ref[part, :, 2 * half :] = (
            projected[:, 2 * half :] + small_ref[V_BIAS : V_BIAS + 1, lanes]
        ).astype(BF)
    mask = head_mask()
    for group in range(GROUPS):
        part, lane = group // 2, (group % 2) * 128
        bias = bias_ref[group * GROUP : (group + 1) * GROUP]
        for side in range(2):
            rows = slice(side * PAD, (side + 1) * PAD)
            query = qkv_ref[part, rows, lane : lane + 128]
            key = qkv_ref[part, rows, half + lane : half + lane + 128]
            value = qkv_ref[part, rows, 2 * half + lane : 2 * half + lane + 128]
            scores = mm_nt(stack_heads(query, mask), key).reshape(GROUP, PAD, PAD) * SCALE
            scores = scores + (bias + mask_ref[side][None])
            peak = jnp.max(scores, -1, keepdims=True)
            expos = jnp.exp(scores - peak)
            totals = jnp.sum(expos, -1, keepdims=True)
            probs = (expos / totals).astype(BF).reshape(STACK, PAD)
            probs_ref[side, group] = probs
            attended = unstack_heads(mm(probs, value), mask)
            att_ref[rows, group * 128 : (group + 1) * 128] = attended.astype(BF)
    first, second = split_halves(att_ref[...])
    near = mm(first, o00[...]) + mm(second, o10[...])
    far = mm(first, o01[...]) + mm(second, o11[...])
    mid_ref[...] = x + jnp.concatenate([near, far], axis=1) + small_ref[OUT_BIAS : OUT_BIAS + 1]


def roll_rows(values_ref, result_ref):
    rest = HALF - ROLL
    result_ref[...] = jnp.zeros_like(result_ref)
    for side in range(2):
        here, there = side * PAD, (1 - side) * PAD
        result_ref[here : here + rest, :] = values_ref[here + ROLL : here + HALF, :]
        result_ref[here + rest : here + HALF, :] = values_ref[there : there + ROLL, :]


def unroll_rows(values_ref, result_ref):
    rest = HALF - ROLL
    result_ref[...] = jnp.zeros_like(result_ref)
    for side in range(2):
        here, there = side * PAD, (1 - side) * PAD
        result_ref[here + ROLL : here + HALF, :] = values_ref[here : here + rest, :]
        result_ref[here : here + ROLL, :] = values_ref[there + rest : there + HALF, :]


def clear_padding(values):
    row = lax.broadcasted_iota(jnp.int32, values.shape, 0) % PAD
    return jnp.where(row < HALF, values, 0.0)


def ffn_fwd_kernel(
    layer, mid_ref, small_ref, u00, u01, u10, u11, d00, d01, d10, d11,
    x_ref, normed_ref, pre_ref, hidden_ref, scratch,
):
    middle = mid_ref[...]
    xhat, _ = norm_parts(middle)
    normed = (
        xhat * small_ref[GAIN_TWO : GAIN_TWO + 1] + small_ref[SHIFT_TWO : SHIFT_TWO + 1]
    ).astype(BF)
    normed_ref[...] = normed
    near, far = split_halves(normed)
    sums = [jnp.zeros((ROWS, D // 2), F32), jnp.zeros((ROWS, D // 2), F32)]
    per_part = FF // 2 // CHUNK
    for chunk in range(FF // CHUNK):
        part, at = chunk // per_part, (chunk % per_part) * CHUNK
        up_own, up_other, down_own, down_other = ((u00, u01, d00, d01), (u10, u11, d10, d11))[part]
        pre = mm(near, up_own[:, at : at + CHUNK]) + mm(far, up_other[:, at : at + CHUNK])
        pre = pre + small_ref[UP_BIAS + chunk : UP_BIAS + chunk + 1]
        pre_ref[:, chunk * CHUNK : (chunk + 1) * CHUNK] = pre
        hidden = (pre * (0.5 * (1.0 + lax.erf(pre * (1.0 / math.sqrt(2.0)))))).astype(BF)
        hidden_ref[:, chunk * CHUNK : (chunk + 1) * CHUNK] = hidden
        sums[0] = sums[0] + mm(hidden, down_own[at : at + CHUNK, :])
        sums[1] = sums[1] + mm(hidden, down_other[at : at + CHUNK, :])
    result = middle + jnp.concatenate(sums, axis=1) + small_ref[DOWN_BIAS : DOWN_BIAS + 1]
    scratch[...] = result
    if layer % 2 == 0:
        roll_rows(scratch, x_ref)
    else:
        unroll_rows(scratch, x_ref)


def ffn_bwd_kernel(
    grad_ref, mid_ref, small_ref, normed_ref, pre_ref, hidden_ref, u00, u01, u10, u11, d00, d01, d10, d11,
    grad_mid_ref, keep_ref, send_ref, small_keep_ref, small_send_ref,
):
    half = D // 2
    grad = grad_ref[...]
    grad_down = grad.astype(BF)
    near, far = split_halves(grad_down)
    normed_near = normed_ref[:, :half]
    per_part = FF // 2 // CHUNK
    outs = (keep_ref, send_ref)
    small_outs = (small_keep_ref, small_send_ref)
    sums = [jnp.zeros((ROWS, half), F32), jnp.zeros((ROWS, half), F32)]
    for chunk in range(FF // CHUNK):
        part, at = chunk // per_part, (chunk % per_part) * CHUNK
        up_own, up_other, down_own, down_other = ((u00, u01, d00, d01), (u10, u11, d10, d11))[part]
        lanes = slice(chunk * CHUNK, (chunk + 1) * CHUNK)
        grad_hidden = mm_nt(near, down_own[at : at + CHUNK, :]) + mm_nt(far, down_other[at : at + CHUNK, :])
        grad_pre_wide = (grad_hidden * gelu_slope(pre_ref[:, lanes])).astype(BF)
        outs[part][at : at + CHUNK, :] = mm_tn(hidden_ref[:, lanes], near).astype(BF)
        grad_up = mm_tn(normed_near, grad_pre_wide).astype(BF)
        bias_sum = jnp.sum(grad_pre_wide.astype(F32), 0, keepdims=True)
        for piece in range(CHUNK // half):
            place = FF // 2 + (at // half + piece) * half
            outs[part][place : place + half, :] = grad_up[:, piece * half : (piece + 1) * half]
            line = 3 + at // half + piece
            small_outs[part][line : line + 1, :] = bias_sum[:, piece * half : (piece + 1) * half]
        sums[0] = sums[0] + mm_nt(grad_pre_wide, up_own[:, at : at + CHUNK])
        sums[1] = sums[1] + mm_nt(grad_pre_wide, up_other[:, at : at + CHUNK])
    grad_normed = jnp.concatenate(sums, axis=1)
    grad_input, grad_gain, grad_shift = norm_back(
        grad_normed, mid_ref[...], small_ref[GAIN_TWO : GAIN_TWO + 1]
    )
    grad_mid_ref[...] = clear_padding(grad + grad_input)
    down_bias = jnp.sum(near.astype(F32), 0, keepdims=True)
    for small in small_outs:
        small[0:1, :] = down_bias
        small[1:2, :] = grad_gain[:, :half]
        small[2:3, :] = grad_shift[:, :half]
        small[7:8, :] = jnp.zeros((1, half), F32)


def attn_bwd_kernel(
    layer, grad_mid_ref, x_ref, small_ref, normed_ref, qkv_ref, probs_ref, att_ref,
    q00, q01, q10, q11, o00, o01, o10, o11, picks_ref, picks_t_ref,
    grad_ref, keep_ref, send_ref, small_keep_ref, small_send_ref, table_ref, grad_qkv, scratch,
):
    half = D // 2
    grad_mid = grad_mid_ref[...]
    grad_att = grad_mid.astype(BF)
    near, far = split_halves(grad_att)
    outs = (keep_ref, send_ref)
    small_outs = (small_keep_ref, small_send_ref)
    mask = head_mask()
    picks = picks_ref[...]
    picks_t = picks_t_ref[...]
    normed_near = normed_ref[:, :half]
    sums = [jnp.zeros((ROWS, half), F32), jnp.zeros((ROWS, half), F32)]
    for part in range(2):
        out_own, out_other = ((o00, o01), (o10, o11))[part]
        qkv_own, qkv_other = ((q00, q01), (q10, q11))[part]
        grad_attended = (mm_nt(near, out_own[...]) + mm_nt(far, out_other[...])).astype(BF)
        outs[part][3 * half : 4 * half, :] = mm_tn(att_ref[:, part * half : (part + 1) * half], near).astype(BF)
        for inner in range(2):
            group, lane = part * 2 + inner, inner * 128
            tables = [jnp.zeros((64, PAD), F32) for _ in range(GROUP)]
            for side in range(2):
                rows = slice(side * PAD, (side + 1) * PAD)
                query = stack_heads(qkv_ref[part, rows, lane : lane + 128], mask)
                key = qkv_ref[part, rows, half + lane : half + lane + 128]
                value = qkv_ref[part, rows, 2 * half + lane : 2 * half + lane + 128]
                grad_out = stack_heads(grad_attended[rows, lane : lane + 128], mask)
                probs_low = probs_ref[side, group]
                probs = probs_low.astype(F32)
                grad_probs = mm_nt(grad_out, value)
                weighted = jnp.sum(probs * grad_probs, -1, keepdims=True)
                grad_scores = (probs * (grad_probs - weighted)).astype(BF)
                grad_value = mm_tn(probs_low, grad_out)
                grad_query = unstack_heads(mm(grad_scores, key), mask) * SCALE
                grad_key = mm_tn(grad_scores, query) * SCALE
                grad_qkv[part, rows, lane : lane + 128] = grad_query.astype(BF)
                grad_qkv[part, rows, half + lane : half + lane + 128] = grad_key.astype(BF)
                grad_qkv[part, rows, 2 * half + lane : 2 * half + lane + 128] = grad_value.astype(BF)
                picked = mm(grad_scores, picks).astype(BF)
                for head in range(GROUP):
                    tables[head] = tables[head] + mm(picks_t[:64], picked[head * PAD : (head + 1) * PAD])
            for head in range(GROUP):
                table_ref[group * GROUP + head] = tables[head][:56]
        grads = grad_qkv[part]
        wide = mm_tn(normed_near, grads).astype(BF)
        for piece in range(3):
            outs[part][piece * half : (piece + 1) * half, :] = wide[:, piece * half : (piece + 1) * half]
        small_outs[part][3:4, :] = jnp.sum(grads[:, :half].astype(F32), 0, keepdims=True)
        small_outs[part][4:5, :] = jnp.sum(grads[:, 2 * half :].astype(F32), 0, keepdims=True)
        sums[0] = sums[0] + mm_nt(grads, qkv_own[...])
        sums[1] = sums[1] + mm_nt(grads, qkv_other[...])
    grad_input, grad_gain, grad_shift = norm_back(
        jnp.concatenate(sums, axis=1), x_ref[...], small_ref[GAIN_ONE : GAIN_ONE + 1]
    )
    total = clear_padding(grad_mid + grad_input)
    if layer % 2 == 1:
        scratch[...] = total
        unroll_rows(scratch, grad_ref)
    else:
        grad_ref[...] = total
    out_bias = jnp.sum(near.astype(F32), 0, keepdims=True)
    for small in small_outs:
        small[0:1, :] = out_bias
        small[1:2, :] = grad_gain[:, :half]
        small[2:3, :] = grad_shift[:, :half]
        small[5:8, :] = jnp.zeros((3, half), F32)


def call(kernel, outs, scratch, args, flops):
    vmem = pl.BlockSpec(memory_space=pltpu.VMEM)
    moved = sum(a.size * a.dtype.itemsize for a in args) + sum(
        math.prod(shape) * jnp.dtype(kind).itemsize for shape, kind in outs
    )
    return pl.pallas_call(
        kernel,
        out_shape=[jax.ShapeDtypeStruct(shape, kind) for shape, kind in outs],
        in_specs=[vmem] * len(args),
        out_specs=[vmem] * len(outs),
        scratch_shapes=scratch,
        compiler_params=pltpu.CompilerParams(vmem_limit_bytes=40 * 1024 * 1024),
        cost_estimate=pl.CostEstimate(flops=flops, bytes_accessed=moved, transcendentals=0),
    )(*args)


def part_of(kernel, layer):
    def run(*refs):
        kernel(layer, *refs)

    return run


def dp_sum(values):
    return lax.psum(values, "dp")


def on_device(
    tokens, cotangent, qkv_weight, qv_bias, out_weight, out_bias, up_weight, up_bias,
    down_weight, down_bias, norm_gain, norm_shift, bias_table, index_map, region_ids,
):
    half = D // 2
    col_own = jnp.concatenate(
        [tokens, cotangent, norm_gain.reshape(4, half), norm_shift.reshape(4, half), out_bias, down_bias], 0
    )
    tables_own = jnp.pad(
        bias_table.transpose(0, 2, 1).reshape(LAYERS * HEADS // 2, TABLE), ((0, 0), (0, 256 - TABLE))
    )
    row_own = jnp.concatenate([qv_bias.reshape(4, half), up_bias.reshape(8, half), tables_own], 0)
    col_other = swap(col_own, "col")
    row_other = swap(row_own, "row")
    col_all = jnp.concatenate([col_own, col_other], 1)

    blocks = []
    for layer in range(LAYERS):
        own = [
            qkv_weight[layer].reshape(half, 3 * half), out_weight[layer], up_weight[layer], down_weight[layer],
        ]
        other_col = [swap(piece, "col") for piece in own]
        other_row = [swap(piece, "row") for piece in own]
        other_both = [swap(piece, "row") for piece in other_col]
        blocks.append(
            [(a, b, c, d) for a, b, c, d in zip(own, other_col, other_row, other_both)]
        )

    small_cols = col_all[2 * IMAGE :].astype(F32)
    row_both = jnp.concatenate([row_own, row_other], 1).astype(F32)
    ups = jnp.concatenate(
        [row_own[4:12].reshape(LAYERS, 2, D), row_other[4:12].reshape(LAYERS, 2, D)], 1
    ).astype(F32)
    smalls = []
    for layer in range(LAYERS):
        smalls.append(
            jnp.concatenate(
                [
                    small_cols[2 * layer : 2 * layer + 2],
                    small_cols[4 + 2 * layer : 6 + 2 * layer],
                    small_cols[8 + layer : 9 + layer],
                    small_cols[10 + layer : 11 + layer],
                    row_both[2 * layer : 2 * layer + 2],
                    ups[layer],
                    jnp.zeros((4, D), F32),
                ],
                0,
            )
        )
    heads = HEADS // 2
    tables = jnp.concatenate(
        [row_own[12 : 12 + heads], row_other[12 : 12 + heads], row_own[12 + heads :], row_other[12 + heads :]], 0
    )
    index_pad = jnp.pad(index_map, ((0, 64 - SPAN), (0, PAD - SPAN)), constant_values=-1)
    picks = np.stack([position_one_hot(layer) for layer in range(LAYERS)])
    picks_t = jnp.asarray(picks.transpose(0, 2, 1), BF)
    picks = jnp.asarray(picks, BF)
    masks = [mask_of(layer, region_ids) for layer in range(LAYERS)]

    (bias,) = call(
        prep_kernel,
        [((LAYERS, HEADS, PAD, PAD), F32)],
        [pltpu.VMEM((64, LAYERS * HEADS, PAD), F32)],
        [tables, index_pad, picks],
        10**7,
    )

    def to_rows(values):
        return jnp.pad(values.reshape(2, HALF, -1), ((0, 0), (0, PAD - HALF), (0, 0))).reshape(ROWS, -1)

    x = to_rows(col_all[:IMAGE].astype(F32))
    saved = []
    for layer in range(LAYERS):
        wq, wo, wu, wd = blocks[layer]
        middle, normed_one, qkv, probs, att = call(
            attn_fwd_kernel,
            [
                ((ROWS, D), F32), ((ROWS, D), BF), ((2, ROWS, 3 * half), BF),
                ((2, GROUPS, STACK, PAD), BF), ((ROWS, D), BF),
            ],
            [],
            [x, smalls[layer], *wq, *wo, bias[layer], masks[layer]],
            10**9,
        )
        result, normed_two, pre, hidden = call(
            part_of(ffn_fwd_kernel, layer),
            [((ROWS, D), F32), ((ROWS, D), BF), ((ROWS, FF), F32), ((ROWS, FF), BF)],
            [pltpu.VMEM((ROWS, D), F32)],
            [middle, smalls[layer], *wu, *wd],
            10**9,
        )
        saved.append((x, middle, normed_one, qkv, probs, att, normed_two, pre, hidden))
        x = result

    def from_rows(values):
        return values.reshape(2, PAD, -1)[:, :HALF, :half].reshape(IMAGE, half).astype(BF)

    output = from_rows(x)
    grad = to_rows(jnp.roll(col_all[IMAGE : 2 * IMAGE], -ROLL, 0).astype(F32))

    one_hot = (index_map[:, :, None] == jnp.arange(256, dtype=jnp.int32)).astype(F32).reshape(SPAN * SPAN, 256)
    sums = [None] * LAYERS
    for layer in reversed(range(LAYERS)):
        x_in, middle, normed_one, qkv, probs, att, normed_two, pre, hidden = saved[layer]
        wq, wo, wu, wd = blocks[layer]
        small_shape = ((8, half), F32)
        grad_mid, keep, send, small_keep, small_send = call(
            ffn_bwd_kernel,
            [((ROWS, D), F32), ((FF, half), BF), ((FF, half), BF), small_shape, small_shape],
            [],
            [grad, middle, smalls[layer], normed_two, pre, hidden, *wu, *wd],
            2 * 10**9,
        )
        ffn_total = dp_sum(keep + swap(send, "row"))
        grad, keep, send, att_keep, att_send, pairs = call(
            part_of(attn_bwd_kernel, layer),
            [
                ((ROWS, D), F32), ((2 * D, half), BF), ((2 * D, half), BF), small_shape, small_shape,
                ((HEADS, 56, PAD), F32),
            ],
            [pltpu.VMEM((2, ROWS, 3 * half), BF), pltpu.VMEM((ROWS, D), F32)],
            [grad_mid, x_in, smalls[layer], normed_one, qkv, probs, att, *wq, *wo, picks[layer], picks_t[layer]],
            2 * 10**9,
        )
        table = jnp.dot(pairs[:, :SPAN, :SPAN].reshape(HEADS, SPAN * SPAN), one_hot, precision=HIGH)
        tail_keep = jnp.concatenate([small_keep, att_keep, table[:heads], jnp.zeros((8, half), F32)], 0)
        tail_send = jnp.concatenate([small_send, att_send, table[heads:], jnp.zeros((8, half), F32)], 0)
        keep = jnp.concatenate([keep, tail_keep.astype(BF)], 0)
        send = jnp.concatenate([send, tail_send.astype(BF)], 0)
        sums[layer] = (ffn_total, dp_sum(keep + swap(send, "row")))
    input_grad = from_rows(grad)

    def both(pick):
        return jnp.stack([pick(*sums[layer]).astype(F32) for layer in range(LAYERS)])

    base = 2 * D
    grad_down_weight = both(lambda f, a: f[: FF // 2])
    grad_up_weight = both(lambda f, a: f[FF // 2 :].reshape(4, half, half).transpose(1, 0, 2).reshape(half, FF // 2))
    grad_qkv_weight = both(lambda f, a: a[: 3 * half].reshape(3, half, half).transpose(1, 0, 2))
    grad_out_weight = both(lambda f, a: a[3 * half : base])
    grad_qv_bias = both(lambda f, a: a[base + 11 : base + 13])
    grad_out_bias = both(lambda f, a: a[base + 8])
    grad_up_bias = both(lambda f, a: a[base + 3 : base + 7].reshape(FF // 2))
    grad_down_bias = both(lambda f, a: a[base])
    grad_norm_gain = both(lambda f, a: jnp.stack([a[base + 9], a[base + 1]]))
    grad_norm_shift = both(lambda f, a: jnp.stack([a[base + 10], a[base + 2]]))
    grad_bias_table = both(lambda f, a: a[base + 16 : base + 24, :TABLE].T)
    return (
        output, input_grad, grad_qkv_weight, grad_qv_bias, grad_out_weight, grad_out_bias, grad_up_weight,
        grad_up_bias, grad_down_weight, grad_down_bias, grad_norm_gain, grad_norm_shift, grad_bias_table,
    )


def solution(mesh):
    in_specs = (
        P(("dp", "row"), "col"),
        P(("dp", "row"), "col"),
        P(None, "col", None, "row"),
        P(None, None, "row"),
        P(None, "row", "col"),
        P(None, "col"),
        P(None, "col", "row"),
        P(None, "row"),
        P(None, "row", "col"),
        P(None, "col"),
        P(None, None, "col"),
        P(None, None, "col"),
        P(None, None, "row"),
        P(),
        P(),
    )
    out_specs = (
        P(("dp", "row"), "col"),
        P(("dp", "row"), "col"),
        P(None, "col", None, "row"),
        P(None, None, "row"),
        P(None, "row", "col"),
        P(None, "col"),
        P(None, "col", "row"),
        P(None, "row"),
        P(None, "row", "col"),
        P(None, "col"),
        P(None, None, "col"),
        P(None, None, "col"),
        P(None, None, "row"),
    )
    return jax.shard_map(
        on_device, mesh=mesh, in_specs=in_specs, out_specs=out_specs, check_vma=False
    )
```

time: 810 us -> 319 us (0.39); the launches traced: 798 us -> 317 us
  blocking collectives: 243 us -> 0 us
  waiting for transfers between devices: 330 us -> 169 us
  matrix products: 45.1 us -> 2.18 us
  Pallas kernels: 0 us -> 36.8 us
  starting transfers between devices: 40.4 us -> 11.3 us
  local copies, waits for them, and re-layouts: 84.5 us -> 59.9 us
  other arithmetic: 37.2 us -> 23.5 us
    psum x2 -> x1, waiting for transfers between devices: 326 us -> 131 us  [dp_sum(): return lax.psum(values, 'dp')]
    unnamed x14 -> x0, blocking collectives: 116 us -> none
    all_gather x16 -> x0, blocking collectives: 86.4 us -> none  [the longest x4 37.2 us: back_col_gather(): return lax.all_gather(values, 'col', axis=0, tiled=True)]
    dot_general x40 -> x2, matrix products: 45.1 us -> 2.18 us  [on_device(): jnp.dot(pairs[:, :SPAN, :SPAN].reshape(HEADS, SPAN * SPAN), one_hot, prec...]
    psum x8 -> x0, blocking collectives: 40.4 us -> none  [the longest x4 20.7 us: norm_forward(): lax.psum((jnp.sum(residual, 1), jnp.sum(residual * residual, 1)), 'col')]
    unnamed x16 -> x0, starting transfers between devices: 40.3 us -> none
    unnamed x276 -> x134, local copies, waits for them, and re-layouts: 51.5 us -> 13.6 us
    ppermute x0 -> x30, waiting for transfers between devices: none -> 37.9 us  [swap(): return lax.ppermute(values, axis, [(0, 1), (1, 0)])]
  transfers between devices with their start and end apart: 18 -> 31, of which waited for: 7 -> 8; matrix products, arithmetic and copies ran while one was open for 4% -> 14% of each run, Pallas kernels for 0% -> 8%
where the time goes in v1:
time: 319 us; the launch traced here: 317 us
  waiting for transfers between devices  169 us (53%)
  local copies, waits for them, and re-layouts  59.9 us (19%)
  Pallas kernels  36.8 us (12%)
  other arithmetic  23.5 us (7%)
  between operations  14.9 us (5%)
  starting transfers between devices  11.3 us (4%)
    psum x1, waiting for transfers between devices, dp_sum(): return lax.psum(values, 'dp')  131 us
    ppermute x30, waiting for transfers between devices, swap(): return lax.ppermute(values, axis, [(0, 1), (1, 0)])  37.9 us
    pallas_call x9, Pallas kernels, call(): pl.pallas_call(kernel, out_shape=[jax.ShapeDtypeStruct(shape, kind) for s...  36.8 us
    unnamed x134, local copies, waits for them, and re-layouts  13.6 us
    ppermute x30, starting transfers between devices, swap(): return lax.ppermute(values, axis, [(0, 1), (1, 0)])  11.3 us
    another operation x11, other arithmetic, both(): jnp.stack([pick(*sums[layer]).astype(F32) for layer in range(LAYERS)])  9.88 us
    another operation x8, local copies, waits for them, and re-layouts, both(): jnp.stack([pick(*sums[layer]).astype(F32) for layer in range(LAYERS)])  7.67 us
  transfers between devices with their start and end apart: 31, of which 8 were waited for; matrix products, arithmetic and copies ran while one was open for 14% of the time, Pallas kernels for 8%

profile of v1, /device:TPU:0, one launch (start us, length us, event | category | flops | bytes accessed | tf_op | source)
XLA Modules:
  0.0 317.4 jit_solution(2499892173972636913)
XLA Ops:
  7.2 1.7 slice_bitcast_fusion.10
  8.9 3.0 collective-permute-start.5
  21.2 5.0 %concatenate.84 = bf16[404,256]{1,0:T(8,128)(2,1)} concatenate(bf16[196,256]{1,0:T(8,128)(2,1)} %param.20, bf16[196,256]{1,0:T(8,128)(2,1)} %param.21, bf16[4,256]{1,0:T(4,128)(2,1)S(1)} %reshape.269, bf16[4,256]{1,0:T(4,128)(2,1)S(1)} %reshape.270, bf16[2,256]{1,0:T(2,128)(2,1)} %param.25, bf16[2,256]{1,0:T(2,128)(2,1)} %param.29), dimensions={0} | concatenate | bytes 413696 | tf_op jit(solution)/shard_map/concatenate | solution.py:391
  26.2 2.0 collective-permute-start
  28.7 3.0 shard_map.291
  35.0 2.0 collective-permute-start.14
  40.8 3.7 %collective-permute-done.2.q01.refs_8_ = bf16[256,768]{1,0:T(8,128)(2,1)} collective-permute-done((bf16[256,768]{1,0:T(8,128)(2,1)S(1)}, bf16[256,768]{1,0:T(8,128)(2,1)}, u32[]{:S(2)}, u32[]{:S(2)}) %collective-permute-start.2) | collective-permute-done | bytes 393248 | tf_op jit(solution)/shard_map/ppermute | solution.py:41
  46.0 6.8 %collective-permute-done.14.q01.refs_8_ = bf16[256,768]{1,0:T(8,128)(2,1)S(1)} collective-permute-done((bf16[256,768]{1,0:T(8,128)(2,1)}, bf16[256,768]{1,0:T(8,128)(2,1)S(1)}, u32[]{:S(2)}, u32[]{:S(2)}) %collective-permute-start.14) | collective-permute-done | bytes 393248 | tf_op jit(solution)/shard_map/ppermute | solution.py:41
  56.0 8.2 %collective-permute-done.8.refs_3_.u01 = bf16[256,1024]{1,0:T(8,128)(2,1)} collective-permute-done((bf16[256,1024]{1,0:T(8,128)(2,1)S(1)}, bf16[256,1024]{1,0:T(8,128)(2,1)}, u32[]{:S(2)}, u32[]{:S(2)}) %collective-permute-start.8) | collective-permute-done | bytes 524320 | tf_op jit(solution)/shard_map/ppermute | solution.py:41
  65.0 10.4 %collective-permute-done.11.refs_7_.d01 = bf16[1024,256]{1,0:T(8,128)(2,1)} collective-permute-done((bf16[1024,256]{1,0:T(8,128)(2,1)S(1)}, bf16[1024,256]{1,0:T(8,128)(2,1)}, u32[]{:S(2)}, u32[]{:S(2)}) %collective-permute-start.11) | collective-permute-done | bytes 524320 | tf_op jit(solution)/shard_map/ppermute | solution.py:41
  75.4 1.8 fusion.13
  77.3 1.7 reshape.271
  78.9 1.7 pad.21
  80.6 1.7 convert_element_type.161
  82.3 1.6 pad.25
  84.4 1.5 fusion.20
  85.9 2.6 concatenate.89.small_ref.refs_1_.refs_2_
  88.5 2.0 concatenate.91.small_ref.refs_1_.refs_2_
  91.6 5.3 %collective-permute-done.23.refs_7_.d01 = bf16[1024,256]{1,0:T(8,128)(2,1)} collective-permute-done((bf16[1024,256]{1,0:T(8,128)(2,1)S(1)}, bf16[1024,256]{1,0:T(8,128)(2,1)}, u32[]{:S(2)}, u32[]{:S(2)}) %collective-permute-start.23) | collective-permute-done | bytes 524320 | tf_op jit(solution)/shard_map/ppermute | solution.py:41
  104.6 3.5 %shard_map.292 = (f32[256,512]{1,0:T(8,128)S(1)}, bf16[256,512]{1,0:T(8,128)(2,1)S(1)}, bf16[2,256,768]{2,1,0:T(8,128)(2,1)S(1)}, bf16[2,4,512,128]{3,2,1,0:T(8,128)(2,1)S(1)}, bf16[256,512]{1,0:T(8,128)(2,1)S(1)}) custom-call(f32[256,512]{1,0:T(8,128)S(1)} %bitcast_convert_fusion.1.x_ref.refs_1_, f32[16,512]{1,0:T(8,128)S(1)} %copy-done.4, ...), custom_call_target="tpu_custom_call" | custom-call | flops 1000000000 | bytes 6717440 | tf_op jit(solution)/shard_map/pallas_call | solution.py:364
  109.0 3.7 %shard_map.293 = (f32[256,512]{1,0:T(8,128)S(1)}, bf16[256,512]{1,0:T(8,128)(2,1)S(1)}, f32[256,2048]{1,0:T(8,128)S(1)}, bf16[256,2048]{1,0:T(8,128)(2,1)S(1)}) custom-call(f32[256,512]{1,0:T(8,128)S(1)} %get-tuple-element.53.refs_0_.mid_ref, f32[16,512]{1,0:T(8,128)S(1)} %copy-done.5, bf16[256,1024]{1,0:T(8,128)(2,1)S(1)} %get-tuple-element.106.refs_2_.u00, ...), custom_call_target="tpu_custom_call" | custom-call | flops 1000000000 | bytes 8683520 | tf_op jit(solution)/shard_map/pallas_call | solution.py:364
  112.7 3.4 %shard_map.294 = (f32[256,512]{1,0:T(8,128)S(1)}, bf16[256,512]{1,0:T(8,128)(2,1)S(1)}, bf16[2,256,768]{2,1,0:T(8,128)(2,1)S(1)}, bf16[2,4,512,128]{3,2,1,0:T(8,128)(2,1)S(1)}, bf16[256,512]{1,0:T(8,128)(2,1)S(1)}) custom-call(f32[256,512]{1,0:T(8,128)S(1)} %get-tuple-element.54.x_ref.refs_1_, f32[16,512]{1,0:T(8,128)S(1)} %copy-done.6, ...), custom_call_target="tpu_custom_call" | custom-call | flops 1000000000 | bytes 6717440 | tf_op jit(solution)/shard_map/pallas_call | solution.py:364
  117.5 3.1 shard_map.295
  120.7 3.9 %shard_map.296 = (f32[256,512]{1,0:T(8,128)S(1)}, bf16[2048,256]{1,0:T(8,128)(2,1)S(1)}, bf16[2048,256]{1,0:T(8,128)(2,1)S(1)}, f32[8,256]{1,0:T(8,128)S(1)}, f32[8,256]{1,0:T(8,128)S(1)}) custom-call(f32[256,512]{1,0:T(8,128)S(1)} %bitcast_convert_fusion.grad_ref, f32[256,512]{1,0:T(8,128)S(1)} %get-tuple-element.55.refs_0_.mid_ref, ...), custom_call_target="tpu_custom_call" | custom-call | flops 2000000000 | bytes 11321344 | tf_op jit(solution)/shard_map/pallas_call | solution.py:364
  124.6 5.9 %shard_map.297 = (f32[256,512]{1,0:T(8,128)S(1)}, bf16[1024,256]{1,0:T(8,128)(2,1)S(1)}, bf16[1024,256]{1,0:T(8,128)(2,1)S(1)}, f32[8,256]{1,0:T(8,128)S(1)}, f3...) custom-call(f32[256,512]{1,0:T(8,128)S(1)} %get-tuple-element.60.refs_0_, f32[256,512]{1,0:T(8,128)S(1)} %get-tuple-element.54.x_ref.refs_1_, ...), custom_call_target="tpu_custom_call" | custom-call | flops 2000000000 | bytes 7651328 | tf_op jit(solution)/shard_map/pallas_call | solution.py:364
  132.5 4.2 %shard_map.298 = (f32[256,512]{1,0:T(8,128)S(1)}, bf16[2048,256]{1,0:T(8,128)(2,1)S(1)}, bf16[2048,256]{1,0:T(8,128)(2,1)S(1)}, f32[8,256]{1,0:T(8,128)S(1)}, f32[8,256]{1,0:T(8,128)S(1)}) custom-call(f32[256,512]{1,0:T(8,128)S(1)} %get-tuple-element.65.grad_ref, f32[256,512]{1,0:T(8,128)S(1)} %get-tuple-element.53.refs_0_.mid_ref, f32[16,512]{1,0:T(8,128)S(1)} %copy-done.5, ...), custom_call_target="tpu_custom_call" | custom-call | flops 2000000000 | bytes 11321344 | tf_op jit(solution)/shard_map/pallas_call | solution.py:364
  136.8 6.2 %shard_map.299 = (f32[256,512]{1,0:T(8,128)S(1)}, bf16[1024,256]{1,0:T(8,128)(2,1)S(1)}, bf16[1024,256]{1,0:T(8,128)(2,1)S(1)}, f32[8,256]{1,0:T(8,128)S(1)}, f3...) custom-call(f32[256,512]{1,0:T(8,128)S(1)} %get-tuple-element.69.refs_0_, ...), custom_call_target="tpu_custom_call" | custom-call | flops 2000000000 | bytes 7651328 | tf_op jit(solution)/shard_map/pallas_call | solution.py:364
  146.2 3.0 collective-permute-done.26
  154.1 130.9 %all-reduce.8.cloned.1.call-done = (bf16[1056,256]{1,0:T(8,128)(2,1)}, bf16[1056,256]{1,0:T(8,128)(2,1)}, bf16[2048,256]{1,0:T(8,128)(2,1)}, bf16[2048,256]{1,0:T(8,128)(2,1)}) async-done(((bf16[1056,256]{1,0:T(8,128)(2,1)}, bf16[1056,256]{1,0:T(8,128)(2,1)}, bf16[2048,256]{1,0:T(8,128)(2,1)}, bf16[2048,256]{1,0:T(8,128)(2,1)}), (bf16[1056,256]{1,0:T(8,128)(2,1)}, bf16[1056,256]{1,0:T(8,128)(2,1)}, ...) | async-done | bytes 3178512 | tf_op jit(solution)/shard_map/psum | solution.py:383
  290.5 1.6 slice_bitcast_fusion.9
  304.5 1.5 maximum_convert_fusion
  306.7 1.5 maximum_convert_fusion.1
  (267 shorter events, 64.7 us)
Async XLA Ops:
  7.2 277.8 %all-reduce.8.cloned.1.call-start = ((), (), s32[]{:S(2)}) async-start(), calls=%async_computation | async-start | bytes 6356992 | tf_op jit(solution)/shard_map/psum | solution.py:383
  8.9 22.8 %collective-permute-start.5 = (bf16[256,256]{1,0:T(8,128)(2,1)}, bf16[256,256]{1,0:T(8,128)(2,1)S(1)}, u32[]{:S(2)}, u32[]{:S(2)}) collective-permute-start(bf16[256,256]{1,0:T(8,128)(2,1)} %get-tuple-element.124.o00.refs_11_), channel_id=1, source_target_pairs={{0,1},{1,0},{2,3},{3,2},{4,5},{5,4},{6,7},{7,6},{8,9},{9,8},{10,11... | collective-permute-start | bytes 393224 | tf_op jit(solution)/shard_map/ppermute | solution.py:41
  11.9 23.1 %collective-permute-start.6 = (bf16[256,256]{1,0:T(8,128)(2,1)}, bf16[256,256]{1,0:T(8,128)(2,1)}, u32[]{:S(2)}, u32[]{:S(2)}) collective-permute-start(bf16[256,256]{1,0:T(8,128)(2,1)} %get-tuple-element.124.o00.refs_11_), channel_id=1, source_target_pairs={{0,2},{2,0},{1,3},{3,1},{4,6},{6,4},{5,7},{7,5},{8,10},{10,8},{9,1... | collective-permute-start | bytes 393224 | tf_op jit(solution)/shard_map/ppermute | solution.py:41
  11.9 23.1 %collective-permute-start.17 = (bf16[256,256]{1,0:T(8,128)(2,1)}, bf16[256,256]{1,0:T(8,128)(2,1)}, u32[]{:S(2)}, u32[]{:S(2)}) collective-permute-start(bf16[256,256]{1,0:T(8,128)(2,1)} %get-tuple-element.123.o00.refs_11_), channel_id=1, source_target_pairs={{0,1},{1,0},{2,3},{3,2},{4,5},{5,4},{6,7},{7,6},{8,9},{9,8},{10,11... | collective-permute-start | bytes 393224 | tf_op jit(solution)/shard_map/ppermute | solution.py:41
  12.0 25.7 %collective-permute-start.18 = (bf16[256,256]{1,0:T(8,128)(2,1)}, bf16[256,256]{1,0:T(8,128)(2,1)}, u32[]{:S(2)}, u32[]{:S(2)}) collective-permute-start(bf16[256,256]{1,0:T(8,128)(2,1)} %get-tuple-element.123.o00.refs_11_), channel_id=1, source_target_pairs={{0,2},{2,0},{1,3},{3,1},{4,6},{6,4},{5,7},{7,5},{8,10},{10,8},{9,1... | collective-permute-start | bytes 393224 | tf_op jit(solution)/shard_map/ppermute | solution.py:41
  15.3 10.9 %collective-permute-start.1 = (bf16[28,256]{1,0:T(8,128)(2,1)}, bf16[28,256]{1,0:T(8,128)(2,1)S(1)}, u32[]{:S(2)}, u32[]{:S(2)}) collective-permute-start(bf16[28,256]{1,0:T(8,128)(2,1)} %pad_maximum_fusion), channel_id=1, source_target_pairs={{0,2},{2,0},{1,3},{3,1},{4,6},{6,4},{5,7},{7,5},{8,10},{10,8},{9,1... | collective-permute-start | bytes 43016 | tf_op jit(solution)/shard_map/ppermute | solution.py:41
  26.2 11.8 %collective-permute-start = (bf16[404,256]{1,0:T(8,128)(2,1)}, bf16[404,256]{1,0:T(8,128)(2,1)}, u32[]{:S(2)}, u32[]{:S(2)}) collective-permute-start(bf16[404,256]{1,0:T(8,128)(2,1)} %concatenate.84), channel_id=1, source_target_pairs={{0,1},{1,0},{2,3},{3,2},{4,5},{5,4},{6,7},{7,6},{8,9},{9,8},{10,11... | collective-permute-start | bytes 620552 | tf_op jit(solution)/shard_map/ppermute | solution.py:41
  32.4 12.1 %collective-permute-start.2 = (bf16[256,768]{1,0:T(8,128)(2,1)S(1)}, bf16[256,768]{1,0:T(8,128)(2,1)}, u32[]{:S(2)}, u32[]{:S(2)}) collective-permute-start(bf16[256,768]{1,0:T(8,128)(2,1)S(1)} %copy.42.q00.refs_7_), channel_id=1, source_target_pairs={{0,1},{1,0},{2,3},{3,2},{4,5},{5,4},{6,7},{7,6},{8,9},{9,8},{10,11... | collective-permute-start | bytes 1179656 | tf_op jit(solution)/shard_map/ppermute | solution.py:41
  34.9 11.0 %collective-permute-start.3 = (bf16[256,768]{1,0:T(8,128)(2,1)S(1)}, bf16[256,768]{1,0:T(8,128)(2,1)S(1)}, u32[]{:S(2)}, u32[]{:S(2)}) collective-permute-start(bf16[256,768]{1,0:T(8,128)(2,1)S(1)} %copy.42.q00.refs_7_), channel_id=1, source_target_pairs={{0,2},{2,0},{1,3},{3,1},{4,6},{6,4},{5,7},{7,5},{8,10},{10,8},{9,1... | collective-permute-start | bytes 1179656 | tf_op jit(solution)/shard_map/ppermute | solution.py:41
  35.0 17.9 %collective-permute-start.14 = (bf16[256,768]{1,0:T(8,128)(2,1)}, bf16[256,768]{1,0:T(8,128)(2,1)S(1)}, u32[]{:S(2)}, u32[]{:S(2)}) collective-permute-start(bf16[256,768]{1,0:T(8,128)(2,1)} %copy.46.q00.refs_7_), channel_id=1, source_target_pairs={{0,1},{1,0},{2,3},{3,2},{4,5},{5,4},{6,7},{7,6},{8,9},{9,8},{10,11... | collective-permute-start | bytes 1179656 | tf_op jit(solution)/shard_map/ppermute | solution.py:41
  37.7 1.6 collective-permute-start.7
  37.9 2.1 collective-permute-start.19
  40.0 24.2 %collective-permute-start.8 = (bf16[256,1024]{1,0:T(8,128)(2,1)S(1)}, bf16[256,1024]{1,0:T(8,128)(2,1)}, u32[]{:S(2)}, u32[]{:S(2)}) collective-permute-start(bf16[256,1024]{1,0:T(8,128)(2,1)S(1)} %get-tuple-element.106.refs_2_.u00), channel_id=1, source_target_pairs={{0,1},{1,0},{2,3},{3,2},{4,5},{5,4},{6,7},{7,6},{8,9},{9,8},{10,11... | collective-permute-start | bytes 1572872 | tf_op jit(solution)/shard_map/ppermute | solution.py:41
  40.7 23.5 %collective-permute-start.9 = (bf16[256,1024]{1,0:T(8,128)(2,1)S(1)}, bf16[256,1024]{1,0:T(8,128)(2,1)S(1)}, u32[]{:S(2)}, u32[]{:S(2)}) collective-permute-start(bf16[256,1024]{1,0:T(8,128)(2,1)S(1)} %get-tuple-element.106.refs_2_.u00), channel_id=1, source_target_pairs={{0,2},{2,0},{1,3},{3,1},{4,6},{6,4},{5,7},{7,5},{8,10},{10,8},{9,1... | collective-permute-start | bytes 1572872 | tf_op jit(solution)/shard_map/ppermute | solution.py:41
  44.5 30.9 %collective-permute-start.11 = (bf16[1024,256]{1,0:T(8,128)(2,1)S(1)}, bf16[1024,256]{1,0:T(8,128)(2,1)}, u32[]{:S(2)}, u32[]{:S(2)}) collective-permute-start(bf16[1024,256]{1,0:T(8,128)(2,1)S(1)} %get-tuple-element.104.refs_6_.d00), channel_id=1, source_target_pairs={{0,1},{1,0},{2,3},{3,2},{4,5},{5,4},{6,7},{7,6},{8,9},{9,8},{10,11... | collective-permute-start | bytes 1572872 | tf_op jit(solution)/shard_map/ppermute | solution.py:41
  45.9 42.6 %copy-start.41 = (f32[4,512]{1,0:T(4,128)S(1)}, f32[4,512]{1,0:T(4,128)}, u32[]{:S(2)}) copy-start(f32[4,512]{1,0:T(4,128)} %get-tuple-element.135) | copy-start | bytes 24580
  45.9 38.0 %collective-permute-start.12 = (bf16[1024,256]{1,0:T(8,128)(2,1)S(1)}, bf16[1024,256]{1,0:T(8,128)(2,1)}, u32[]{:S(2)}, u32[]{:S(2)}) collective-permute-start(bf16[1024,256]{1,0:T(8,128)(2,1)S(1)} %get-tuple-element.104.refs_6_.d00), channel_id=1, source_target_pairs={{0,2},{2,0},{1,3},{3,1},{4,6},{6,4},{5,7},{7,5},{8,10},{10,8},{9,1... | collective-permute-start | bytes 1572872 | tf_op jit(solution)/shard_map/ppermute | solution.py:41
  52.8 2.4 collective-permute-start.15
  56.0 35.5 %collective-permute-start.20 = (bf16[256,1024]{1,0:T(8,128)(2,1)S(1)}, bf16[256,1024]{1,0:T(8,128)(2,1)}, u32[]{:S(2)}, u32[]{:S(2)}) collective-permute-start(bf16[256,1024]{1,0:T(8,128)(2,1)S(1)} %get-tuple-element.105.refs_2_.u00), channel_id=1, source_target_pairs={{0,1},{1,0},{2,3},{3,2},{4,5},{5,4},{6,7},{7,6},{8,9},{9,8},{10,11... | collective-permute-start | bytes 1572872 | tf_op jit(solution)/shard_map/ppermute | solution.py:41
  64.2 32.7 %collective-permute-start.23 = (bf16[1024,256]{1,0:T(8,128)(2,1)S(1)}, bf16[1024,256]{1,0:T(8,128)(2,1)}, u32[]{:S(2)}, u32[]{:S(2)}) collective-permute-start(bf16[1024,256]{1,0:T(8,128)(2,1)S(1)} %get-tuple-element.103.refs_6_.d00), channel_id=1, source_target_pairs={{0,1},{1,0},{2,3},{3,2},{4,5},{5,4},{6,7},{7,6},{8,9},{9,8},{10,11... | collective-permute-start | bytes 1572872 | tf_op jit(solution)/shard_map/ppermute | solution.py:41
  65.0 32.4 %collective-permute-start.10 = (bf16[256,1024]{1,0:T(8,128)(2,1)}, bf16[256,1024]{1,0:T(8,128)(2,1)}, u32[]{:S(2)}, u32[]{:S(2)}) collective-permute-start(bf16[256,1024]{1,0:T(8,128)(2,1)} %collective-permute-done.8.refs_3_.u01), channel_id=1, source_target_pairs={{0,2},{2,0},{1,3},{3,1},{4,6},{6,4},{5,7},{7,5},{8,10},{10,8},{9,1... | collective-permute-start | bytes 1572872 | tf_op jit(solution)/shard_map/ppermute | solution.py:41
  75.4 22.0 %collective-permute-start.13 = (bf16[1024,256]{1,0:T(8,128)(2,1)}, bf16[1024,256]{1,0:T(8,128)(2,1)}, u32[]{:S(2)}, u32[]{:S(2)}) collective-permute-start(bf16[1024,256]{1,0:T(8,128)(2,1)} %collective-permute-done.11.refs_7_.d01), channel_id=1, source_target_pairs={{0,2},{2,0},{1,3},{3,1},{4,6},{6,4},{5,7},{7,5},{8,10},{10,8},{9,1... | collective-permute-start | bytes 1572872 | tf_op jit(solution)/shard_map/ppermute | solution.py:41
  83.9 13.0 %collective-permute-start.4 = (bf16[256,768]{1,0:T(8,128)(2,1)}, bf16[256,768]{1,0:T(8,128)(2,1)}, u32[]{:S(2)}, u32[]{:S(2)}) collective-permute-start(bf16[256,768]{1,0:T(8,128)(2,1)} %collective-permute-done.2.q01.refs_8_), channel_id=1, source_target_pairs={{0,2},{2,0},{1,3},{3,1},{4,6},{6,4},{5,7},{7,5},{8,10},{10,8},{9,1... | collective-permute-start | bytes 1179656 | tf_op jit(solution)/shard_map/ppermute | solution.py:41
  91.5 26.0 %collective-permute-start.21 = (bf16[256,1024]{1,0:T(8,128)(2,1)S(1)}, bf16[256,1024]{1,0:T(8,128)(2,1)S(1)}, u32[]{:S(2)}, u32[]{:S(2)}) collective-permute-start(bf16[256,1024]{1,0:T(8,128)(2,1)S(1)} %get-tuple-element.105.refs_2_.u00), channel_id=1, source_target_pairs={{0,2},{2,0},{1,3},{3,1},{4,6},{6,4},{5,7},{7,5},{8,10},{10,8},{9,1... | collective-permute-start | bytes 1572872 | tf_op jit(solution)/shard_map/ppermute | solution.py:41
  96.9 20.6 %collective-permute-start.24 = (bf16[1024,256]{1,0:T(8,128)(2,1)S(1)}, bf16[1024,256]{1,0:T(8,128)(2,1)S(1)}, u32[]{:S(2)}, u32[]{:S(2)}) collective-permute-start(bf16[1024,256]{1,0:T(8,128)(2,1)S(1)} %get-tuple-element.103.refs_6_.d00), channel_id=1, source_target_pairs={{0,2},{2,0},{1,3},{3,1},{4,6},{6,4},{5,7},{7,5},{8,10},{10,8},{9,1... | collective-permute-start | bytes 1572872 | tf_op jit(solution)/shard_map/ppermute | solution.py:41
  96.9 15.7 %collective-permute-start.16 = (bf16[256,768]{1,0:T(8,128)(2,1)}, bf16[256,768]{1,0:T(8,128)(2,1)S(1)}, u32[]{:S(2)}, u32[]{:S(2)}) collective-permute-start(bf16[256,768]{1,0:T(8,128)(2,1)} %copy-done.11), channel_id=1, source_target_pairs={{0,2},{2,0},{1,3},{3,1},{4,6},{6,4},{5,7},{7,5},{8,10},{10,8},{9,1... | collective-permute-start | bytes 1179656 | tf_op jit(solution)/shard_map/ppermute | solution.py:41
  97.4 20.1 %collective-permute-start.22 = (bf16[256,1024]{1,0:T(8,128)(2,1)}, bf16[256,1024]{1,0:T(8,128)(2,1)S(1)}, u32[]{:S(2)}, u32[]{:S(2)}) collective-permute-start(bf16[256,1024]{1,0:T(8,128)(2,1)} %collective-permute-done.20.refs_3_.u01), channel_id=1, source_target_pairs={{0,2},{2,0},{1,3},{3,1},{4,6},{6,4},{5,7},{7,5},{8,10},{10,8},{9,1... | collective-permute-start | bytes 1572872 | tf_op jit(solution)/shard_map/ppermute | solution.py:41
  97.5 20.1 %collective-permute-start.25 = (bf16[1024,256]{1,0:T(8,128)(2,1)}, bf16[1024,256]{1,0:T(8,128)(2,1)S(1)}, u32[]{:S(2)}, u32[]{:S(2)}) collective-permute-start(bf16[1024,256]{1,0:T(8,128)(2,1)} %collective-permute-done.23.refs_7_.d01), channel_id=1, source_target_pairs={{0,2},{2,0},{1,3},{3,1},{4,6},{6,4},{5,7},{7,5},{8,10},{10,8},{9,1... | collective-permute-start | bytes 1572872 | tf_op jit(solution)/shard_map/ppermute | solution.py:41
  132.3 12.9 %collective-permute-start.27 = (bf16[1056,256]{1,0:T(8,128)(2,1)S(1)}, bf16[1056,256]{1,0:T(8,128)(2,1)S(1)}, u32[]{:S(2)}, u32[]{:S(2)}) collective-permute-start(bf16[1056,256]{1,0:T(8,128)(2,1)S(1)} %constant_dynamic-update-slice_fusion.15), channel_id=1, source_target_pairs={{0,2},{2,0},{1,3},{3,1},{4,6},{6,4},{5,7},{7,5},{8,10},{10,8},{9,1... | collective-permute-start | bytes 1622024 | tf_op jit(solution)/shard_map/ppermute | solution.py:41
  144.2 5.9 %collective-permute-start.29 = (bf16[2048,256]{1,0:T(8,128)(2,1)S(1)}, bf16[2048,256]{1,0:T(8,128)(2,1)S(1)}, u32[]{:S(2)}, u32[]{:S(2)}) collective-permute-start(bf16[2048,256]{1,0:T(8,128)(2,1)S(1)} %get-tuple-element.92), channel_id=1, source_target_pairs={{0,2},{2,0},{1,3},{3,1},{4,6},{6,4},{5,7},{7,5},{8,10},{10,8},{9,1... | collective-permute-start | bytes 3145736 | tf_op jit(solution)/shard_map/ppermute | solution.py:41
  144.6 6.7 %collective-permute-start.28 = (bf16[2048,256]{1,0:T(8,128)(2,1)S(1)}, bf16[2048,256]{1,0:T(8,128)(2,1)S(1)}, u32[]{:S(2)}, u32[]{:S(2)}) collective-permute-start(bf16[2048,256]{1,0:T(8,128)(2,1)S(1)} %get-tuple-element.90), channel_id=1, source_target_pairs={{0,2},{2,0},{1,3},{3,1},{4,6},{6,4},{5,7},{7,5},{8,10},{10,8},{9,1... | collective-permute-start | bytes 3145736 | tf_op jit(solution)/shard_map/ppermute | solution.py:41
  144.7 4.4 %collective-permute-start.26 = (bf16[1056,256]{1,0:T(8,128)(2,1)S(1)}, bf16[1056,256]{1,0:T(8,128)(2,1)S(1)}, u32[]{:S(2)}, u32[]{:S(2)}) collective-permute-start(bf16[1056,256]{1,0:T(8,128)(2,1)S(1)} %constant_dynamic-update-slice_fusion.5), channel_id=1, source_target_pairs={{0,2},{2,0},{1,3},{3,1},{4,6},{6,4},{5,7},{7,5},{8,10},{10,8},{9,1... | collective-permute-start | bytes 1622024 | tf_op jit(solution)/shard_map/ppermute | solution.py:41
  (60 other events, 260.6 us)
Sparse Core Ops, SparseCore 0:
  152.7 132.1 all-reduce.7

commit v2 on v1

v2 whole, which is shorter than its diff:
```python
import math

import jax
import jax.numpy as jnp
import numpy as np
from jax import lax
from jax.experimental import pallas as pl
from jax.experimental.pallas import tpu as pltpu
from jax.sharding import PartitionSpec as P

D = 512
HEADS = 16
HEAD_DIM = 32
FF = 2048
GRID = 14
WINDOW = 7
SHIFT = 3
TABLE = 169
LAYERS = 2
SPAN = WINDOW * WINDOW
IMAGE = GRID * GRID

EPS = 1e-05
NEG = -1000000000.0
HIGH = lax.Precision.HIGHEST
SCALE = 1.0 / math.sqrt(HEAD_DIM)

HALF = IMAGE // 2
PAD = 128
ROWS = 2 * PAD
ROLL = SHIFT * GRID
GROUP = 128 // HEAD_DIM
GROUPS = HEADS // GROUP
STACK = GROUP * PAD
CHUNK = 512
BF = jnp.bfloat16
F32 = jnp.float32


def swap(values, axis):
    return lax.ppermute(values, axis, [(0, 1), (1, 0)])


def mm(left, right):
    return lax.dot_general(left, right, (((1,), (0,)), ((), ())), preferred_element_type=F32)


def mm_nt(left, right):
    return lax.dot_general(left, right, (((1,), (1,)), ((), ())), preferred_element_type=F32)


def mm_tn(left, right):
    return lax.dot_general(left, right, (((0,), (0,)), ((), ())), preferred_element_type=F32)


def token_positions(layer):
    token = np.arange(HALF)
    line, column = token // GRID, token % GRID
    if layer % 2 == 1:
        column = (column - SHIFT) % GRID
    return line * WINDOW + column % WINDOW, column // WINDOW, line * GRID + column


def position_one_hot(layer):
    position, _, _ = token_positions(layer)
    picks = np.zeros((PAD, PAD), np.float32)
    picks[np.arange(HALF), position] = 1.0
    return picks


def mask_of(layer, region_ids):
    _, window, place = token_positions(layer)
    same = np.zeros((PAD, PAD), bool)
    same[:HALF, :HALF] = window[:, None] == window[None, :]
    same[HALF:, :HALF] = True
    allowed = jnp.broadcast_to(jnp.asarray(same)[None], (2, PAD, PAD))
    if layer % 2 == 1:
        ids = jnp.roll(region_ids.reshape(2, WINDOW, GRID), SHIFT, 2).reshape(2, HALF)
        ids = jnp.pad(ids, ((0, 0), (0, PAD - HALF)), constant_values=-1)
        pad_row = jnp.asarray(np.arange(PAD) >= HALF)[None, :, None]
        allowed = allowed & ((ids[:, :, None] == ids[:, None, :]) | pad_row)
    return jnp.where(allowed, 0.0, NEG).astype(F32)


def head_mask():
    lane = lax.broadcasted_iota(jnp.int32, (STACK, PAD), 1) // HEAD_DIM
    row = lax.broadcasted_iota(jnp.int32, (STACK, PAD), 0) // PAD
    return lane == row


def stack_heads(values, mask):
    tiled = jnp.concatenate([values] * GROUP, axis=0)
    return jnp.where(mask, tiled, jnp.zeros_like(tiled))


def unstack_heads(values, mask):
    kept = jnp.where(mask, values, 0.0)
    total = kept[0:PAD]
    for head in range(1, GROUP):
        total = total + kept[head * PAD : (head + 1) * PAD]
    return total


def norm_parts(values):
    average = jnp.mean(values, -1, keepdims=True)
    centred = values - average
    variance = jnp.mean(centred * centred, -1, keepdims=True)
    inverse = lax.rsqrt(variance + EPS)
    return centred * inverse, inverse


def norm_back(grad_normed, values, gain):
    xhat, inverse = norm_parts(values)
    scaled = grad_normed * gain
    mean_one = jnp.mean(scaled, -1, keepdims=True)
    mean_two = jnp.mean(scaled * xhat, -1, keepdims=True)
    grad_input = inverse * (scaled - mean_one - xhat * mean_two)
    return grad_input, jnp.sum(grad_normed * xhat, 0, keepdims=True), jnp.sum(grad_normed, 0, keepdims=True)


def split_halves(values):
    return values[:, : D // 2], values[:, D // 2 :]


def gelu_and_slope(values):
    below = 0.5 * (1.0 + lax.erf(values * (1.0 / math.sqrt(2.0))))
    density = jnp.exp(-0.5 * values * values) * (1.0 / math.sqrt(2.0 * math.pi))
    return values * below, below + values * density


TABLE_ROWS = 176

GAIN_ONE, GAIN_TWO, SHIFT_ONE, SHIFT_TWO, OUT_BIAS, DOWN_BIAS, Q_BIAS, V_BIAS, UP_BIAS = 0, 1, 2, 3, 4, 5, 6, 7, 8


def prep_kernel(
    parity_ref, misc_ref, misc_far, row_ref, row_far, index_ref, picks_ref,
    x_ref, grad_ref, small_zero, small_one, bias_zero, bias_one, pairs_ref, index_pad, flat,
):
    half, quarter = D // 2, D // 4
    even = parity_ref[0] == 0

    def ordered(values):
        low, high = values[:, :quarter], values[:, quarter:]
        return jnp.where(even, low, high), jnp.where(even, high, low)

    def lay_out(at):
        first, second = ordered(misc_far[at : at + 208, :].astype(F32))
        flat[:, 0:half] = misc_ref[at : at + 208, :].astype(F32)
        flat[:, half : half + quarter] = first
        flat[:, half + quarter :] = second

    x_ref[...] = jnp.zeros_like(x_ref)
    grad_ref[...] = jnp.zeros_like(grad_ref)
    lay_out(TOKENS_AT)
    x_ref[0:HALF, :] = flat[0:HALF, :]
    x_ref[PAD : PAD + HALF, :] = flat[HALF:IMAGE, :]
    lay_out(COT_AT)
    rest = HALF - ROLL
    grad_ref[0:HALF, :] = flat[ROLL : ROLL + HALF, :]
    grad_ref[PAD : PAD + rest, :] = flat[ROLL + HALF : IMAGE, :]
    grad_ref[PAD + rest : PAD + HALF, :] = flat[0:ROLL, :]

    near = misc_ref[SMALL_AT:MISC_ROWS, :].astype(F32)
    far_first, far_second = ordered(misc_far[SMALL_AT:MISC_ROWS, :].astype(F32))
    rows_near, rows_far = row_ref[...].astype(F32), row_far[...].astype(F32)
    for layer, small in enumerate((small_zero, small_one)):
        small[...] = jnp.zeros_like(small)

        def features(row, source):
            small[row : row + 1, 0:half] = near[source : source + 1]
            small[row : row + 1, half : half + quarter] = far_first[source : source + 1]
            small[row : row + 1, half + quarter :] = far_second[source : source + 1]

        for which in range(2):
            features(GAIN_ONE + which, 2 * layer + which)
            features(SHIFT_ONE + which, 4 + 2 * layer + which)
            for part, source in enumerate((rows_near, rows_far)):
                lanes = slice(part * half, (part + 1) * half)
                at = 2 * layer + which
                small[Q_BIAS + which : Q_BIAS + which + 1, lanes] = source[at : at + 1]
                line = UP_BIAS + 2 * part + which
                for piece in range(2):
                    at = 4 + 2 * (2 * which + piece) + layer
                    small[line : line + 1, piece * half : (piece + 1) * half] = source[at : at + 1]
        features(OUT_BIAS, 8 + layer)
        features(DOWN_BIAS, 10 + layer)

    heads = HEADS // 2
    tables = []
    for layer in range(LAYERS):
        for source in (rows_near, rows_far):
            tables.append(source[16 + layer * heads : 16 + (layer + 1) * heads, :TABLE_ROWS])
    table = jnp.concatenate(tables, 0).astype(BF)
    index_pad[...] = jnp.full(index_pad.shape, -1, jnp.int32)
    index_pad[0:SPAN, 0:SPAN] = index_ref[...]
    pairs_ref[SPAN:64] = jnp.zeros((64 - SPAN, LAYERS * HEADS, PAD), F32)
    for position in range(SPAN):
        wanted = index_pad[position : position + 1, :]
        hot = (lax.broadcasted_iota(jnp.int32, (TABLE_ROWS, PAD), 0) == wanted).astype(F32).astype(BF)
        pairs_ref[position] = mm(table, hot)
    for layer, bias_ref in enumerate((bias_zero, bias_one)):
        picks = picks_ref[layer]
        for head in range(HEADS):
            bias = pairs_ref[:, layer * HEADS + head, :]
            spread = mm(picks[:, :64], bias.astype(BF)).astype(BF)
            bias_ref[head] = mm_nt(spread, picks)


class Fetch:
    def __init__(self, copies, ref):
        self.copies, self.ref, self.waiting = copies, ref, True

    def start(self):
        for copy in self.copies:
            copy.start()

    def ready(self):
        if self.waiting:
            self.waiting = False
            for copy in self.copies:
                copy.wait()
        return self.ref

    def __getitem__(self, index):
        return self.ready()[index]


def whole_fetch(source, room, sems, at):
    return Fetch([pltpu.make_async_copy(source, room, sems.at[at])], room)


def attn_weights(layer, sources, rooms, sems, at):
    half, quarter = D // 2, D // 4
    qkv, out, from_col, from_dp, whole_row, from_col_row, from_dp_row = sources
    qkvs, outs = [], []
    whole_at = layer * TAIL_AT
    for part, packs in enumerate(((from_col, from_dp), (from_col_row, from_dp_row))):
        room_qkv, room_out = rooms[2 * part], rooms[2 * part + 1]
        pairs, pairs_out = [], []
        for kind in range(3):
            lines = slice(whole_at + QKV_AT + kind * half, whole_at + QKV_AT + (kind + 1) * half)
            source = qkv.at[layer, kind] if part == 0 else whole_row.at[lines, :]
            pairs.append((source, room_qkv.at[kind, 0:half, :]))
        source = out.at[layer] if part == 0 else whole_row.at[whole_at + OUT_AT : whole_at + TAIL_AT, :]
        pairs_out.append((source, room_out.at[:, 0:half]))
        for slot, pack in enumerate(packs):
            first = half + slot * quarter
            for kind in range(3):
                pairs.append(
                    (
                        pack.at[kind * quarter : (kind + 1) * quarter, :],
                        room_qkv.at[kind, first : first + quarter, :],
                    )
                )
            for side in range(2):
                lanes = slice(side * quarter, (side + 1) * quarter)
                pairs_out.append((pack.at[3 * quarter : 4 * quarter, lanes], room_out.at[lanes, first : first + quarter]))
        for found, room, list_of in ((pairs, room_qkv, qkvs), (pairs_out, room_out, outs)):
            copies = []
            for source, target in found:
                copies.append(pltpu.make_async_copy(source, target, sems.at[at]))
                at += 1
            list_of.append(Fetch(copies, room))
    return qkvs, outs


ATTN_COPIES = 2 * (9 + 5)
ATTN_ROOMS = [((3, D, D // 2), BF), ((D // 2, D), BF)] * 2


def ffn_weights(layer, sources, rooms, sems, at):
    half, quarter, wide = D // 2, D // 4, FF // 4
    up, down, from_col, from_dp, whole_row, from_col_row, from_dp_row = sources
    ups, downs = [], []
    whole_at = layer * TAIL_AT
    for part, packs in enumerate(((from_col, from_dp), (from_col_row, from_dp_row))):
        room_up, room_down = rooms[2 * part], rooms[2 * part + 1]
        pairs, pairs_down = [], []
        for piece in range(4):
            lanes = slice(piece * half, (piece + 1) * half)
            lines = slice(whole_at + UP_AT + piece * half, whole_at + UP_AT + (piece + 1) * half)
            source = up.at[layer, :, lanes] if part == 0 else whole_row.at[lines, :]
            pairs.append((source, room_up.at[0:half, lanes]))
        source = down.at[layer] if part == 0 else whole_row.at[whole_at + DOWN_AT : whole_at + UP_AT, :]
        pairs_down.append((source, room_down.at[:, 0:half]))
        for slot, pack in enumerate(packs):
            first = half + slot * quarter
            for piece in range(4):
                lanes = slice(piece * half, (piece + 1) * half)
                pairs.append(
                    (
                        pack.at[D + piece * quarter : D + (piece + 1) * quarter, :],
                        room_up.at[first : first + quarter, lanes],
                    )
                )
            for side in range(2):
                lanes = slice(side * quarter, (side + 1) * quarter)
                pairs_down.append(
                    (
                        pack.at[2 * D :, lanes],
                        room_down.at[side * wide : (side + 1) * wide, first : first + quarter],
                    )
                )
        for found, room, list_of in ((pairs, room_up, ups), (pairs_down, room_down, downs)):
            copies = []
            for source, target in found:
                copies.append(pltpu.make_async_copy(source, target, sems.at[at]))
                at += 1
            list_of.append(Fetch(copies, room))
    return ups, downs


FFN_COPIES = 2 * (12 + 5)
FFN_ROOMS = [((D, FF // 2), BF), ((FF // 2, D), BF)] * 2


def misc_kernel(qv_bias, up_bias, table, misc_row):
    half = D // 2
    rows = [qv_bias[0], qv_bias[1]] + [up_bias[:, piece * half : (piece + 1) * half] for piece in range(4)]
    rows = [row.astype(F32) for row in rows] + [jnp.zeros((4, half), F32)]
    misc_row[0:16, :] = jnp.concatenate(rows, 0).astype(BF)
    tables = jnp.concatenate([table[layer].astype(F32) for layer in range(LAYERS)], 0)
    misc_row[16:32, :] = jnp.pad(tables, ((0, 0), (0, half - TABLE))).astype(BF)


def pack_kernel(
    parity_ref, qkv, out, up, down, tokens, cot, gain, shift, out_bias, down_bias, _,
    misc_out, pack_zero, pack_one, whole, *rest,
):
    rooms, results, (in_sems, out_sems) = rest[:8], rest[8:11], rest[11:]
    half, quarter = D // 2, D // 4
    even = parity_ref[0] == 0
    fetched = []
    for layer in range(LAYERS):
        for number, source in enumerate((qkv, out, up, down)):
            at = 4 * layer + number
            fetched.append(whole_fetch(source.at[layer], rooms[at], in_sems, at))
    for item in fetched:
        item.start()
    sent = []

    def send(source, target):
        copy = pltpu.make_async_copy(source, target, out_sems.at[len(sent)])
        copy.start()
        sent.append(copy)

    misc = results[0]
    misc[...] = jnp.zeros_like(misc)
    misc[TOKENS_AT : TOKENS_AT + IMAGE, :] = tokens[...]
    misc[COT_AT : COT_AT + IMAGE, :] = cot[...]
    rows = [gain[0], gain[1], shift[0], shift[1], out_bias[...], down_bias[...]]
    misc[SMALL_AT : SMALL_AT + 12, :] = jnp.concatenate([row.astype(F32) for row in rows], 0).astype(BF)
    send(misc, misc_out)
    for layer in range(LAYERS):
        pack = results[1 + layer]
        at = layer * TAIL_AT
        qkv_l, out_l, up_l, down_l = [item.ready() for item in fetched[4 * layer : 4 * layer + 4]]
        for kind in range(3):
            pack[kind * quarter : (kind + 1) * quarter, :] = jnp.where(
                even, qkv_l[kind, 0:quarter, :], qkv_l[kind, quarter:half, :]
            )
        chosen = jnp.where(even, out_l[:, 0:quarter], out_l[:, quarter:half])
        pack[3 * quarter : 4 * quarter, 0:quarter] = chosen[0:quarter]
        pack[3 * quarter : 4 * quarter, quarter:half] = chosen[quarter:half]
        chosen = jnp.where(even, up_l[0:quarter, :], up_l[quarter:half, :])
        for piece in range(4):
            lines = slice(D + piece * quarter, D + (piece + 1) * quarter)
            pack[lines, :] = chosen[:, piece * half : (piece + 1) * half]
        chosen = jnp.where(even, down_l[:, 0:quarter], down_l[:, quarter:half])
        pack[2 * D :, 0:quarter] = chosen[0 : FF // 4]
        pack[2 * D :, quarter:half] = chosen[FF // 4 :]
        send(pack, (pack_zero, pack_one)[layer])
        send(down_l, whole.at[at + DOWN_AT : at + UP_AT, :])
        for piece in range(4):
            lines = slice(at + UP_AT + piece * half, at + UP_AT + (piece + 1) * half)
            send(up_l.at[:, piece * half : (piece + 1) * half], whole.at[lines, :])
        for kind in range(3):
            send(qkv_l.at[kind], whole.at[at + QKV_AT + kind * half : at + QKV_AT + (kind + 1) * half, :])
        send(out_l, whole.at[at + OUT_AT : at + TAIL_AT, :])
    for copy in sent:
        copy.wait()


def after_kernel(*refs):
    pass


def after(value, token):
    (result,) = call(
        after_kernel, [(value.shape, value.dtype)], [], [value, token], 0, [ANY] * 2, [ANY], limit=1, aliases={0: 0}
    )
    return result


TOKENS_AT, COT_AT, SMALL_AT, MISC_ROWS = 0, 208, 416, 432


def combine_kernel(place_ref, ffn_keep, ffn_got, keep, got, tail_keep, tail_got, *rest):
    pieces_ref, one_ref, two_ref, flat = rest[-4:]
    flat[0:FF, :] = ffn_keep[...].astype(F32) + ffn_got[...].astype(F32)
    flat[FF : FF + 2 * D, :] = keep[...].astype(F32) + got[...].astype(F32)
    flat[TAIL_AT:, :] = jnp.zeros((BLOCK_ROWS - TAIL_AT, D // 2), F32)
    flat[TAIL_AT : TAIL_AT + 24, :] = tail_keep[...] + tail_got[...]
    for number in range(2 * RING):
        pieces_ref[number] = flat[number * PIECE : (number + 1) * PIECE, :].astype(BF)
    place = place_ref[0]
    one_ref[...] = pieces_ref[lax.rem(place + RING - 1, RING)]
    two_ref[...] = pieces_ref[RING + lax.rem(place + 1, RING)]


def attn_fwd_kernel(
    layer, weights, x_ref, small_ref, bias_ref, mask_ref, mid_ref, normed_ref, qkv_ref, probs_ref, att_ref,
):
    qkv_weights, out_weights = weights
    x = x_ref[...]
    xhat, _ = norm_parts(x)
    normed = (
        xhat * small_ref[GAIN_ONE : GAIN_ONE + 1] + small_ref[SHIFT_ONE : SHIFT_ONE + 1]
    ).astype(BF)
    normed_ref[...] = normed
    half = D // 2
    for part in range(2):
        lanes = slice(part * half, (part + 1) * half)
        for kind in range(3):
            projected = mm(normed, qkv_weights[part][kind])
            if kind != 1:
                row = Q_BIAS if kind == 0 else V_BIAS
                projected = projected + small_ref[row : row + 1, lanes]
            qkv_ref[part, :, kind * half : (kind + 1) * half] = projected.astype(BF)
    mask = head_mask()
    for group in range(GROUPS):
        part, lane = group // 2, (group % 2) * 128
        bias = bias_ref[group * GROUP : (group + 1) * GROUP]
        for side in range(2):
            rows = slice(side * PAD, (side + 1) * PAD)
            query = qkv_ref[part, rows, lane : lane + 128]
            key = qkv_ref[part, rows, half + lane : half + lane + 128]
            value = qkv_ref[part, rows, 2 * half + lane : 2 * half + lane + 128]
            scores = mm_nt(stack_heads(query, mask), key).reshape(GROUP, PAD, PAD) * SCALE
            scores = scores + (bias + mask_ref[side][None])
            peak = jnp.max(scores, -1, keepdims=True)
            expos = jnp.exp(scores - peak)
            totals = jnp.sum(expos, -1, keepdims=True)
            probs = (expos / totals).astype(BF).reshape(STACK, PAD)
            probs_ref[side, group] = probs
            attended = unstack_heads(mm(probs, value), mask)
            att_ref[rows, group * 128 : (group + 1) * 128] = attended.astype(BF)
    first, second = split_halves(att_ref[...])
    mixed = mm(first, out_weights[0][...]) + mm(second, out_weights[1][...])
    mid_ref[...] = x + mixed + small_ref[OUT_BIAS : OUT_BIAS + 1]


def roll_rows(values_ref, result_ref):
    rest = HALF - ROLL
    result_ref[...] = jnp.zeros_like(result_ref)
    for side in range(2):
        here, there = side * PAD, (1 - side) * PAD
        result_ref[here : here + rest, :] = values_ref[here + ROLL : here + HALF, :]
        result_ref[here + rest : here + HALF, :] = values_ref[there : there + ROLL, :]


def unroll_rows(values_ref, result_ref):
    rest = HALF - ROLL
    result_ref[...] = jnp.zeros_like(result_ref)
    for side in range(2):
        here, there = side * PAD, (1 - side) * PAD
        result_ref[here + ROLL : here + HALF, :] = values_ref[here : here + rest, :]
        result_ref[here : here + ROLL, :] = values_ref[there + rest : there + HALF, :]


def clear_padding(values):
    row = lax.broadcasted_iota(jnp.int32, values.shape, 0) % PAD
    return jnp.where(row < HALF, values, 0.0)


def ffn_fwd_kernel(
    layer, weights, mid_ref, small_ref, x_ref, normed_ref, slope_ref, hidden_ref, scratch, flat,
):
    up_weights, down_weights = weights
    half = D // 2
    middle = mid_ref[...]
    xhat, _ = norm_parts(middle)
    normed = (
        xhat * small_ref[GAIN_TWO : GAIN_TWO + 1] + small_ref[SHIFT_TWO : SHIFT_TWO + 1]
    ).astype(BF)
    normed_ref[...] = normed
    total = jnp.zeros((ROWS, D), F32)
    per_part = FF // 2 // CHUNK
    for chunk in range(FF // CHUNK):
        part, at = chunk // per_part, (chunk % per_part) * CHUNK
        pre = mm(normed, up_weights[part][:, at : at + CHUNK]) + small_ref[UP_BIAS + chunk : UP_BIAS + chunk + 1]
        hidden, slope = gelu_and_slope(pre)
        hidden = hidden.astype(BF)
        slope_ref[:, chunk * CHUNK : (chunk + 1) * CHUNK] = slope.astype(BF)
        hidden_ref[:, chunk * CHUNK : (chunk + 1) * CHUNK] = hidden
        total = total + mm(hidden, down_weights[part][at : at + CHUNK, :])
    result = middle + total + small_ref[DOWN_BIAS : DOWN_BIAS + 1]
    scratch[...] = result
    if layer % 2 == 0:
        roll_rows(scratch, x_ref)
    else:
        rest = HALF - ROLL
        flat[ROLL : ROLL + HALF, :] = scratch[0:HALF, 0:half]
        flat[ROLL + HALF : IMAGE, :] = scratch[PAD : PAD + rest, 0:half]
        flat[0:ROLL, :] = scratch[PAD + rest : PAD + HALF, 0:half]
        x_ref[...] = flat[0:IMAGE, :].astype(BF)


def ffn_bwd_kernel(
    layer, weights, grad_ref, slope_ref, hidden_ref, normed_ref, small_ref, mid_ref,
    grad_mid_ref, keep_ref, send_ref, small_keep_ref, small_send_ref,
):
    up_weights, down_weights = weights
    half = D // 2
    grad = grad_ref[...]
    grad_down = grad.astype(BF)
    near = grad_down[:, :half]
    per_part = FF // 2 // CHUNK
    outs = (keep_ref, send_ref)
    small_outs = (small_keep_ref, small_send_ref)
    grad_normed = jnp.zeros((ROWS, D), F32)
    for chunk in range(FF // CHUNK):
        part, at = chunk // per_part, (chunk % per_part) * CHUNK
        at_lanes = slice(at, at + CHUNK)
        lanes = slice(chunk * CHUNK, (chunk + 1) * CHUNK)
        grad_hidden = mm_nt(grad_down, down_weights[part][at_lanes, :])
        grad_pre_wide = (grad_hidden * slope_ref[:, lanes].astype(F32)).astype(BF)
        outs[part][at : at + CHUNK, :] = mm_tn(hidden_ref[:, lanes], near).astype(BF)
        grad_up = mm_tn(normed_ref[:, :half], grad_pre_wide).astype(BF)
        bias_sum = jnp.sum(grad_pre_wide.astype(F32), 0, keepdims=True)
        for piece in range(CHUNK // half):
            place = FF // 2 + (at // half + piece) * half
            outs[part][place : place + half, :] = grad_up[:, piece * half : (piece + 1) * half]
            line = 3 + at // half + piece
            small_outs[part][line : line + 1, :] = bias_sum[:, piece * half : (piece + 1) * half]
        grad_normed = grad_normed + mm_nt(grad_pre_wide, up_weights[part][:, at_lanes])
    grad_input, grad_gain, grad_shift = norm_back(
        grad_normed, mid_ref[...], small_ref[GAIN_TWO : GAIN_TWO + 1]
    )
    grad_mid_ref[...] = clear_padding(grad + grad_input)
    down_bias = jnp.sum(near.astype(F32), 0, keepdims=True)
    for small in small_outs:
        small[0:1, :] = down_bias
        small[1:2, :] = grad_gain[:, :half]
        small[2:3, :] = grad_shift[:, :half]
        small[7:8, :] = jnp.zeros((1, half), F32)


def attn_bwd_kernel(
    layer, weights, grad_mid_ref, att_ref, qkv_ref, probs_ref, picks_ref, picks_t_ref, normed_ref, small_ref, x_ref,
    grad_ref, keep_ref, send_ref, small_keep_ref, small_send_ref, table_ref, grad_qkv, scratch, flat,
):
    qkv_weights, out_weights = weights
    half = D // 2
    grad_mid = grad_mid_ref[...]
    grad_att = grad_mid.astype(BF)
    near = grad_att[:, :half]
    outs = (keep_ref, send_ref)
    small_outs = (small_keep_ref, small_send_ref)
    mask = head_mask()
    grad_normed = jnp.zeros((ROWS, D), F32)
    for part in range(2):
        grad_attended = mm_nt(grad_att, out_weights[part][...]).astype(BF)
        outs[part][3 * half : 4 * half, :] = mm_tn(att_ref[:, part * half : (part + 1) * half], near).astype(BF)
        for inner in range(2):
            group, lane = part * 2 + inner, inner * 128
            tables = [jnp.zeros((64, PAD), F32) for _ in range(GROUP)]
            for side in range(2):
                rows = slice(side * PAD, (side + 1) * PAD)
                query = stack_heads(qkv_ref[part, rows, lane : lane + 128], mask)
                key = qkv_ref[part, rows, half + lane : half + lane + 128]
                value = qkv_ref[part, rows, 2 * half + lane : 2 * half + lane + 128]
                grad_out = stack_heads(grad_attended[rows, lane : lane + 128], mask)
                probs_low = probs_ref[side, group]
                probs = probs_low.astype(F32)
                grad_probs = mm_nt(grad_out, value)
                weighted = jnp.sum(probs * grad_probs, -1, keepdims=True)
                grad_scores = (probs * (grad_probs - weighted)).astype(BF)
                grad_value = mm_tn(probs_low, grad_out)
                grad_query = unstack_heads(mm(grad_scores, key), mask) * SCALE
                grad_key = mm_tn(grad_scores, query) * SCALE
                grad_qkv[part, rows, lane : lane + 128] = grad_query.astype(BF)
                grad_qkv[part, rows, half + lane : half + lane + 128] = grad_key.astype(BF)
                grad_qkv[part, rows, 2 * half + lane : 2 * half + lane + 128] = grad_value.astype(BF)
                picked = mm(grad_scores, picks_ref[...]).astype(BF)
                for head in range(GROUP):
                    tables[head] = tables[head] + mm(picks_t_ref[0:64, :], picked[head * PAD : (head + 1) * PAD])
            for head in range(GROUP):
                table_ref[group * GROUP + head] = tables[head][:56]
        for kind in range(3):
            lanes = slice(kind * half, (kind + 1) * half)
            grads = grad_qkv[part, :, lanes]
            outs[part][kind * half : (kind + 1) * half, :] = mm_tn(normed_ref[:, :half], grads).astype(BF)
            grad_normed = grad_normed + mm_nt(grads, qkv_weights[part][kind])
            if kind != 1:
                line = 3 + kind // 2
                small_outs[part][line : line + 1, :] = jnp.sum(grads.astype(F32), 0, keepdims=True)
    grad_input, grad_gain, grad_shift = norm_back(
        grad_normed, x_ref[...], small_ref[GAIN_ONE : GAIN_ONE + 1]
    )
    total = clear_padding(grad_mid + grad_input)
    scratch[...] = total
    if layer % 2 == 1:
        unroll_rows(scratch, grad_ref)
    else:
        flat[0:HALF, :] = scratch[0:HALF, 0:half]
        flat[HALF:IMAGE, :] = scratch[PAD : PAD + HALF, 0:half]
        grad_ref[...] = flat[0:IMAGE, :].astype(BF)
    out_bias = jnp.sum(near.astype(F32), 0, keepdims=True)
    for small in small_outs:
        small[0:1, :] = out_bias
        small[1:2, :] = grad_gain[:, :half]
        small[2:3, :] = grad_shift[:, :half]
        small[5:8, :] = jnp.zeros((3, half), F32)


DOWN_AT, UP_AT, QKV_AT, OUT_AT, TAIL_AT = 0, 1024, 2048, 2816, 3072
BLOCK_ROWS = 3200
RING = 8
PIECE = BLOCK_ROWS // (2 * RING)


def unpack_kernel(count, *refs):
    starts = refs[0]
    pieces = refs[1 : 1 + 2 * count]
    (qkv_ref, qv_ref, out_ref, out_bias_ref, up_ref, up_bias_ref, down_ref, down_bias_ref,
     gain_ref, shift_ref, table_ref, block) = refs[1 + 2 * count :]
    half = D // 2
    for layer in range(LAYERS):
        for number in range(count):
            piece = pieces[layer * count + number]
            size = piece.shape[0]
            at = pl.multiple_of(starts[number], 8)
            block[pl.ds(at, size), :] = piece[...].astype(F32)
        down_ref[layer] = block[DOWN_AT : DOWN_AT + FF // 2, :]
        for piece in range(4):
            up_ref[layer, :, piece * half : (piece + 1) * half] = block[
                UP_AT + piece * half : UP_AT + (piece + 1) * half, :
            ]
        for kind in range(3):
            qkv_ref[layer, kind] = block[QKV_AT + kind * half : QKV_AT + (kind + 1) * half, :]
        out_ref[layer] = block[OUT_AT : OUT_AT + half, :]
        tail = block[TAIL_AT : TAIL_AT + 24, :]
        down_bias_ref[layer : layer + 1, :] = tail[0:1]
        gain_ref[layer, 1:2, :] = tail[1:2]
        shift_ref[layer, 1:2, :] = tail[2:3]
        for piece in range(4):
            up_bias_ref[layer : layer + 1, piece * half : (piece + 1) * half] = tail[3 + piece : 4 + piece]
        out_bias_ref[layer : layer + 1, :] = tail[8:9]
        gain_ref[layer, 0:1, :] = tail[9:10]
        shift_ref[layer, 0:1, :] = tail[10:11]
        qv_ref[layer] = tail[11:13]
        table_ref[layer] = tail[16:24, :TABLE]


ANY = pl.BlockSpec(memory_space=pl.ANY)
VMEM = pl.BlockSpec(memory_space=pltpu.VMEM)
SMEM = pl.BlockSpec(memory_space=pltpu.SMEM)


def call(kernel, outs, scratch, args, micros, specs=None, out_specs=None, limit=40, aliases=None):
    return pl.pallas_call(
        kernel,
        out_shape=[jax.ShapeDtypeStruct(shape, kind) for shape, kind in outs],
        in_specs=specs or [VMEM] * len(args),
        out_specs=out_specs or [VMEM] * len(outs),
        scratch_shapes=scratch,
        input_output_aliases=aliases or {},
        compiler_params=pltpu.CompilerParams(vmem_limit_bytes=limit * 1024 * 1024),
        cost_estimate=pl.CostEstimate(flops=int(micros * 1.15e6), bytes_accessed=0, transcendentals=0),
    )(*args)


def layer_call(kernel, layer, outs, scratch, weights, args, micros, attn, behind=()):
    rooms, weight_copies, load = (
        (ATTN_ROOMS, ATTN_COPIES, attn_weights) if attn else (FFN_ROOMS, FFN_COPIES, ffn_weights)
    )

    def run(*refs):
        refs = list(refs)

        def take(number):
            taken = refs[:number]
            del refs[:number]
            return taken

        weight_refs, arg_refs, _, out_refs = take(len(weights)), take(len(args)), take(len(behind)), take(len(outs))
        weight_rooms, arg_rooms, others, (sems,) = take(len(rooms)), take(len(args)), take(len(scratch)), take(1)
        fetched = [
            whole_fetch(ref, room, sems, weight_copies + at) for at, (ref, room) in enumerate(zip(arg_refs, arg_rooms))
        ]
        loaded = load(layer, weight_refs, weight_rooms, sems, 0)
        if kernel in FORWARD:
            pending = fetched[:2] + loaded[0] + fetched[2:] + loaded[1]
        else:
            pending = fetched[:1] + loaded[1] + fetched[1:] + loaded[0]
        for item in pending:
            item.start()
        kernel(layer, loaded, *fetched, *out_refs, *others)
        for item in pending:
            item.ready()

    spaces = (
        [pltpu.VMEM(shape, kind) for shape, kind in rooms]
        + [pltpu.VMEM(a.shape, a.dtype) for a in args]
        + scratch
        + [pltpu.SemaphoreType.DMA((weight_copies + len(args),))]
    )
    operands = [*weights, *args, *behind]
    return call(run, outs, spaces, operands, micros, [ANY] * len(operands))


FORWARD = (attn_fwd_kernel, ffn_fwd_kernel)


def part_of(kernel, layer):
    def run(*refs):
        return kernel(layer, *refs)

    return run


def ring_perms():
    order = [0, 2, 4, 6, 7, 5, 3, 1]
    onward = [(order[i], order[(i + 1) % RING]) for i in range(RING)]
    return onward, [(b, a) for a, b in onward]


def ring_sum(pieces, place, one, two):
    onward, back = ring_perms()
    for step in range(RING - 1):
        one, two = lax.ppermute(one, "dp", onward), lax.ppermute(two, "dp", back)
        one = one + pick(pieces, (place - 2 - step) % RING)
        two = two + pick(pieces, RING + (place + 2 + step) % RING)
    return ring_gather(one, two)


def pick(values, index):
    return lax.dynamic_index_in_dim(values, index, 0, keepdims=False)


def ring_gather(one, two):
    onward, back = ring_perms()
    pieces = [one, two]
    for _ in range(RING - 1):
        one, two = lax.ppermute(one, "dp", onward), lax.ppermute(two, "dp", back)
        pieces += [one, two]
    return pieces


def piece_starts(place):
    starts = []
    for step in range(RING):
        starts += [((place - step) % RING) * PIECE, (RING + (place + step) % RING) * PIECE]
    return jnp.stack(starts).astype(jnp.int32)


def on_device(
    ring, tokens, cotangent, qkv_weight, qv_bias, out_weight, out_bias, up_weight, up_bias,
    down_weight, down_bias, norm_gain, norm_shift, bias_table, index_map, region_ids,
):
    half, quarter = D // 2, D // 4
    device = lax.axis_index("dp")
    parity = device % 2
    neighbours = [(i, i ^ 1) for i in range(lax.axis_size("dp"))]

    wholes = [qkv_weight.transpose(0, 2, 1, 3), out_weight, up_weight, down_weight]
    parity_ref = parity.astype(jnp.int32).reshape(1)
    (misc_row,) = call(
        misc_kernel, [((32, half), BF)], [], [qv_bias, up_bias, bias_table.transpose(0, 2, 1)], 1
    )
    row_far = swap(misc_row, "row")
    sources = [*wholes, tokens, cotangent, norm_gain, norm_shift, out_bias, down_bias]
    pack_outs = [((MISC_ROWS, half), BF), ((3 * D, half), BF), ((3 * D, half), BF)]
    misc, *packs, whole = call(
        pack_kernel,
        [*pack_outs, ((LAYERS * TAIL_AT, half), BF)],
        [pltpu.VMEM(value.shape[1:], value.dtype) for value in wholes] * LAYERS
        + [pltpu.VMEM(shape, kind) for shape, kind in pack_outs]
        + [pltpu.SemaphoreType.DMA((8,)), pltpu.SemaphoreType.DMA((21,))],
        [parity_ref, *sources, misc_row],
        3,
        [SMEM] + [ANY] * 4 + [VMEM] * 6 + [ANY],
        [ANY] * 4,
        limit=60,
    )
    whole_row, misc_far = swap(whole, "row"), swap(misc, "col")
    from_col = [swap(pack, "col") for pack in packs]
    from_col[0] = after(from_col[0], misc_far)

    def block(pack, token):
        from_dp = lax.ppermute(pack, "dp", neighbours)
        if token is not None:
            from_dp = after(from_dp, token)
        return [pack, from_dp, whole_row, swap(pack, "row"), swap(from_dp, "row")]

    blocks = [block(from_col[0], None)]
    picks = np.stack([position_one_hot(layer) for layer in range(LAYERS)])
    picks_t = [jnp.asarray(pick.T, BF) for pick in picks]
    picks_all = jnp.asarray(picks, BF)
    picks = [jnp.asarray(pick, BF) for pick in picks]
    masks = [mask_of(layer, region_ids) for layer in range(LAYERS)]
    wide = ((ROWS, D), F32)
    x, grad, *rest = call(
        prep_kernel,
        [wide, wide, ((16, D), F32), ((16, D), F32), ((HEADS, PAD, PAD), F32), ((HEADS, PAD, PAD), F32)],
        [
            pltpu.VMEM((64, LAYERS * HEADS, PAD), F32), pltpu.VMEM((56, PAD), jnp.int32),
            pltpu.VMEM((208, D), F32),
        ],
        [parity_ref, misc, misc_far, misc_row, row_far, index_map, picks_all],
        4,
        [SMEM] + [VMEM] * 6,
    )
    smalls, bias = rest[:2], rest[2:4]
    from_col[1] = after(from_col[1], x)

    image = ((IMAGE, half), BF)
    saved = []
    for layer in range(LAYERS):
        middle, normed_one, qkv, probs, att = layer_call(
            attn_fwd_kernel,
            layer,
            [
                wide, ((ROWS, D), BF), ((2, ROWS, 3 * half), BF),
                ((2, GROUPS, STACK, PAD), BF), ((ROWS, D), BF),
            ],
            [],
            [*wholes[:2], *blocks[layer]],
            [x, smalls[layer], bias[layer], masks[layer]],
            4,
            True,
        )
        result, normed_two, pre, hidden = layer_call(
            ffn_fwd_kernel,
            layer,
            [wide if layer < LAYERS - 1 else image, ((ROWS, D), BF), ((ROWS, FF), BF), ((ROWS, FF), BF)],
            [pltpu.VMEM((ROWS, D), F32), pltpu.VMEM((200, half), F32)],
            [*wholes[2:], *blocks[layer]],
            [middle, smalls[layer]],
            4,
            False,
        )
        if layer == 0:
            blocks.append(block(from_col[1], result))
        saved.append((x, middle, normed_one, qkv, probs, att, normed_two, pre, hidden))
        x = result
    output = x

    heads = HEADS // 2
    one_hot = (index_map[:, :, None] == jnp.arange(256, dtype=jnp.int32)).astype(F32).reshape(SPAN * SPAN, 256)
    sums = [None] * LAYERS
    place = jnp.where(parity == 0, device // 2, RING - 1 - device // 2)
    place_ref = place.astype(jnp.int32).reshape(1)
    for layer in reversed(range(LAYERS)):
        x_in, middle, normed_one, qkv, probs, att, normed_two, pre, hidden = saved[layer]
        small_shape = ((8, half), F32)
        grad_mid, ffn_keep, ffn_send, small_keep, small_send = layer_call(
            ffn_bwd_kernel,
            layer,
            [wide, ((FF, half), BF), ((FF, half), BF), small_shape, small_shape],
            [],
            [*wholes[2:], *blocks[layer]],
            [grad, pre, hidden, normed_two, smalls[layer], middle],
            5,
            False,
        )
        ffn_got = swap(ffn_send, "row")
        grad, keep, send, att_keep, att_send, counts = layer_call(
            attn_bwd_kernel,
            layer,
            [
                wide if layer > 0 else image, ((2 * D, half), BF), ((2 * D, half), BF), small_shape, small_shape,
                ((HEADS, 56, PAD), F32),
            ],
            [pltpu.VMEM((2, ROWS, 3 * half), BF), pltpu.VMEM((ROWS, D), F32), pltpu.VMEM((200, half), F32)],
            [*wholes[:2], *blocks[layer]],
            [grad_mid, att, qkv, probs, picks[layer], picks_t[layer], normed_one, smalls[layer], x_in],
            6,
            True,
        )
        got = swap(send, "row")
        table = jnp.dot(counts[:, :SPAN, :SPAN].reshape(HEADS, SPAN * SPAN), one_hot, precision=HIGH)
        tail_keep = jnp.concatenate([small_keep, att_keep, table[:heads]], 0)
        tail_send = jnp.concatenate([small_send, att_send, table[heads:]], 0)
        pieces, one, two = call(
            combine_kernel,
            [((2 * RING, PIECE, half), BF), ((PIECE, half), BF), ((PIECE, half), BF)],
            [pltpu.VMEM((BLOCK_ROWS, half), F32)],
            [place_ref, ffn_keep, ffn_got, keep, got, tail_keep, swap(tail_send, "row")],
            2,
            [SMEM] + [VMEM] * 6,
            limit=24,
        )
        if ring:
            sums[layer] = ring_sum(pieces, place, one, two)
        else:
            sums[layer] = [lax.psum(pieces.reshape(BLOCK_ROWS, half), "dp")]
    input_grad = grad

    count = len(sums[0])
    starts = piece_starts(place) if ring else jnp.zeros((1,), jnp.int32)
    qkv, qv, outw, outb, up, upb, down, downb, gain, shift, table = call(
        part_of(unpack_kernel, count),
        [
            ((LAYERS, 3, half, half), F32), ((LAYERS, 2, half), F32), ((LAYERS, half, half), F32),
            ((LAYERS, half), F32), ((LAYERS, half, FF // 2), F32), ((LAYERS, FF // 2), F32),
            ((LAYERS, FF // 2, half), F32), ((LAYERS, half), F32), ((LAYERS, 2, half), F32),
            ((LAYERS, 2, half), F32), ((LAYERS, heads, TABLE), F32),
        ],
        [pltpu.VMEM((BLOCK_ROWS, half), F32)],
        [starts, *sums[0], *sums[1]],
        4,
        [SMEM] + [VMEM] * (2 * count),
    )
    return (
        output, input_grad, qkv.transpose(0, 2, 1, 3), qv, outw, outb, up, upb, down, downb, gain, shift,
        table.transpose(0, 2, 1),
    )


def solution(mesh):
    in_specs = (
        P(("dp", "row"), "col"),
        P(("dp", "row"), "col"),
        P(None, "col", None, "row"),
        P(None, None, "row"),
        P(None, "row", "col"),
        P(None, "col"),
        P(None, "col", "row"),
        P(None, "row"),
        P(None, "row", "col"),
        P(None, "col"),
        P(None, None, "col"),
        P(None, None, "col"),
        P(None, None, "row"),
        P(),
        P(),
    )
    out_specs = (
        P(("dp", "row"), "col"),
        P(("dp", "row"), "col"),
        P(None, "col", None, "row"),
        P(None, None, "row"),
        P(None, "row", "col"),
        P(None, "col"),
        P(None, "col", "row"),
        P(None, "row"),
        P(None, "row", "col"),
        P(None, "col"),
        P(None, None, "col"),
        P(None, None, "col"),
        P(None, None, "row"),
    )
    ring = mesh.shape["dp"] == RING
    return jax.shard_map(
        part_of(on_device, ring), mesh=mesh, in_specs=in_specs, out_specs=out_specs, check_vma=False
    )
```

time: 319 us -> 230 us (0.72)
  waiting for transfers between devices: 169 us -> 71.8 us
  starting transfers between devices: 11.3 us -> 70.4 us
  local copies, waits for them, and re-layouts: 59.9 us -> 16.7 us
  Pallas kernels: 36.8 us -> 63.2 us
  other arithmetic: 23.5 us -> 0.61 us
  between operations: 14.9 us -> 1.84 us
    psum x1 -> x0, waiting for transfers between devices: 131 us -> none  [dp_sum(): return lax.psum(values, 'dp')]
    ppermute x0 -> x58, starting transfers between devices: none -> 63.2 us  [the longest x28 30.1 us: ring_gather(): one, two = (lax.ppermute(one, 'dp', onward), lax.ppermute(two, 'dp', back))]
    ppermute x0 -> x58, waiting for transfers between devices: none -> 46.6 us  [the longest x2 21.5 us: block(): from_dp = lax.ppermute(pack, 'dp', neighbours)]
    pallas_call x9 -> x17, Pallas kernels: 36.8 us -> 63.2 us  [call(): pl.pallas_call(kernel, out_shape=[jax.ShapeDtypeStruct(shape, kind) for s...]
    ppermute x30 -> x15, waiting for transfers between devices: 37.9 us -> 25.2 us  [swap(): return lax.ppermute(values, axis, [(0, 1), (1, 0)])]
    another operation x14 -> x1, local copies, waits for them, and re-layouts: 12.2 us -> 0.09 us  [piece_starts(): return jnp.stack(starts).astype(jnp.int32)]
    another operation x13 -> x0, other arithmetic: 9.95 us -> none  [the longest x11 9.88 us: both(): jnp.stack([pick(*sums[layer]).astype(F32) for layer in range(LAYERS)])]
    concatenate x7 -> x0, local copies, waits for them, and re-layouts: 9.63 us -> none  [the longest x1 5 us: on_device(): jnp.concatenate([tokens, cotangent, norm_gain.reshape(4, half), norm_shif...]
  transfers between devices with their start and end apart: 31 -> 73, of which waited for: 8 -> 35; matrix products, arithmetic and copies ran while one was open for 14% -> 1% of each run, Pallas kernels for 8% -> 11%
where the time goes in v2:
time: 230 us; the launch traced here: 227 us
  waiting for transfers between devices  71.8 us (31%)
  starting transfers between devices  70.4 us (31%)
  Pallas kernels  63.2 us (27%)
  local copies, waits for them, and re-layouts  16.7 us (7%)
    pallas_call x17, Pallas kernels, call(): pl.pallas_call(kernel, out_shape=[jax.ShapeDtypeStruct(shape, kind) for s...  63.2 us
    ppermute x28, starting transfers between devices, ring_gather(): one, two = (lax.ppermute(one, 'dp', onward), lax.ppermute(two, 'dp', back))  30.1 us
    ppermute x28, starting transfers between devices, ring_sum(): one, two = (lax.ppermute(one, 'dp', onward), lax.ppermute(two, 'dp', back))  29.7 us
    ppermute x15, waiting for transfers between devices, swap(): return lax.ppermute(values, axis, [(0, 1), (1, 0)])  25.2 us
    ppermute x2, waiting for transfers between devices, block(): from_dp = lax.ppermute(pack, 'dp', neighbours)  21.5 us
    unnamed x142, local copies, waits for them, and re-layouts  16.4 us
    ppermute x28, waiting for transfers between devices, ring_sum(): one, two = (lax.ppermute(one, 'dp', onward), lax.ppermute(two, 'dp', back))  16.2 us
    ppermute x28, waiting for transfers between devices, ring_gather(): one, two = (lax.ppermute(one, 'dp', onward), lax.ppermute(two, 'dp', back))  8.91 us
  transfers between devices with their start and end apart: 73, of which 35 were waited for; matrix products, arithmetic and copies ran while one was open for 1% of the time, Pallas kernels for 11%

profile of v2, /device:TPU:0, one launch (start us, length us, event | category | flops | bytes accessed | tf_op | source)
XLA Modules:
  0.0 226.8 jit_solution(12518617128792780091)
XLA Ops:
  3.3 5.0 %shard_map.319 = (bf16[432,256]{1,0:T(8,128)(2,1)}, bf16[1536,256]{1,0:T(8,128)(2,1)}, bf16[1536,256]{1,0:T(8,128)(2,1)}, bf16[6144,256]{1,0:T(8,128)(2,1)}) custom-call(s32[1]{0:T(128)} %bitcast.parity_ref, bf16[2,3,256,256]{3,2,1,0:T(8,128)(2,1)} %bitcast.86, bf16[2,256,256]{2,1,0:T(8,128)(2,1)} %refs_1_.15, bf16[2,256,1024]{2,1,0:T(8,128)(2,1)} %refs_0_.7, ...), custom_call_target="tpu_custom_call" | custom-call | flops 3450000 | tf_op jit(solution)/shard_map/pallas_call | solution.py:663
  8.9 2.6 %collective-permute-start.4 = (bf16[1536,256]{1,0:T(8,128)(2,1)}, bf16[1536,256]{1,0:T(8,128)(2,1)S(1)}, u32[]{:S(2)}, u32[]{:S(2)}) collective-permute-start(bf16[1536,256]{1,0:T(8,128)(2,1)} %get-tuple-element.83), channel_id=1, source_target_pairs={{0,1},{1,0},{2,3},{3,2},{4,5},{5,4},{6,7},{7,6},{8,9},{9,8},{10,11... | collective-permute-start | bytes 2359304 | tf_op jit(solution)/shard_map/ppermute | solution.py:41
  11.6 23.0 %collective-permute-done.1.misc_far.refs_1_ = bf16[432,256]{1,0:T(8,128)(2,1)S(1)} collective-permute-done((bf16[432,256]{1,0:T(8,128)(2,1)}, bf16[432,256]{1,0:T(8,128)(2,1)S(1)}, u32[]{:S(2)}, u32[]{:S(2)}) %collective-permute-start.1) | collective-permute-done | bytes 221216 | tf_op jit(solution)/shard_map/ppermute | solution.py:41
  34.6 1.8 collective-permute-start.5
  38.5 15.5 %collective-permute-done.5.refs_3_ = bf16[1536,256]{1,0:T(8,128)(2,1)S(1)} collective-permute-done((bf16[1536,256]{1,0:T(8,128)(2,1)S(1)}, bf16[1536,256]{1,0:T(8,128)(2,1)S(1)}, u32[]{:S(2)}, u32[]{:S(2)}) %collective-permute-start.5) | collective-permute-done | bytes 786464 | tf_op jit(solution)/shard_map/ppermute | solution.py:793
  54.0 3.6 %shard_map.320 = (f32[256,512]{1,0:T(8,128)S(1)}, f32[256,512]{1,0:T(8,128)S(1)}, f32[16,512]{1,0:T(8,128)S(1)}, f32[16,512]{1,0:T(8,128)S(1)}, f32[16,128,128]{...) custom-call(s32[1]{0:T(128)} %bitcast.parity_ref, bf16[432,256]{1,0:T(8,128)(2,1)S(1)} %copy-done.48, ...), custom_call_target="tpu_custom_call" | custom-call | flops 4600000 | tf_op jit(solution)/shard_map/pallas_call | solution.py:663
  59.6 6.1 %shard_map.323 = (f32[256,512]{1,0:T(8,128)S(1)}, bf16[256,512]{1,0:T(8,128)(2,1)S(1)}, bf16[2,256,768]{2,1,0:T(8,128)(2,1)S(1)}, bf16[2,4,512,128]{3,2,1,0:T(8,128)(2,1)S(1)}, bf16[256,512]{1,0:T(8,128)(2,1)S(1)}) custom-call(bf16[2,3,256,256]{3,2,1,0:T(8,128)(2,1)S(1)} %bitcast.87, bf16[2,256,256]{2,1,0:T(8,128)(2,1)S(1)} %copy-done.14, ...), custom_call_target="tpu_custom_call" | custom-call | flops 4600000 | tf_op jit(solution)/shard_map/pallas_call | solution.py:663
  67.5 3.7 %shard_map.324 = (f32[256,512]{1,0:T(8,128)S(1)}, bf16[256,512]{1,0:T(8,128)(2,1)S(1)}, bf16[256,2048]{1,0:T(8,128)(2,1)S(1)}, bf16[256,2048]{1,0:T(8,128)(2,1)S(1)}) custom-call(bf16[2,256,1024]{2,1,0:T(8,128)(2,1)S(1)} %copy-done, bf16[2,1024,256]{2,1,0:T(8,128)(2,1)S(1)} %copy-done.2, bf16[1536,256]{1,0:T(8,128)(2,1)S(1)} %shard_map.322.refs_2_, ...), custom_call_target="tpu_custom_call" | custom-call | flops 4600000 | tf_op jit(solution)/shard_map/pallas_call | solution.py:663
  72.0 6.0 %collective-permute-done.3.refs_0_ = bf16[1536,256]{1,0:T(8,128)(2,1)} collective-permute-done((bf16[1536,256]{1,0:T(8,128)(2,1)}, bf16[1536,256]{1,0:T(8,128)(2,1)}, u32[]{:S(2)}, u32[]{:S(2)}) %collective-permute-start.3) | collective-permute-done | bytes 786464 | tf_op jit(solution)/shard_map/ppermute | solution.py:793
  79.3 2.1 collective-permute-done.10.refs_6_
  84.8 4.9 %shard_map.326 = (f32[256,512]{1,0:T(8,128)S(1)}, bf16[256,512]{1,0:T(8,128)(2,1)S(1)}, bf16[2,256,768]{2,1,0:T(8,128)(2,1)S(1)}, bf16[2,4,512,128]{3,2,1,0:T(8,128)(2,1)S(1)}, bf16[256,512]{1,0:T(8,128)(2,1)S(1)}) custom-call(bf16[2,3,256,256]{3,2,1,0:T(8,128)(2,1)S(1)} %bitcast.88, bf16[2,256,256]{2,1,0:T(8,128)(2,1)S(1)} %copy-done.14, ...), custom_call_target="tpu_custom_call" | custom-call | flops 4600000 | tf_op jit(solution)/shard_map/pallas_call | solution.py:663
  91.5 4.7 %shard_map.327 = (bf16[196,256]{1,0:T(8,128)(2,1)}, bf16[256,512]{1,0:T(8,128)(2,1)S(1)}, bf16[256,2048]{1,0:T(8,128)(2,1)S(1)}, bf16[256,2048]{1,0:T(8,128)(2,1)S(1)}) custom-call(bf16[2,256,1024]{2,1,0:T(8,128)(2,1)S(1)} %copy-done.1, bf16[2,1024,256]{2,1,0:T(8,128)(2,1)S(1)} %copy-done.3, bf16[1536,256]{1,0:T(8,128)(2,1)} %shard_map.321.refs_2_, ...), custom_call_target="tpu_custom_call" | custom-call | flops 4600000 | tf_op jit(solution)/shard_map/pallas_call | solution.py:663
  96.2 5.4 %shard_map.328 = (f32[256,512]{1,0:T(8,128)S(1)}, bf16[2048,256]{1,0:T(8,128)(2,1)S(1)}, bf16[2048,256]{1,0:T(8,128)(2,1)S(1)}, f32[8,256]{1,0:T(8,128)S(1)}, f32[8,256]{1,0:T(8,128)S(1)}) custom-call(bf16[2,256,1024]{2,1,0:T(8,128)(2,1)S(1)} %copy-done.1, bf16[2,1024,256]{2,1,0:T(8,128)(2,1)S(1)} %copy-done.3, bf16[1536,256]{1,0:T(8,128)(2,1)} %shard_map.321.refs_2_, ...), custom_call_target="tpu_custom_call" | custom-call | flops 5750000 | tf_op jit(solution)/shard_map/pallas_call | solution.py:663
  106.1 8.6 %shard_map.329 = (f32[256,512]{1,0:T(8,128)S(1)}, bf16[1024,256]{1,0:T(8,128)(2,1)S(1)}, bf16[1024,256]{1,0:T(8,128)(2,1)S(1)}, f32[8,256]{1,0:T(8,128)S(1)}, f3...) custom-call(bf16[2,3,256,256]{3,2,1,0:T(8,128)(2,1)S(1)} %bitcast.89, bf16[2,256,256]{2,1,0:T(8,128)(2,1)S(1)} %copy-done.14, ...), custom_call_target="tpu_custom_call" | custom-call | flops 6900000 | tf_op jit(solution)/shard_map/pallas_call | solution.py:663
  115.6 5.4 %shard_map.330 = (f32[256,512]{1,0:T(8,128)S(1)}, bf16[2048,256]{1,0:T(8,128)(2,1)S(1)}, bf16[2048,256]{1,0:T(8,128)(2,1)S(1)}, f32[8,256]{1,0:T(8,128)S(1)}, f32[8,256]{1,0:T(8,128)S(1)}) custom-call(bf16[2,256,1024]{2,1,0:T(8,128)(2,1)S(1)} %copy-done.1, bf16[2,1024,256]{2,1,0:T(8,128)(2,1)S(1)} %copy-done.3, bf16[1536,256]{1,0:T(8,128)(2,1)S(1)} %copy-done.5, ...), custom_call_target="tpu_custom_call" | custom-call | flops 5750000 | tf_op jit(solution)/shard_map/pallas_call | solution.py:663
  121.3 10.4 %shard_map.331 = (bf16[196,256]{1,0:T(8,128)(2,1)}, bf16[1024,256]{1,0:T(8,128)(2,1)S(1)}, bf16[1024,256]{1,0:T(8,128)(2,1)S(1)}, f32[8,256]{1,0:T(8,128)S(1)}, ...) custom-call(bf16[2,3,256,256]{3,2,1,0:T(8,128)(2,1)S(1)} %bitcast.90, bf16[2,256,256]{2,1,0:T(8,128)(2,1)S(1)} %copy-done.14, ...), custom_call_target="tpu_custom_call" | custom-call | flops 6900000 | tf_op jit(solution)/shard_map/pallas_call | solution.py:663
  156.5 2.0 collective-permute-start.24
  159.4 2.5 %collective-permute-start.55 = (bf16[200,256]{1,0:T(8,128)(2,1)S(1)}, bf16[200,256]{1,0:T(8,128)(2,1)S(1)}, u32[]{:S(2)}, u32[]{:S(2)}) collective-permute-start(bf16[200,256]{1,0:T(8,128)(2,1)S(1)} %get-tuple-element.155), channel_id=1, source_target_pairs={{8,0},{16,8},{24,16},{28,24},{20,28},{12,20},{4,12},{0,4},{9,1},{1... | collective-permute-start | bytes 307208 | tf_op jit(solution)/shard_map/ppermute | solution.py:733
  162.0 1.9 collective-permute-done.17
  180.0 1.9 collective-permute-start.51
  191.0 2.1 collective-permute-start.61
  193.4 1.9 collective-permute-start.32
  195.8 2.1 collective-permute-start.63
  198.4 2.2 collective-permute-start.34
  201.4 1.9 collective-permute-start.65
  204.0 2.1 collective-permute-start.36
  206.3 2.0 collective-permute-start.67
  209.0 1.8 collective-permute-start.38
  211.0 1.9 collective-permute-start.69
  215.7 1.9 collective-permute-start.71
  220.4 2.3 %collective-permute-done.72.refs_32_ = bf16[200,256]{1,0:T(8,128)(2,1)S(1)} collective-permute-done((bf16[200,256]{1,0:T(8,128)(2,1)S(1)}, bf16[200,256]{1,0:T(8,128)(2,1)S(1)}, u32[]{:S(2)}, u32[]{:S(2)}) %collective-permute-start.72) | collective-permute-done | bytes 102432 | tf_op jit(solution)/shard_map/ppermute | solution.py:747
  222.7 3.9 %shard_map.334 = (f32[2,3,256,256]{3,2,1,0:T(8,128)}, f32[2,2,256]{2,1,0:T(2,128)}, f32[2,256,256]{2,1,0:T(8,128)}, f32[2,256]{1,0:T(2,128)}, f32[2,256,1024]{2,...) custom-call(s32[16]{0:T(128)S(1)} %stack.67.refs_0_, ...), custom_call_target="tpu_custom_call" | custom-call | flops 4600000 | tf_op jit(solution)/shard_map/pallas_call | solution.py:663
  (303 shorter events, 81.9 us)
Async XLA Ops:
  8.4 51.1 %collective-permute-start.6 = (bf16[6144,256]{1,0:T(8,128)(2,1)}, bf16[6144,256]{1,0:T(8,128)(2,1)S(1)}, u32[]{:S(2)}, u32[]{:S(2)}) collective-permute-start(bf16[6144,256]{1,0:T(8,128)(2,1)} %get-tuple-element.84), channel_id=1, source_target_pairs={{0,2},{2,0},{1,3},{3,1},{4,6},{6,4},{5,7},{7,5},{8,10},{10,8},{9,1... | collective-permute-start | bytes 9437192 | tf_op jit(solution)/shard_map/ppermute | solution.py:41
  8.9 25.7 %collective-permute-start.4 = (bf16[1536,256]{1,0:T(8,128)(2,1)}, bf16[1536,256]{1,0:T(8,128)(2,1)S(1)}, u32[]{:S(2)}, u32[]{:S(2)}) collective-permute-start(bf16[1536,256]{1,0:T(8,128)(2,1)} %get-tuple-element.83), channel_id=1, source_target_pairs={{0,1},{1,0},{2,3},{3,2},{4,5},{5,4},{6,7},{7,6},{8,9},{9,8},{10,11... | collective-permute-start | bytes 2359304 | tf_op jit(solution)/shard_map/ppermute | solution.py:41
  11.5 23.1 %collective-permute-start.1 = (bf16[432,256]{1,0:T(8,128)(2,1)}, bf16[432,256]{1,0:T(8,128)(2,1)S(1)}, u32[]{:S(2)}, u32[]{:S(2)}) collective-permute-start(bf16[432,256]{1,0:T(8,128)(2,1)} %get-tuple-element.81.misc_ref), channel_id=1, source_target_pairs={{0,1},{1,0},{2,3},{3,2},{4,5},{5,4},{6,7},{7,6},{8,9},{9,8},{10,11... | collective-permute-start | bytes 663560 | tf_op jit(solution)/shard_map/ppermute | solution.py:41
  34.6 19.4 %collective-permute-start.5 = (bf16[1536,256]{1,0:T(8,128)(2,1)S(1)}, bf16[1536,256]{1,0:T(8,128)(2,1)S(1)}, u32[]{:S(2)}, u32[]{:S(2)}) collective-permute-start(bf16[1536,256]{1,0:T(8,128)(2,1)S(1)} %shard_map.322.refs_2_), channel_id=1, source_target_pairs={{0,4},{4,0},{8,12},{12,8},{16,20},{20,16},{24,28},{28,24},{1,5},{5... | collective-permute-start | bytes 2359304 | tf_op jit(solution)/shard_map/ppermute | solution.py:793
  36.4 21.2 %collective-permute-start = (bf16[1536,256]{1,0:T(8,128)(2,1)S(1)}, bf16[1536,256]{1,0:T(8,128)(2,1)}, u32[]{:S(2)}, u32[]{:S(2)}) collective-permute-start(bf16[1536,256]{1,0:T(8,128)(2,1)S(1)} %copy-done.70), channel_id=1, source_target_pairs={{0,1},{1,0},{2,3},{3,2},{4,5},{5,4},{6,7},{7,6},{8,9},{9,8},{10,11... | collective-permute-start | bytes 2359304 | tf_op jit(solution)/shard_map/ppermute | solution.py:41
  37.9 16.1 %collective-permute-start.2 = (bf16[32,256]{1,0:T(8,128)(2,1)S(1)}, bf16[32,256]{1,0:T(8,128)(2,1)S(1)}, u32[]{:S(2)}, u32[]{:S(2)}) collective-permute-start(bf16[32,256]{1,0:T(8,128)(2,1)S(1)} %copy-done.50), channel_id=1, source_target_pairs={{0,2},{2,0},{1,3},{3,1},{4,6},{6,4},{5,7},{7,5},{8,10},{10,8},{9,1... | collective-permute-start | bytes 49160 | tf_op jit(solution)/shard_map/ppermute | solution.py:41
  37.9 21.5 %collective-permute-start.7 = (bf16[1536,256]{1,0:T(8,128)(2,1)S(1)}, bf16[1536,256]{1,0:T(8,128)(2,1)S(1)}, u32[]{:S(2)}, u32[]{:S(2)}) collective-permute-start(bf16[1536,256]{1,0:T(8,128)(2,1)S(1)} %shard_map.322.refs_2_), channel_id=1, source_target_pairs={{0,2},{2,0},{1,3},{3,1},{4,6},{6,4},{5,7},{7,5},{8,10},{10,8},{9,1... | collective-permute-start | bytes 2359304 | tf_op jit(solution)/shard_map/ppermute | solution.py:41
  57.7 20.3 %collective-permute-start.3 = (bf16[1536,256]{1,0:T(8,128)(2,1)}, bf16[1536,256]{1,0:T(8,128)(2,1)}, u32[]{:S(2)}, u32[]{:S(2)}) collective-permute-start(bf16[1536,256]{1,0:T(8,128)(2,1)} %shard_map.321.refs_2_), channel_id=1, source_target_pairs={{0,4},{4,0},{8,12},{12,8},{16,20},{20,16},{24,28},{28,24},{1,5},{5... | collective-permute-start | bytes 2359304 | tf_op jit(solution)/shard_map/ppermute | solution.py:793
  59.3 20.1 %collective-permute-start.9 = (bf16[1536,256]{1,0:T(8,128)(2,1)}, bf16[1536,256]{1,0:T(8,128)(2,1)}, u32[]{:S(2)}, u32[]{:S(2)}) collective-permute-start(bf16[1536,256]{1,0:T(8,128)(2,1)} %shard_map.321.refs_2_), channel_id=1, source_target_pairs={{0,2},{2,0},{1,3},{3,1},{4,6},{6,4},{5,7},{7,5},{8,10},{10,8},{9,1... | collective-permute-start | bytes 2359304 | tf_op jit(solution)/shard_map/ppermute | solution.py:41
  121.0 14.6 %collective-permute-start.11 = (bf16[2048,256]{1,0:T(8,128)(2,1)S(1)}, bf16[2048,256]{1,0:T(8,128)(2,1)S(1)}, u32[]{:S(2)}, u32[]{:S(2)}) collective-permute-start(bf16[2048,256]{1,0:T(8,128)(2,1)S(1)} %get-tuple-element.113), channel_id=1, source_target_pairs={{0,2},{2,0},{1,3},{3,1},{4,6},{6,4},{5,7},{7,5},{8,10},{10,8},{9,1... | collective-permute-start | bytes 3145736 | tf_op jit(solution)/shard_map/ppermute | solution.py:41
  132.1 6.5 %collective-permute-start.42 = (bf16[2048,256]{1,0:T(8,128)(2,1)S(1)}, bf16[2048,256]{1,0:T(8,128)(2,1)S(1)}, u32[]{:S(2)}, u32[]{:S(2)}) collective-permute-start(bf16[2048,256]{1,0:T(8,128)(2,1)S(1)} %copy-done.61), channel_id=1, source_target_pairs={{0,2},{2,0},{1,3},{3,1},{4,6},{6,4},{5,7},{7,5},{8,10},{10,8},{9,1... | collective-permute-start | bytes 3145736 | tf_op jit(solution)/shard_map/ppermute | solution.py:41
  144.4 5.7 %collective-permute-start.15 = (bf16[200,256]{1,0:T(8,128)(2,1)S(1)}, bf16[200,256]{1,0:T(8,128)(2,1)S(1)}, u32[]{:S(2)}, u32[]{:S(2)}) collective-permute-start(bf16[200,256]{1,0:T(8,128)(2,1)S(1)} %get-tuple-element.174), channel_id=1, source_target_pairs={{0,8},{8,16},{16,24},{24,28},{28,20},{20,12},{12,4},{4,0},{1,9},{9... | collective-permute-start | bytes 307208 | tf_op jit(solution)/shard_map/ppermute | solution.py:733
  145.9 6.3 %collective-permute-start.53 = (bf16[200,256]{1,0:T(8,128)(2,1)S(1)}, bf16[200,256]{1,0:T(8,128)(2,1)S(1)}, u32[]{:S(2)}, u32[]{:S(2)}) collective-permute-start(bf16[200,256]{1,0:T(8,128)(2,1)S(1)} %get-tuple-element.159), channel_id=1, source_target_pairs={{8,0},{16,8},{24,16},{28,24},{20,28},{12,20},{4,12},{0,4},{9,1},{1... | collective-permute-start | bytes 307208 | tf_op jit(solution)/shard_map/ppermute | solution.py:733
  159.4 6.6 %collective-permute-start.55 = (bf16[200,256]{1,0:T(8,128)(2,1)S(1)}, bf16[200,256]{1,0:T(8,128)(2,1)S(1)}, u32[]{:S(2)}, u32[]{:S(2)}) collective-permute-start(bf16[200,256]{1,0:T(8,128)(2,1)S(1)} %get-tuple-element.155), channel_id=1, source_target_pairs={{8,0},{16,8},{24,16},{28,24},{20,28},{12,20},{4,12},{0,4},{9,1},{1... | collective-permute-start | bytes 307208 | tf_op jit(solution)/shard_map/ppermute | solution.py:733
  166.5 5.6 %collective-permute-start.56 = (bf16[200,256]{1,0:T(8,128)(2,1)S(1)}, bf16[200,256]{1,0:T(8,128)(2,1)S(1)}, u32[]{:S(2)}, u32[]{:S(2)}) collective-permute-start(bf16[200,256]{1,0:T(8,128)(2,1)S(1)} %get-tuple-element.153), channel_id=1, source_target_pairs={{8,0},{16,8},{24,16},{28,24},{20,28},{12,20},{4,12},{0,4},{9,1},{1... | collective-permute-start | bytes 307208 | tf_op jit(solution)/shard_map/ppermute | solution.py:733
  168.0 5.6 %collective-permute-start.49 = (bf16[200,256]{1,0:T(8,128)(2,1)S(1)}, bf16[200,256]{1,0:T(8,128)(2,1)S(1)}, u32[]{:S(2)}, u32[]{:S(2)}) collective-permute-start(bf16[200,256]{1,0:T(8,128)(2,1)S(1)} %get-tuple-element.154), channel_id=1, source_target_pairs={{0,8},{8,16},{16,24},{24,28},{28,20},{20,12},{12,4},{4,0},{1,9},{9... | collective-permute-start | bytes 307208 | tf_op jit(solution)/shard_map/ppermute | solution.py:733
  169.3 6.4 %collective-permute-start.26 = (bf16[200,256]{1,0:T(8,128)(2,1)S(1)}, bf16[200,256]{1,0:T(8,128)(2,1)S(1)}, u32[]{:S(2)}, u32[]{:S(2)}) collective-permute-start(bf16[200,256]{1,0:T(8,128)(2,1)S(1)} %get-tuple-element.165), channel_id=1, source_target_pairs={{8,0},{16,8},{24,16},{28,24},{20,28},{12,20},{4,12},{0,4},{9,1},{1... | collective-permute-start | bytes 307208 | tf_op jit(solution)/shard_map/ppermute | solution.py:733
  173.6 5.5 %collective-permute-start.57 = (bf16[200,256]{1,0:T(8,128)(2,1)S(1)}, bf16[200,256]{1,0:T(8,128)(2,1)S(1)}, u32[]{:S(2)}, u32[]{:S(2)}) collective-permute-start(bf16[200,256]{1,0:T(8,128)(2,1)S(1)} %get-tuple-element.151), channel_id=1, source_target_pairs={{8,0},{16,8},{24,16},{28,24},{20,28},{12,20},{4,12},{0,4},{9,1},{1... | collective-permute-start | bytes 307208 | tf_op jit(solution)/shard_map/ppermute | solution.py:733
  174.1 5.8 %collective-permute-start.50 = (bf16[200,256]{1,0:T(8,128)(2,1)S(1)}, bf16[200,256]{1,0:T(8,128)(2,1)S(1)}, u32[]{:S(2)}, u32[]{:S(2)}) collective-permute-start(bf16[200,256]{1,0:T(8,128)(2,1)S(1)} %get-tuple-element.152), channel_id=1, source_target_pairs={{0,8},{8,16},{16,24},{24,28},{28,20},{20,12},{12,4},{4,0},{1,9},{9... | collective-permute-start | bytes 307208 | tf_op jit(solution)/shard_map/ppermute | solution.py:733
  175.7 6.2 %collective-permute-start.27 = (bf16[200,256]{1,0:T(8,128)(2,1)S(1)}, bf16[200,256]{1,0:T(8,128)(2,1)S(1)}, u32[]{:S(2)}, u32[]{:S(2)}) collective-permute-start(bf16[200,256]{1,0:T(8,128)(2,1)S(1)} %get-tuple-element.163), channel_id=1, source_target_pairs={{8,0},{16,8},{24,16},{28,24},{20,28},{12,20},{4,12},{0,4},{9,1},{1... | collective-permute-start | bytes 307208 | tf_op jit(solution)/shard_map/ppermute | solution.py:733
  176.2 5.8 %collective-permute-start.20 = (bf16[200,256]{1,0:T(8,128)(2,1)S(1)}, bf16[200,256]{1,0:T(8,128)(2,1)S(1)}, u32[]{:S(2)}, u32[]{:S(2)}) collective-permute-start(bf16[200,256]{1,0:T(8,128)(2,1)S(1)} %get-tuple-element.164), channel_id=1, source_target_pairs={{0,8},{8,16},{16,24},{24,28},{28,20},{20,12},{12,4},{4,0},{1,9},{9... | collective-permute-start | bytes 307208 | tf_op jit(solution)/shard_map/ppermute | solution.py:733
  179.9 5.7 %collective-permute-start.58 = (bf16[200,256]{1,0:T(8,128)(2,1)S(1)}, bf16[200,256]{1,0:T(8,128)(2,1)S(1)}, u32[]{:S(2)}, u32[]{:S(2)}) collective-permute-start(bf16[200,256]{1,0:T(8,128)(2,1)S(1)} %get-tuple-element.149), channel_id=1, source_target_pairs={{8,0},{16,8},{24,16},{28,24},{20,28},{12,20},{4,12},{0,4},{9,1},{1... | collective-permute-start | bytes 307208 | tf_op jit(solution)/shard_map/ppermute | solution.py:733
  180.0 5.5 %collective-permute-start.51 = (bf16[200,256]{1,0:T(8,128)(2,1)S(1)}, bf16[200,256]{1,0:T(8,128)(2,1)S(1)}, u32[]{:S(2)}, u32[]{:S(2)}) collective-permute-start(bf16[200,256]{1,0:T(8,128)(2,1)S(1)} %get-tuple-element.150), channel_id=1, source_target_pairs={{0,8},{8,16},{16,24},{24,28},{28,20},{20,12},{12,4},{4,0},{1,9},{9... | collective-permute-start | bytes 307208 | tf_op jit(solution)/shard_map/ppermute | solution.py:733
  182.0 5.7 %collective-permute-start.28 = (bf16[200,256]{1,0:T(8,128)(2,1)S(1)}, bf16[200,256]{1,0:T(8,128)(2,1)S(1)}, u32[]{:S(2)}, u32[]{:S(2)}) collective-permute-start(bf16[200,256]{1,0:T(8,128)(2,1)S(1)} %get-tuple-element.162.refs_1_), channel_id=1, source_target_pairs={{0,8},{8,16},{16,24},{24,28},{28,20},{20,12},{12,4},{4,0},{1,9},{9... | collective-permute-start | bytes 307208 | tf_op jit(solution)/shard_map/ppermute | solution.py:747
  183.6 5.8 %collective-permute-start.29 = (bf16[200,256]{1,0:T(8,128)(2,1)S(1)}, bf16[200,256]{1,0:T(8,128)(2,1)S(1)}, u32[]{:S(2)}, u32[]{:S(2)}) collective-permute-start(bf16[200,256]{1,0:T(8,128)(2,1)S(1)} %get-tuple-element.161.refs_2_), channel_id=1, source_target_pairs={{8,0},{16,8},{24,16},{28,24},{20,28},{12,20},{4,12},{0,4},{9,1},{1... | collective-permute-start | bytes 307208 | tf_op jit(solution)/shard_map/ppermute | solution.py:747
  187.4 5.8 %collective-permute-start.60 = (bf16[200,256]{1,0:T(8,128)(2,1)S(1)}, bf16[200,256]{1,0:T(8,128)(2,1)S(1)}, u32[]{:S(2)}, u32[]{:S(2)}) collective-permute-start(bf16[200,256]{1,0:T(8,128)(2,1)S(1)} %get-tuple-element.147.refs_18_), channel_id=1, source_target_pairs={{8,0},{16,8},{24,16},{28,24},{20,28},{12,20},{4,12},{0,4},{9,1},{1... | collective-permute-start | bytes 307208 | tf_op jit(solution)/shard_map/ppermute | solution.py:747
  187.7 5.7 %collective-permute-start.30 = (bf16[200,256]{1,0:T(8,128)(2,1)S(1)}, bf16[200,256]{1,0:T(8,128)(2,1)S(1)}, u32[]{:S(2)}, u32[]{:S(2)}) collective-permute-start(bf16[200,256]{1,0:T(8,128)(2,1)S(1)} %collective-permute-done.28.refs_3_), channel_id=1, source_target_pairs={{0,8},{8,16},{16,24},{24,28},{28,20},{20,12},{12,4},{4,0},{1,9},{9... | collective-permute-start | bytes 307208 | tf_op jit(solution)/shard_map/ppermute | solution.py:747
  189.5 5.8 %collective-permute-start.31 = (bf16[200,256]{1,0:T(8,128)(2,1)S(1)}, bf16[200,256]{1,0:T(8,128)(2,1)S(1)}, u32[]{:S(2)}, u32[]{:S(2)}) collective-permute-start(bf16[200,256]{1,0:T(8,128)(2,1)S(1)} %collective-permute-done.29.refs_4_), channel_id=1, source_target_pairs={{8,0},{16,8},{24,16},{28,24},{20,28},{12,20},{4,12},{0,4},{9,1},{1... | collective-permute-start | bytes 307208 | tf_op jit(solution)/shard_map/ppermute | solution.py:747
  195.8 5.6 %collective-permute-start.63 = (bf16[200,256]{1,0:T(8,128)(2,1)S(1)}, bf16[200,256]{1,0:T(8,128)(2,1)S(1)}, u32[]{:S(2)}, u32[]{:S(2)}) collective-permute-start(bf16[200,256]{1,0:T(8,128)(2,1)S(1)} %collective-permute-done.61.refs_21_), channel_id=1, source_target_pairs={{0,8},{8,16},{16,24},{24,28},{28,20},{20,12},{12,4},{4,0},{1,9},{9... | collective-permute-start | bytes 307208 | tf_op jit(solution)/shard_map/ppermute | solution.py:747
  197.9 6.0 %collective-permute-start.64 = (bf16[200,256]{1,0:T(8,128)(2,1)S(1)}, bf16[200,256]{1,0:T(8,128)(2,1)S(1)}, u32[]{:S(2)}, u32[]{:S(2)}) collective-permute-start(bf16[200,256]{1,0:T(8,128)(2,1)S(1)} %collective-permute-done.62.refs_22_), channel_id=1, source_target_pairs={{8,0},{16,8},{24,16},{28,24},{20,28},{12,20},{4,12},{0,4},{9,1},{1... | collective-permute-start | bytes 307208 | tf_op jit(solution)/shard_map/ppermute | solution.py:747
  198.4 5.6 %collective-permute-start.34 = (bf16[200,256]{1,0:T(8,128)(2,1)S(1)}, bf16[200,256]{1,0:T(8,128)(2,1)S(1)}, u32[]{:S(2)}, u32[]{:S(2)}) collective-permute-start(bf16[200,256]{1,0:T(8,128)(2,1)S(1)} %collective-permute-done.32.refs_7_), channel_id=1, source_target_pairs={{0,8},{8,16},{16,24},{24,28},{28,20},{20,12},{12,4},{4,0},{1,9},{9... | collective-permute-start | bytes 307208 | tf_op jit(solution)/shard_map/ppermute | solution.py:747
  200.6 5.5 %collective-permute-start.35 = (bf16[200,256]{1,0:T(8,128)(2,1)S(1)}, bf16[200,256]{1,0:T(8,128)(2,1)S(1)}, u32[]{:S(2)}, u32[]{:S(2)}) collective-permute-start(bf16[200,256]{1,0:T(8,128)(2,1)S(1)} %collective-permute-done.33.refs_8_), channel_id=1, source_target_pairs={{8,0},{16,8},{24,16},{28,24},{20,28},{12,20},{4,12},{0,4},{9,1},{1... | collective-permute-start | bytes 307208 | tf_op jit(solution)/shard_map/ppermute | solution.py:747
  (112 other events, 843.7 us)

commit v3 on v2

--- a/solution.py
+++ b/solution.py
@@ -326,7 +326,7 @@
 
 def pack_kernel(
     parity_ref, qkv, out, up, down, tokens, cot, gain, shift, out_bias, down_bias, _,
-    misc_out, pack_zero, pack_one, whole, *rest,
+    pack_zero, pack_one, whole, *rest,
 ):
     rooms, results, (in_sems, out_sems) = rest[:8], rest[8:11], rest[11:]
     half, quarter = D // 2, D // 4
@@ -351,7 +351,7 @@
     misc[COT_AT : COT_AT + IMAGE, :] = cot[...]
     rows = [gain[0], gain[1], shift[0], shift[1], out_bias[...], down_bias[...]]
     misc[SMALL_AT : SMALL_AT + 12, :] = jnp.concatenate([row.astype(F32) for row in rows], 0).astype(BF)
-    send(misc, misc_out)
+    send(misc, pack_zero.at[0:MISC_ROWS, :])
     for layer in range(LAYERS):
         pack = results[1 + layer]
         at = layer * TAIL_AT
@@ -370,7 +370,7 @@
         chosen = jnp.where(even, down_l[:, 0:quarter], down_l[:, quarter:half])
         pack[2 * D :, 0:quarter] = chosen[0 : FF // 4]
         pack[2 * D :, quarter:half] = chosen[FF // 4 :]
-        send(pack, (pack_zero, pack_one)[layer])
+        send(pack, pack_zero.at[MISC_ROWS:, :] if layer == 0 else pack_one)
         send(down_l, whole.at[at + DOWN_AT : at + UP_AT, :])
         for piece in range(4):
             lines = slice(at + UP_AT + piece * half, at + UP_AT + (piece + 1) * half)
@@ -711,6 +711,73 @@
     return call(run, outs, spaces, operands, micros, [ANY] * len(operands))
 
 
+def turn_call(layer, forward, blocks, wholes, named, outs):
+    half = D // 2
+    weights = [*wholes[2:], *blocks, *wholes[:2], *blocks]
+    names, args = list(named), list(named.values())
+    inner = {"normed_two": ((ROWS, D), BF), "slope": ((ROWS, FF), BF), "hidden": ((ROWS, FF), BF)}
+    inner = inner if forward else {}
+    spaces = [
+        ((ROWS, D), F32), ((200, half), F32), ((ROWS, D), F32), ((2, ROWS, 3 * half), BF), *inner.values(),
+    ]
+
+    def run(*refs):
+        refs = list(refs)
+
+        def take(number):
+            taken = refs[:number]
+            del refs[:number]
+            return taken
+
+        weight_refs, arg_refs, out_refs = take(14), take(len(args)), take(len(outs))
+        ffn_rooms, attn_rooms, arg_rooms = take(4), take(4), take(len(args))
+        scratch, flat, grad_mid, grad_qkv = take(4)
+        made = dict(zip(inner, take(len(inner))))
+        (sems,) = take(1)
+        ups, downs = ffn_weights(layer, weight_refs[:7], ffn_rooms, sems, 0)
+        qkvs, mixes = attn_weights(layer, weight_refs[7:], attn_rooms, sems, FFN_COPIES)
+        got = {
+            name: whole_fetch(ref, room, sems, FFN_COPIES + ATTN_COPIES + at)
+            for at, (name, ref, room) in enumerate(zip(names, arg_refs, arg_rooms))
+        }
+        early = ("middle", "small") if forward else ("grad", "slope", "hidden")
+        late = [got[name] for name in names if name not in early]
+        early = [got[name] for name in early]
+        if forward:
+            pending = [*early, *ups, *downs, *late, *mixes, *qkvs]
+        else:
+            pending = [early[0], downs[0], *early[1:], got["normed_two"], ups[0], downs[1], ups[1]]
+            pending += [item for item in late if item is not got["normed_two"]] + [*mixes, *qkvs]
+        for item in pending:
+            item.start()
+        got.update(made)
+        outputs = list(out_refs)
+        if forward:
+            ffn_fwd_kernel(
+                layer, (ups, downs), got["middle"], got["small"], outputs.pop(0), got["normed_two"], got["slope"],
+                got["hidden"], scratch, flat,
+            )
+        ffn_bwd_kernel(
+            layer, (ups, downs), got["grad"], got["slope"], got["hidden"], got["normed_two"], got["small"],
+            got["middle"], grad_mid, *outputs[:4],
+        )
+        attn_bwd_kernel(
+            layer, (qkvs, mixes), grad_mid, got["att"], got["qkv"], got["probs"], got["picks"], got["picks_t"],
+            got["normed_one"], got["small"], got["x"], *outputs[4:], grad_qkv, scratch, flat,
+        )
+        for item in pending:
+            item.ready()
+
+    scratch = (
+        [pltpu.VMEM(shape, kind) for shape, kind in FFN_ROOMS + ATTN_ROOMS]
+        + [pltpu.VMEM(a.shape, a.dtype) for a in args]
+        + [pltpu.VMEM(shape, kind) for shape, kind in spaces]
+        + [pltpu.SemaphoreType.DMA((FFN_COPIES + ATTN_COPIES + len(args),))]
+    )
+    operands = [*weights, *args]
+    return call(run, outs, scratch, operands, 12, [ANY] * len(operands))
+
+
 FORWARD = (attn_fwd_kernel, ffn_fwd_kernel)
 
 
@@ -773,29 +840,29 @@
     row_far = swap(misc_row, "row")
     sources = [*wholes, tokens, cotangent, norm_gain, norm_shift, out_bias, down_bias]
     pack_outs = [((MISC_ROWS, half), BF), ((3 * D, half), BF), ((3 * D, half), BF)]
-    misc, *packs, whole = call(
+    packs = [None, None]
+    packs[0], packs[1], whole = call(
         pack_kernel,
-        [*pack_outs, ((LAYERS * TAIL_AT, half), BF)],
+        [((MISC_ROWS + 3 * D, half), BF), ((3 * D, half), BF), ((LAYERS * TAIL_AT, half), BF)],
         [pltpu.VMEM(value.shape[1:], value.dtype) for value in wholes] * LAYERS
         + [pltpu.VMEM(shape, kind) for shape, kind in pack_outs]
         + [pltpu.SemaphoreType.DMA((8,)), pltpu.SemaphoreType.DMA((21,))],
         [parity_ref, *sources, misc_row],
         3,
         [SMEM] + [ANY] * 4 + [VMEM] * 6 + [ANY],
-        [ANY] * 4,
+        [ANY] * 3,
         limit=60,
     )
-    whole_row, misc_far = swap(whole, "row"), swap(misc, "col")
+    whole_row = swap(whole, "row")
     from_col = [swap(pack, "col") for pack in packs]
-    from_col[0] = after(from_col[0], misc_far)
+    misc, misc_far = packs[0][:MISC_ROWS], from_col[0][:MISC_ROWS]
+    from_col[0] = from_col[0][MISC_ROWS:]
 
     def block(pack, token):
         from_dp = lax.ppermute(pack, "dp", neighbours)
-        if token is not None:
-            from_dp = after(from_dp, token)
+        from_dp = after(from_dp, token)
         return [pack, from_dp, whole_row, swap(pack, "row"), swap(from_dp, "row")]
 
-    blocks = [block(from_col[0], None)]
     picks = np.stack([position_one_hot(layer) for layer in range(LAYERS)])
     picks_t = [jnp.asarray(pick.T, BF) for pick in picks]
     picks_all = jnp.asarray(picks, BF)
@@ -814,7 +881,7 @@
         [SMEM] + [VMEM] * 6,
     )
     smalls, bias = rest[:2], rest[2:4]
-    from_col[1] = after(from_col[1], x)
+    blocks = [block(from_col[0], x)]
 
     image = ((IMAGE, half), BF)
     saved = []
@@ -831,11 +898,15 @@
             [x, smalls[layer], bias[layer], masks[layer]],
             4,
             True,
+            [from_col[1]] if layer == 0 else [],
         )
+        if layer == LAYERS - 1:
+            saved.append((x, middle, normed_one, qkv, probs, att, None, None, None))
+            break
         result, normed_two, pre, hidden = layer_call(
             ffn_fwd_kernel,
             layer,
-            [wide if layer < LAYERS - 1 else image, ((ROWS, D), BF), ((ROWS, FF), BF), ((ROWS, FF), BF)],
+            [wide, ((ROWS, D), BF), ((ROWS, FF), BF), ((ROWS, FF), BF)],
             [pltpu.VMEM((ROWS, D), F32), pltpu.VMEM((200, half), F32)],
             [*wholes[2:], *blocks[layer]],
             [middle, smalls[layer]],
@@ -846,7 +917,6 @@
             blocks.append(block(from_col[1], result))
         saved.append((x, middle, normed_one, qkv, probs, att, normed_two, pre, hidden))
         x = result
-    output = x
 
     heads = HEADS // 2
     one_hot = (index_map[:, :, None] == jnp.arange(256, dtype=jnp.int32)).astype(F32).reshape(SPAN * SPAN, 256)
@@ -856,30 +926,30 @@
     for layer in reversed(range(LAYERS)):
         x_in, middle, normed_one, qkv, probs, att, normed_two, pre, hidden = saved[layer]
         small_shape = ((8, half), F32)
-        grad_mid, ffn_keep, ffn_send, small_keep, small_send = layer_call(
-            ffn_bwd_kernel,
+        named = {
+            "middle": middle, "small": smalls[layer], "grad": grad, "slope": pre, "hidden": hidden,
+            "normed_two": normed_two, "att": att, "qkv": qkv, "probs": probs, "picks": picks[layer],
+            "picks_t": picks_t[layer], "normed_one": normed_one, "x": x_in,
+        }
+        named = {name: value for name, value in named.items() if value is not None}
+        last = layer == LAYERS - 1
+        results = turn_call(
             layer,
-            [wide, ((FF, half), BF), ((FF, half), BF), small_shape, small_shape],
-            [],
-            [*wholes[2:], *blocks[layer]],
-            [grad, pre, hidden, normed_two, smalls[layer], middle],
-            5,
-            False,
-        )
-        ffn_got = swap(ffn_send, "row")
-        grad, keep, send, att_keep, att_send, counts = layer_call(
-            attn_bwd_kernel,
-            layer,
-            [
+            last,
+            blocks[layer],
+            wholes,
+            named,
+            [image] * last
+            + [
+                ((FF, half), BF), ((FF, half), BF), small_shape, small_shape,
                 wide if layer > 0 else image, ((2 * D, half), BF), ((2 * D, half), BF), small_shape, small_shape,
                 ((HEADS, 56, PAD), F32),
             ],
-            [pltpu.VMEM((2, ROWS, 3 * half), BF), pltpu.VMEM((ROWS, D), F32), pltpu.VMEM((200, half), F32)],
-            [*wholes[:2], *blocks[layer]],
-            [grad_mid, att, qkv, probs, picks[layer], picks_t[layer], normed_one, smalls[layer], x_in],
-            6,
-            True,
         )
+        if last:
+            output, *results = results
+        ffn_keep, ffn_send, small_keep, small_send, grad, keep, send, att_keep, att_send, counts = results
+        ffn_got = swap(ffn_send, "row")
         got = swap(send, "row")
         table = jnp.dot(counts[:, :SPAN, :SPAN].reshape(HEADS, SPAN * SPAN), one_hot, precision=HIGH)
         tail_keep = jnp.concatenate([small_keep, att_keep, table[:heads]], 0)

time: 230 us -> 212 us (0.922)
  Pallas kernels: 63.2 us -> 58.1 us
  local copies, waits for them, and re-layouts: 16.7 us -> 11.7 us
  starting transfers between devices: 70.4 us -> 66.2 us
  waiting for transfers between devices: 71.8 us -> 67.8 us
    ppermute x2, waiting for transfers between devices: 21.5 us -> 15 us  [block(): from_dp = lax.ppermute(pack, 'dp', neighbours)]
    unnamed x142 -> x108, local copies, waits for them, and re-layouts: 16.4 us -> 10.4 us
    pallas_call x17 -> x13, Pallas kernels: 63.2 us -> 58.1 us  [call(): pl.pallas_call(kernel, out_shape=[jax.ShapeDtypeStruct(shape, kind) for s...]
    ppermute x28, starting transfers between devices: 30.1 us -> 27 us  [ring_gather(): one, two = (lax.ppermute(one, 'dp', onward), lax.ppermute(two, 'dp', back))]
    ppermute x15 -> x14, waiting for transfers between devices: 25.2 us -> 27 us  [swap(): return lax.ppermute(values, axis, [(0, 1), (1, 0)])]
    ppermute x15 -> x14, starting transfers between devices: 7.18 us -> 7.05 us  [swap(): return lax.ppermute(values, axis, [(0, 1), (1, 0)])]
  transfers between devices with their start and end apart: 73 -> 72, of which waited for: 35 -> 46; matrix products, arithmetic and copies ran while one was open for 1% -> 2% of each run, Pallas kernels for 11% -> 14%
where the time goes in v3:
time: 212 us; the launch traced here: 208 us
  waiting for transfers between devices  67.8 us (32%)
  starting transfers between devices  66.2 us (31%)
  Pallas kernels  58.1 us (27%)
  local copies, waits for them, and re-layouts  11.7 us (6%)
  matrix products  2.18 us (1%)
    pallas_call x13, Pallas kernels, call(): pl.pallas_call(kernel, out_shape=[jax.ShapeDtypeStruct(shape, kind) for s...  58.1 us
    ppermute x28, starting transfers between devices, ring_sum(): one, two = (lax.ppermute(one, 'dp', onward), lax.ppermute(two, 'dp', back))  29.8 us
    ppermute x28, starting transfers between devices, ring_gather(): one, two = (lax.ppermute(one, 'dp', onward), lax.ppermute(two, 'dp', back))  27 us
    ppermute x14, waiting for transfers between devices, swap(): return lax.ppermute(values, axis, [(0, 1), (1, 0)])  27 us
    ppermute x28, waiting for transfers between devices, ring_sum(): one, two = (lax.ppermute(one, 'dp', onward), lax.ppermute(two, 'dp', back))  15.3 us
    ppermute x2, waiting for transfers between devices, block(): from_dp = lax.ppermute(pack, 'dp', neighbours)  15 us
    ppermute x28, waiting for transfers between devices, ring_gather(): one, two = (lax.ppermute(one, 'dp', onward), lax.ppermute(two, 'dp', back))  10.6 us
    unnamed x108, local copies, waits for them, and re-layouts  10.4 us
  transfers between devices with their start and end apart: 72, of which 46 were waited for; matrix products, arithmetic and copies ran while one was open for 2% of the time, Pallas kernels for 14%

profile of v3, /device:TPU:0, one launch (start us, length us, event | category | flops | bytes accessed | tf_op | source)
XLA Modules:
  0.0 208.3 jit_solution(5607938024038091891)
XLA Ops:
  3.4 5.0 %shard_map.319 = (bf16[1968,256]{1,0:T(8,128)(2,1)}, bf16[1536,256]{1,0:T(8,128)(2,1)}, bf16[6144,256]{1,0:T(8,128)(2,1)}) custom-call(s32[1]{0:T(128)} %bitcast.parity_ref, bf16[2,3,256,256]{3,2,1,0:T(8,128)(2,1)} %bitcast.86, bf16[2,256,256]{2,1,0:T(8,128)(2,1)} %refs_8_.3, bf16[2,256,1024]{2,1,0:T(8,128)(2,1)} %refs_0_.5, bf16[2,1024,256]{2,1,0:T(8,128)(2,1)} %refs_1_.9, ...), custom_call_target="tpu_custom_call" | custom-call | flops 3450000 | tf_op jit(solution)/shard_map/pallas_call | solution.py:663
  8.9 2.6 %collective-permute-start.2 = (bf16[1968,256]{1,0:T(8,128)(2,1)}, bf16[1968,256]{1,0:T(8,128)(2,1)S(1)}, u32[]{:S(2)}, u32[]{:S(2)}) collective-permute-start(bf16[1968,256]{1,0:T(8,128)(2,1)} %get-tuple-element.75), channel_id=1, source_target_pairs={{0,1},{1,0},{2,3},{3,2},{4,5},{5,4},{6,7},{7,6},{8,9},{9,8},{10,11... | collective-permute-start | bytes 3022856 | tf_op jit(solution)/shard_map/ppermute | solution.py:41
  11.5 23.1 %collective-permute-done.2 = bf16[1968,256]{1,0:T(8,128)(2,1)S(1)} collective-permute-done((bf16[1968,256]{1,0:T(8,128)(2,1)}, bf16[1968,256]{1,0:T(8,128)(2,1)S(1)}, u32[]{:S(2)}, u32[]{:S(2)}) %collective-permute-start.2) | collective-permute-done | bytes 1007648 | tf_op jit(solution)/shard_map/ppermute | solution.py:41
  34.6 1.8 collective-permute-start.3
  39.6 3.6 %shard_map.320 = (f32[256,512]{1,0:T(8,128)S(1)}, f32[256,512]{1,0:T(8,128)S(1)}, f32[16,512]{1,0:T(8,128)S(1)}, f32[16,512]{1,0:T(8,128)S(1)}, f32[16,128,128]{...) custom-call(s32[1]{0:T(128)} %bitcast.parity_ref, bf16[432,256]{1,0:T(8,128)(2,1)S(1)} %slice.36.misc_ref, ...), custom_call_target="tpu_custom_call" | custom-call | flops 4600000 | tf_op jit(solution)/shard_map/pallas_call | solution.py:663
  43.9 10.1 %collective-permute-done.3.refs_0_ = bf16[1536,256]{1,0:T(8,128)(2,1)S(1)} collective-permute-done((bf16[1536,256]{1,0:T(8,128)(2,1)S(1)}, bf16[1536,256]{1,0:T(8,128)(2,1)S(1)}, u32[]{:S(2)}, u32[]{:S(2)}) %collective-permute-start.3) | collective-permute-done | bytes 786464 | tf_op jit(solution)/shard_map/ppermute | solution.py:862
  56.4 6.6 %shard_map.322 = (f32[256,512]{1,0:T(8,128)S(1)}, bf16[256,512]{1,0:T(8,128)(2,1)S(1)}, bf16[2,256,768]{2,1,0:T(8,128)(2,1)S(1)}, bf16[2,4,512,128]{3,2,1,0:T(8,128)(2,1)S(1)}, bf16[256,512]{1,0:T(8,128)(2,1)S(1)}) custom-call(bf16[2,3,256,256]{3,2,1,0:T(8,128)(2,1)S(1)} %bitcast.87, bf16[2,256,256]{2,1,0:T(8,128)(2,1)S(1)} %copy-done.15, ...), custom_call_target="tpu_custom_call" | custom-call | flops 4600000 | tf_op jit(solution)/shard_map/pallas_call | solution.py:663
  64.9 3.7 %shard_map.323 = (f32[256,512]{1,0:T(8,128)S(1)}, bf16[256,512]{1,0:T(8,128)(2,1)S(1)}, bf16[256,2048]{1,0:T(8,128)(2,1)S(1)}, bf16[256,2048]{1,0:T(8,128)(2,1)S(1)}) custom-call(bf16[2,256,1024]{2,1,0:T(8,128)(2,1)S(1)} %copy-done.7, bf16[2,1024,256]{2,1,0:T(8,128)(2,1)S(1)} %copy-done.9, bf16[1536,256]{1,0:T(8,128)(2,1)S(1)} %slice.46.refs_2_.refs_9_, ...), custom_call_target="tpu_custom_call" | custom-call | flops 4600000 | tf_op jit(solution)/shard_map/pallas_call | solution.py:663
  69.4 4.9 %collective-permute-done.1.refs_0_ = bf16[1536,256]{1,0:T(8,128)(2,1)} collective-permute-done((bf16[1536,256]{1,0:T(8,128)(2,1)}, bf16[1536,256]{1,0:T(8,128)(2,1)}, u32[]{:S(2)}, u32[]{:S(2)}) %collective-permute-start.1) | collective-permute-done | bytes 786464 | tf_op jit(solution)/shard_map/ppermute | solution.py:862
  75.6 2.1 %collective-permute-done.9.refs_6_.refs_13_ = bf16[1536,256]{1,0:T(8,128)(2,1)} collective-permute-done((bf16[1536,256]{1,0:T(8,128)(2,1)}, bf16[1536,256]{1,0:T(8,128)(2,1)}, u32[]{:S(2)}, u32[]{:S(2)}) %collective-permute-start.9) | collective-permute-done | bytes 786464 | tf_op jit(solution)/shard_map/ppermute | solution.py:41
  81.1 5.1 %shard_map.325 = (f32[256,512]{1,0:T(8,128)S(1)}, bf16[256,512]{1,0:T(8,128)(2,1)S(1)}, bf16[2,256,768]{2,1,0:T(8,128)(2,1)S(1)}, bf16[2,4,512,128]{3,2,1,0:T(8,128)(2,1)S(1)}, bf16[256,512]{1,0:T(8,128)(2,1)S(1)}) custom-call(bf16[2,3,256,256]{3,2,1,0:T(8,128)(2,1)S(1)} %bitcast.88, bf16[2,256,256]{2,1,0:T(8,128)(2,1)S(1)} %copy-done.15, ...), custom_call_target="tpu_custom_call" | custom-call | flops 4600000 | tf_op jit(solution)/shard_map/pallas_call | solution.py:663
  86.5 13.9 %shard_map.326 = (bf16[196,256]{1,0:T(8,128)(2,1)}, bf16[2048,256]{1,0:T(8,128)(2,1)S(1)}, bf16[2048,256]{1,0:T(8,128)(2,1)S(1)}, f32[8,256]{1,0:T(8,128)S(1)}, ...) custom-call(bf16[2,256,1024]{2,1,0:T(8,128)(2,1)S(1)} %copy-done.8, ...), custom_call_target="tpu_custom_call" | custom-call | flops 13800000 | tf_op jit(solution)/shard_map/pallas_call | solution.py:663
  100.7 14.8 %shard_map.327 = (bf16[2048,256]{1,0:T(8,128)(2,1)S(1)}, bf16[2048,256]{1,0:T(8,128)(2,1)S(1)}, f32[8,256]{1,0:T(8,128)S(1)}, f32[8,256]{1,0:T(8,128)S(1)}, bf16...) custom-call(bf16[2,256,1024]{2,1,0:T(8,128)(2,1)S(1)} %copy-done.8, ...), custom_call_target="tpu_custom_call" | custom-call | flops 13800000 | tf_op jit(solution)/shard_map/pallas_call | solution.py:663
  120.1 1.7 collective-permute-start.44
  123.2 1.7 collective-permute-start.13
  126.7 1.6 collective-permute-start.45
  132.2 1.8 collective-permute-done.52
  140.4 2.0 collective-permute-start.47
  143.3 2.3 %collective-permute-start.16 = (bf16[200,256]{1,0:T(8,128)(2,1)S(1)}, bf16[200,256]{1,0:T(8,128)(2,1)S(1)}, u32[]{:S(2)}, u32[]{:S(2)}) collective-permute-start(bf16[200,256]{1,0:T(8,128)(2,1)S(1)} %get-tuple-element.158), channel_id=1, source_target_pairs={{0,8},{8,16},{16,24},{24,28},{28,20},{20,12},{12,4},{4,0},{1,9},{9... | collective-permute-start | bytes 307208 | tf_op jit(solution)/shard_map/ppermute | solution.py:800
  145.8 1.8 collective-permute-done.54
  148.1 1.7 collective-permute-start.55
  153.5 1.8 collective-permute-start.56
  163.3 2.0 collective-permute-start.26
  165.9 1.9 collective-permute-start.59
  171.4 2.1 %collective-permute-start.61 = (bf16[200,256]{1,0:T(8,128)(2,1)S(1)}, bf16[200,256]{1,0:T(8,128)(2,1)S(1)}, u32[]{:S(2)}, u32[]{:S(2)}) collective-permute-start(bf16[200,256]{1,0:T(8,128)(2,1)S(1)} %collective-permute-done.59.refs_20_), channel_id=1, source_target_pairs={{8,0},{16,8},{24,16},{28,24},{20,28},{12,20},{4,12},{0,4},{9,1},{1... | collective-permute-start | bytes 307208 | tf_op jit(solution)/shard_map/ppermute | solution.py:814
  176.7 1.9 collective-permute-start.63
  182.4 2.0 collective-permute-start.65
  187.7 1.9 collective-permute-start.67
  192.3 1.9 collective-permute-start.69
  197.0 1.9 collective-permute-start.71
  201.6 1.9 collective-permute-done.39.refs_15_
  204.1 3.9 %shard_map.330 = (f32[2,3,256,256]{3,2,1,0:T(8,128)}, f32[2,2,256]{2,1,0:T(2,128)}, f32[2,256,256]{2,1,0:T(8,128)}, f32[2,256]{1,0:T(2,128)}, f32[2,256,1024]{2,...) custom-call(s32[16]{0:T(128)S(1)} %stack.67.refs_0_, ...), custom_call_target="tpu_custom_call" | custom-call | flops 4600000 | tf_op jit(solution)/shard_map/pallas_call | solution.py:663
  (266 shorter events, 71.7 us)
Async XLA Ops:
  8.4 47.9 %collective-permute-start.5 = (bf16[6144,256]{1,0:T(8,128)(2,1)}, bf16[6144,256]{1,0:T(8,128)(2,1)S(1)}, u32[]{:S(2)}, u32[]{:S(2)}) collective-permute-start(bf16[6144,256]{1,0:T(8,128)(2,1)} %get-tuple-element.77), channel_id=1, source_target_pairs={{0,2},{2,0},{1,3},{3,1},{4,6},{6,4},{5,7},{7,5},{8,10},{10,8},{9,1... | collective-permute-start | bytes 9437192 | tf_op jit(solution)/shard_map/ppermute | solution.py:41
  8.9 25.7 %collective-permute-start.2 = (bf16[1968,256]{1,0:T(8,128)(2,1)}, bf16[1968,256]{1,0:T(8,128)(2,1)S(1)}, u32[]{:S(2)}, u32[]{:S(2)}) collective-permute-start(bf16[1968,256]{1,0:T(8,128)(2,1)} %get-tuple-element.75), channel_id=1, source_target_pairs={{0,1},{1,0},{2,3},{3,2},{4,5},{5,4},{6,7},{7,6},{8,9},{9,8},{10,11... | collective-permute-start | bytes 3022856 | tf_op jit(solution)/shard_map/ppermute | solution.py:41
  34.6 19.4 %collective-permute-start.3 = (bf16[1536,256]{1,0:T(8,128)(2,1)S(1)}, bf16[1536,256]{1,0:T(8,128)(2,1)S(1)}, u32[]{:S(2)}, u32[]{:S(2)}) collective-permute-start(bf16[1536,256]{1,0:T(8,128)(2,1)S(1)} %slice.46.refs_2_.refs_9_), channel_id=1, source_target_pairs={{0,4},{4,0},{8,12},{12,8},{16,20},{20,16},{24,28},{28,24},{1,5},{5... | collective-permute-start | bytes 2359304 | tf_op jit(solution)/shard_map/ppermute | solution.py:862
  36.4 19.1 %collective-permute-start = (bf16[1536,256]{1,0:T(8,128)(2,1)}, bf16[1536,256]{1,0:T(8,128)(2,1)}, u32[]{:S(2)}, u32[]{:S(2)}) collective-permute-start(bf16[1536,256]{1,0:T(8,128)(2,1)} %get-tuple-element.74), channel_id=1, source_target_pairs={{0,1},{1,0},{2,3},{3,2},{4,5},{5,4},{6,7},{7,6},{8,9},{9,8},{10,11... | collective-permute-start | bytes 2359304 | tf_op jit(solution)/shard_map/ppermute | solution.py:41
  38.9 17.1 %collective-permute-start.6 = (bf16[1536,256]{1,0:T(8,128)(2,1)S(1)}, bf16[1536,256]{1,0:T(8,128)(2,1)S(1)}, u32[]{:S(2)}, u32[]{:S(2)}) collective-permute-start(bf16[1536,256]{1,0:T(8,128)(2,1)S(1)} %slice.46.refs_2_.refs_9_), channel_id=1, source_target_pairs={{0,2},{2,0},{1,3},{3,1},{4,6},{6,4},{5,7},{7,5},{8,10},{10,8},{9,1... | collective-permute-start | bytes 2359304 | tf_op jit(solution)/shard_map/ppermute | solution.py:41
  55.6 18.7 %collective-permute-start.1 = (bf16[1536,256]{1,0:T(8,128)(2,1)}, bf16[1536,256]{1,0:T(8,128)(2,1)}, u32[]{:S(2)}, u32[]{:S(2)}) collective-permute-start(bf16[1536,256]{1,0:T(8,128)(2,1)} %collective-permute-done.refs_11_.refs_2_.refs_9_), channel_id=1, source_target_pairs={{0,4},{4,0},{8,12},{12,8},{16,20},{20,16},{24,28},{28,24},{1,5},{5... | collective-permute-start | bytes 2359304 | tf_op jit(solution)/shard_map/ppermute | solution.py:862
  56.1 19.5 %collective-permute-start.8 = (bf16[1536,256]{1,0:T(8,128)(2,1)}, bf16[1536,256]{1,0:T(8,128)(2,1)}, u32[]{:S(2)}, u32[]{:S(2)}) collective-permute-start(bf16[1536,256]{1,0:T(8,128)(2,1)} %collective-permute-done.refs_11_.refs_2_.refs_9_), channel_id=1, source_target_pairs={{0,2},{2,0},{1,3},{3,1},{4,6},{6,4},{5,7},{7,5},{8,10},{10,8},{9,1... | collective-permute-start | bytes 2359304 | tf_op jit(solution)/shard_map/ppermute | solution.py:41
  100.3 19.0 %collective-permute-start.41 = (bf16[2048,256]{1,0:T(8,128)(2,1)S(1)}, bf16[2048,256]{1,0:T(8,128)(2,1)S(1)}, u32[]{:S(2)}, u32[]{:S(2)}) collective-permute-start(bf16[2048,256]{1,0:T(8,128)(2,1)S(1)} %get-tuple-element.113), channel_id=1, source_target_pairs={{0,2},{2,0},{1,3},{3,1},{4,6},{6,4},{5,7},{7,5},{8,10},{10,8},{9,1... | collective-permute-start | bytes 3145736 | tf_op jit(solution)/shard_map/ppermute | solution.py:41
  115.4 7.0 %collective-permute-start.10 = (bf16[2048,256]{1,0:T(8,128)(2,1)S(1)}, bf16[2048,256]{1,0:T(8,128)(2,1)S(1)}, u32[]{:S(2)}, u32[]{:S(2)}) collective-permute-start(bf16[2048,256]{1,0:T(8,128)(2,1)S(1)} %get-tuple-element.101), channel_id=1, source_target_pairs={{0,2},{2,0},{1,3},{3,1},{4,6},{6,4},{5,7},{7,5},{8,10},{10,8},{9,1... | collective-permute-start | bytes 3145736 | tf_op jit(solution)/shard_map/ppermute | solution.py:41
  123.2 5.6 %collective-permute-start.13 = (bf16[200,256]{1,0:T(8,128)(2,1)S(1)}, bf16[200,256]{1,0:T(8,128)(2,1)S(1)}, u32[]{:S(2)}, u32[]{:S(2)}) collective-permute-start(bf16[200,256]{1,0:T(8,128)(2,1)S(1)} %get-tuple-element.109), channel_id=1, source_target_pairs={{0,8},{8,16},{16,24},{24,28},{28,20},{20,12},{12,4},{4,0},{1,9},{9... | collective-permute-start | bytes 307208 | tf_op jit(solution)/shard_map/ppermute | solution.py:800
  126.7 5.5 %collective-permute-start.45 = (bf16[200,256]{1,0:T(8,128)(2,1)S(1)}, bf16[200,256]{1,0:T(8,128)(2,1)S(1)}, u32[]{:S(2)}, u32[]{:S(2)}) collective-permute-start(bf16[200,256]{1,0:T(8,128)(2,1)S(1)} %get-tuple-element.148), channel_id=1, source_target_pairs={{0,8},{8,16},{16,24},{24,28},{28,20},{20,12},{12,4},{4,0},{1,9},{9... | collective-permute-start | bytes 307208 | tf_op jit(solution)/shard_map/ppermute | solution.py:800
  128.3 5.7 %collective-permute-start.52 = (bf16[200,256]{1,0:T(8,128)(2,1)S(1)}, bf16[200,256]{1,0:T(8,128)(2,1)S(1)}, u32[]{:S(2)}, u32[]{:S(2)}) collective-permute-start(bf16[200,256]{1,0:T(8,128)(2,1)S(1)} %get-tuple-element.147), channel_id=1, source_target_pairs={{8,0},{16,8},{24,16},{28,24},{20,28},{12,20},{4,12},{0,4},{9,1},{1... | collective-permute-start | bytes 307208 | tf_op jit(solution)/shard_map/ppermute | solution.py:800
  129.7 6.3 %collective-permute-start.14 = (bf16[200,256]{1,0:T(8,128)(2,1)S(1)}, bf16[200,256]{1,0:T(8,128)(2,1)S(1)}, u32[]{:S(2)}, u32[]{:S(2)}) collective-permute-start(bf16[200,256]{1,0:T(8,128)(2,1)S(1)} %get-tuple-element.162), channel_id=1, source_target_pairs={{0,8},{8,16},{16,24},{24,28},{28,20},{20,12},{12,4},{4,0},{1,9},{9... | collective-permute-start | bytes 307208 | tf_op jit(solution)/shard_map/ppermute | solution.py:800
  131.4 5.5 %collective-permute-start.21 = (bf16[200,256]{1,0:T(8,128)(2,1)S(1)}, bf16[200,256]{1,0:T(8,128)(2,1)S(1)}, u32[]{:S(2)}, u32[]{:S(2)}) collective-permute-start(bf16[200,256]{1,0:T(8,128)(2,1)S(1)} %get-tuple-element.161), channel_id=1, source_target_pairs={{8,0},{16,8},{24,16},{28,24},{20,28},{12,20},{4,12},{0,4},{9,1},{1... | collective-permute-start | bytes 307208 | tf_op jit(solution)/shard_map/ppermute | solution.py:800
  136.9 5.5 %collective-permute-start.15 = (bf16[200,256]{1,0:T(8,128)(2,1)S(1)}, bf16[200,256]{1,0:T(8,128)(2,1)S(1)}, u32[]{:S(2)}, u32[]{:S(2)}) collective-permute-start(bf16[200,256]{1,0:T(8,128)(2,1)S(1)} %get-tuple-element.160), channel_id=1, source_target_pairs={{0,8},{8,16},{16,24},{24,28},{28,20},{20,12},{12,4},{4,0},{1,9},{9... | collective-permute-start | bytes 307208 | tf_op jit(solution)/shard_map/ppermute | solution.py:800
  140.4 5.4 %collective-permute-start.47 = (bf16[200,256]{1,0:T(8,128)(2,1)S(1)}, bf16[200,256]{1,0:T(8,128)(2,1)S(1)}, u32[]{:S(2)}, u32[]{:S(2)}) collective-permute-start(bf16[200,256]{1,0:T(8,128)(2,1)S(1)} %get-tuple-element.144), channel_id=1, source_target_pairs={{0,8},{8,16},{16,24},{24,28},{28,20},{20,12},{12,4},{4,0},{1,9},{9... | collective-permute-start | bytes 307208 | tf_op jit(solution)/shard_map/ppermute | solution.py:800
  143.3 6.5 %collective-permute-start.16 = (bf16[200,256]{1,0:T(8,128)(2,1)S(1)}, bf16[200,256]{1,0:T(8,128)(2,1)S(1)}, u32[]{:S(2)}, u32[]{:S(2)}) collective-permute-start(bf16[200,256]{1,0:T(8,128)(2,1)S(1)} %get-tuple-element.158), channel_id=1, source_target_pairs={{0,8},{8,16},{16,24},{24,28},{28,20},{20,12},{12,4},{4,0},{1,9},{9... | collective-permute-start | bytes 307208 | tf_op jit(solution)/shard_map/ppermute | solution.py:800
  150.3 5.6 %collective-permute-start.17 = (bf16[200,256]{1,0:T(8,128)(2,1)S(1)}, bf16[200,256]{1,0:T(8,128)(2,1)S(1)}, u32[]{:S(2)}, u32[]{:S(2)}) collective-permute-start(bf16[200,256]{1,0:T(8,128)(2,1)S(1)} %get-tuple-element.156), channel_id=1, source_target_pairs={{0,8},{8,16},{16,24},{24,28},{28,20},{20,12},{12,4},{4,0},{1,9},{9... | collective-permute-start | bytes 307208 | tf_op jit(solution)/shard_map/ppermute | solution.py:800
  151.4 5.7 %collective-permute-start.24 = (bf16[200,256]{1,0:T(8,128)(2,1)S(1)}, bf16[200,256]{1,0:T(8,128)(2,1)S(1)}, u32[]{:S(2)}, u32[]{:S(2)}) collective-permute-start(bf16[200,256]{1,0:T(8,128)(2,1)S(1)} %get-tuple-element.155), channel_id=1, source_target_pairs={{8,0},{16,8},{24,16},{28,24},{20,28},{12,20},{4,12},{0,4},{9,1},{1... | collective-permute-start | bytes 307208 | tf_op jit(solution)/shard_map/ppermute | solution.py:800
  153.0 6.1 %collective-permute-start.49 = (bf16[200,256]{1,0:T(8,128)(2,1)S(1)}, bf16[200,256]{1,0:T(8,128)(2,1)S(1)}, u32[]{:S(2)}, u32[]{:S(2)}) collective-permute-start(bf16[200,256]{1,0:T(8,128)(2,1)S(1)} %get-tuple-element.140), channel_id=1, source_target_pairs={{0,8},{8,16},{16,24},{24,28},{28,20},{20,12},{12,4},{4,0},{1,9},{9... | collective-permute-start | bytes 307208 | tf_op jit(solution)/shard_map/ppermute | solution.py:800
  153.5 5.7 %collective-permute-start.56 = (bf16[200,256]{1,0:T(8,128)(2,1)S(1)}, bf16[200,256]{1,0:T(8,128)(2,1)S(1)}, u32[]{:S(2)}, u32[]{:S(2)}) collective-permute-start(bf16[200,256]{1,0:T(8,128)(2,1)S(1)} %get-tuple-element.139), channel_id=1, source_target_pairs={{8,0},{16,8},{24,16},{28,24},{20,28},{12,20},{4,12},{0,4},{9,1},{1... | collective-permute-start | bytes 307208 | tf_op jit(solution)/shard_map/ppermute | solution.py:800
  157.8 5.4 %collective-permute-start.25 = (bf16[200,256]{1,0:T(8,128)(2,1)S(1)}, bf16[200,256]{1,0:T(8,128)(2,1)S(1)}, u32[]{:S(2)}, u32[]{:S(2)}) collective-permute-start(bf16[200,256]{1,0:T(8,128)(2,1)S(1)} %get-tuple-element.153), channel_id=1, source_target_pairs={{8,0},{16,8},{24,16},{28,24},{20,28},{12,20},{4,12},{0,4},{9,1},{1... | collective-permute-start | bytes 307208 | tf_op jit(solution)/shard_map/ppermute | solution.py:800
  159.2 6.1 %collective-permute-start.50 = (bf16[200,256]{1,0:T(8,128)(2,1)S(1)}, bf16[200,256]{1,0:T(8,128)(2,1)S(1)}, u32[]{:S(2)}, u32[]{:S(2)}) collective-permute-start(bf16[200,256]{1,0:T(8,128)(2,1)S(1)} %get-tuple-element.138), channel_id=1, source_target_pairs={{0,8},{8,16},{16,24},{24,28},{28,20},{20,12},{12,4},{4,0},{1,9},{9... | collective-permute-start | bytes 307208 | tf_op jit(solution)/shard_map/ppermute | solution.py:800
  159.9 5.8 %collective-permute-start.57 = (bf16[200,256]{1,0:T(8,128)(2,1)S(1)}, bf16[200,256]{1,0:T(8,128)(2,1)S(1)}, u32[]{:S(2)}, u32[]{:S(2)}) collective-permute-start(bf16[200,256]{1,0:T(8,128)(2,1)S(1)} %get-tuple-element.137), channel_id=1, source_target_pairs={{8,0},{16,8},{24,16},{28,24},{20,28},{12,20},{4,12},{0,4},{9,1},{1... | collective-permute-start | bytes 307208 | tf_op jit(solution)/shard_map/ppermute | solution.py:800
  165.8 5.7 %collective-permute-start.58 = (bf16[200,256]{1,0:T(8,128)(2,1)S(1)}, bf16[200,256]{1,0:T(8,128)(2,1)S(1)}, u32[]{:S(2)}, u32[]{:S(2)}) collective-permute-start(bf16[200,256]{1,0:T(8,128)(2,1)S(1)} %get-tuple-element.136.refs_17_), channel_id=1, source_target_pairs={{0,8},{8,16},{16,24},{24,28},{28,20},{20,12},{12,4},{4,0},{1,9},{9... | collective-permute-start | bytes 307208 | tf_op jit(solution)/shard_map/ppermute | solution.py:814
  165.9 5.5 %collective-permute-start.59 = (bf16[200,256]{1,0:T(8,128)(2,1)S(1)}, bf16[200,256]{1,0:T(8,128)(2,1)S(1)}, u32[]{:S(2)}, u32[]{:S(2)}) collective-permute-start(bf16[200,256]{1,0:T(8,128)(2,1)S(1)} %get-tuple-element.135.refs_18_), channel_id=1, source_target_pairs={{8,0},{16,8},{24,16},{28,24},{20,28},{12,20},{4,12},{0,4},{9,1},{1... | collective-permute-start | bytes 307208 | tf_op jit(solution)/shard_map/ppermute | solution.py:814
  169.0 5.8 %collective-permute-start.28 = (bf16[200,256]{1,0:T(8,128)(2,1)S(1)}, bf16[200,256]{1,0:T(8,128)(2,1)S(1)}, u32[]{:S(2)}, u32[]{:S(2)}) collective-permute-start(bf16[200,256]{1,0:T(8,128)(2,1)S(1)} %get-tuple-element.149.refs_2_), channel_id=1, source_target_pairs={{8,0},{16,8},{24,16},{28,24},{20,28},{12,20},{4,12},{0,4},{9,1},{1... | collective-permute-start | bytes 307208 | tf_op jit(solution)/shard_map/ppermute | solution.py:814
  171.4 5.3 %collective-permute-start.61 = (bf16[200,256]{1,0:T(8,128)(2,1)S(1)}, bf16[200,256]{1,0:T(8,128)(2,1)S(1)}, u32[]{:S(2)}, u32[]{:S(2)}) collective-permute-start(bf16[200,256]{1,0:T(8,128)(2,1)S(1)} %collective-permute-done.59.refs_20_), channel_id=1, source_target_pairs={{8,0},{16,8},{24,16},{28,24},{20,28},{12,20},{4,12},{0,4},{9,1},{1... | collective-permute-start | bytes 307208 | tf_op jit(solution)/shard_map/ppermute | solution.py:814
  176.7 5.8 %collective-permute-start.62 = (bf16[200,256]{1,0:T(8,128)(2,1)S(1)}, bf16[200,256]{1,0:T(8,128)(2,1)S(1)}, u32[]{:S(2)}, u32[]{:S(2)}) collective-permute-start(bf16[200,256]{1,0:T(8,128)(2,1)S(1)} %collective-permute-done.60.refs_21_), channel_id=1, source_target_pairs={{0,8},{8,16},{16,24},{24,28},{28,20},{20,12},{12,4},{4,0},{1,9},{9... | collective-permute-start | bytes 307208 | tf_op jit(solution)/shard_map/ppermute | solution.py:814
  176.7 5.7 %collective-permute-start.63 = (bf16[200,256]{1,0:T(8,128)(2,1)S(1)}, bf16[200,256]{1,0:T(8,128)(2,1)S(1)}, u32[]{:S(2)}, u32[]{:S(2)}) collective-permute-start(bf16[200,256]{1,0:T(8,128)(2,1)S(1)} %collective-permute-done.61.refs_22_), channel_id=1, source_target_pairs={{8,0},{16,8},{24,16},{28,24},{20,28},{12,20},{4,12},{0,4},{9,1},{1... | collective-permute-start | bytes 307208 | tf_op jit(solution)/shard_map/ppermute | solution.py:814
  178.7 5.9 %collective-permute-start.31 = (bf16[200,256]{1,0:T(8,128)(2,1)S(1)}, bf16[200,256]{1,0:T(8,128)(2,1)S(1)}, u32[]{:S(2)}, u32[]{:S(2)}) collective-permute-start(bf16[200,256]{1,0:T(8,128)(2,1)S(1)} %collective-permute-done.29.refs_5_), channel_id=1, source_target_pairs={{0,8},{8,16},{16,24},{24,28},{28,20},{20,12},{12,4},{4,0},{1,9},{9... | collective-permute-start | bytes 307208 | tf_op jit(solution)/shard_map/ppermute | solution.py:814
  180.0 5.6 %collective-permute-start.32 = (bf16[200,256]{1,0:T(8,128)(2,1)S(1)}, bf16[200,256]{1,0:T(8,128)(2,1)S(1)}, u32[]{:S(2)}, u32[]{:S(2)}) collective-permute-start(bf16[200,256]{1,0:T(8,128)(2,1)S(1)} %collective-permute-done.30.refs_6_), channel_id=1, source_target_pairs={{8,0},{16,8},{24,16},{28,24},{20,28},{12,20},{4,12},{0,4},{9,1},{1... | collective-permute-start | bytes 307208 | tf_op jit(solution)/shard_map/ppermute | solution.py:814
  (94 other events, 721.4 us)

commit v4 on v3

--- a/solution.py
+++ b/solution.py
@@ -315,7 +315,7 @@
 FFN_ROOMS = [((D, FF // 2), BF), ((FF // 2, D), BF)] * 2
 
 
-def misc_kernel(qv_bias, up_bias, table, misc_row):
+def misc_kernel(qv_bias, up_bias, table, _, misc_row):
     half = D // 2
     rows = [qv_bias[0], qv_bias[1]] + [up_bias[:, piece * half : (piece + 1) * half] for piece in range(4)]
     rows = [row.astype(F32) for row in rows] + [jnp.zeros((4, half), F32)]
@@ -325,7 +325,7 @@
 
 
 def pack_kernel(
-    parity_ref, qkv, out, up, down, tokens, cot, gain, shift, out_bias, down_bias, _,
+    parity_ref, qkv, out, up, down, tokens, cot, gain, shift, out_bias, down_bias,
     pack_zero, pack_one, whole, *rest,
 ):
     rooms, results, (in_sems, out_sems) = rest[:8], rest[8:11], rest[11:]
@@ -834,10 +834,6 @@
 
     wholes = [qkv_weight.transpose(0, 2, 1, 3), out_weight, up_weight, down_weight]
     parity_ref = parity.astype(jnp.int32).reshape(1)
-    (misc_row,) = call(
-        misc_kernel, [((32, half), BF)], [], [qv_bias, up_bias, bias_table.transpose(0, 2, 1)], 1
-    )
-    row_far = swap(misc_row, "row")
     sources = [*wholes, tokens, cotangent, norm_gain, norm_shift, out_bias, down_bias]
     pack_outs = [((MISC_ROWS, half), BF), ((3 * D, half), BF), ((3 * D, half), BF)]
     packs = [None, None]
@@ -847,12 +843,21 @@
         [pltpu.VMEM(value.shape[1:], value.dtype) for value in wholes] * LAYERS
         + [pltpu.VMEM(shape, kind) for shape, kind in pack_outs]
         + [pltpu.SemaphoreType.DMA((8,)), pltpu.SemaphoreType.DMA((21,))],
-        [parity_ref, *sources, misc_row],
+        [parity_ref, *sources],
         3,
-        [SMEM] + [ANY] * 4 + [VMEM] * 6 + [ANY],
+        [SMEM] + [ANY] * 4 + [VMEM] * 6,
         [ANY] * 3,
         limit=60,
     )
+    (misc_row,) = call(
+        misc_kernel,
+        [((32, half), BF)],
+        [],
+        [qv_bias, up_bias, bias_table.transpose(0, 2, 1), packs[1]],
+        1,
+        [VMEM] * 3 + [ANY],
+    )
+    row_far = swap(misc_row, "row")
     whole_row = swap(whole, "row")
     from_col = [swap(pack, "col") for pack in packs]
     misc, misc_far = packs[0][:MISC_ROWS], from_col[0][:MISC_ROWS]

time: 212 us -> 210 us (level)
  waiting for transfers between devices: 67.8 us -> 64.8 us
    unnamed x108 -> x106, local copies, waits for them, and re-layouts: 10.4 us -> 9.15 us
  transfers between devices with their start and end apart: 72 -> 72, of which waited for: 46 -> 44; matrix products, arithmetic and copies ran while one was open for 2% -> 2% of each run, Pallas kernels for 14% -> 15%
where the time goes in v4:
time: 210 us; the launch traced here: 206 us
  starting transfers between devices  67.8 us (32%)
  waiting for transfers between devices  64.8 us (31%)
  Pallas kernels  58.1 us (28%)
  local copies, waits for them, and re-layouts  10.5 us (5%)
  matrix products  2.18 us (1%)
    pallas_call x13, Pallas kernels, call(): pl.pallas_call(kernel, out_shape=[jax.ShapeDtypeStruct(shape, kind) for s...  58.1 us
    ppermute x28, starting transfers between devices, ring_sum(): one, two = (lax.ppermute(one, 'dp', onward), lax.ppermute(two, 'dp', back))  29.8 us
    ppermute x28, starting transfers between devices, ring_gather(): one, two = (lax.ppermute(one, 'dp', onward), lax.ppermute(two, 'dp', back))  28.5 us
    ppermute x14, waiting for transfers between devices, swap(): return lax.ppermute(values, axis, [(0, 1), (1, 0)])  27 us
    ppermute x28, waiting for transfers between devices, ring_sum(): one, two = (lax.ppermute(one, 'dp', onward), lax.ppermute(two, 'dp', back))  15.3 us
    ppermute x2, waiting for transfers between devices, block(): from_dp = lax.ppermute(pack, 'dp', neighbours)  13.5 us
    unnamed x106, local copies, waits for them, and re-layouts  9.15 us
    ppermute x28, waiting for transfers between devices, ring_gather(): one, two = (lax.ppermute(one, 'dp', onward), lax.ppermute(two, 'dp', back))  9.12 us
  transfers between devices with their start and end apart: 72, of which 44 were waited for; matrix products, arithmetic and copies ran while one was open for 2% of the time, Pallas kernels for 15%

profile of v4, /device:TPU:0, one launch (start us, length us, event | category | flops | bytes accessed | tf_op | source)
XLA Modules:
  0.0 205.7 jit_solution(9718594258446471346)
XLA Ops:
  0.7 5.0 %shard_map.318 = (bf16[1968,256]{1,0:T(8,128)(2,1)}, bf16[1536,256]{1,0:T(8,128)(2,1)}, bf16[6144,256]{1,0:T(8,128)(2,1)}) custom-call(s32[1]{0:T(128)} %bitcast.parity_ref, bf16[2,3,256,256]{3,2,1,0:T(8,128)(2,1)} %bitcast.86, bf16[2,256,256]{2,1,0:T(8,128)(2,1)} %refs_8_.3, bf16[2,256,1024]{2,1,0:T(8,128)(2,1)} %refs_0_.5, bf16[2,1024,256]{2,1,0:T(8,128)(2,1)} %refs_1_.9, ...), custom_call_target="tpu_custom_call" | custom-call | flops 3450000 | tf_op jit(solution)/shard_map/pallas_call | solution.py:663
  6.2 2.6 %collective-permute-start.2 = (bf16[1968,256]{1,0:T(8,128)(2,1)}, bf16[1968,256]{1,0:T(8,128)(2,1)S(1)}, u32[]{:S(2)}, u32[]{:S(2)}) collective-permute-start(bf16[1968,256]{1,0:T(8,128)(2,1)} %get-tuple-element.75), channel_id=1, source_target_pairs={{0,1},{1,0},{2,3},{3,2},{4,5},{5,4},{6,7},{7,6},{8,9},{9,8},{10,11... | collective-permute-start | bytes 3022856 | tf_op jit(solution)/shard_map/ppermute | solution.py:41
  8.8 23.1 %collective-permute-done.2 = bf16[1968,256]{1,0:T(8,128)(2,1)S(1)} collective-permute-done((bf16[1968,256]{1,0:T(8,128)(2,1)}, bf16[1968,256]{1,0:T(8,128)(2,1)S(1)}, u32[]{:S(2)}, u32[]{:S(2)}) %collective-permute-start.2) | collective-permute-done | bytes 1007648 | tf_op jit(solution)/shard_map/ppermute | solution.py:41
  32.0 1.8 collective-permute-start.3
  37.0 3.6 %shard_map.320 = (f32[256,512]{1,0:T(8,128)S(1)}, f32[256,512]{1,0:T(8,128)S(1)}, f32[16,512]{1,0:T(8,128)S(1)}, f32[16,512]{1,0:T(8,128)S(1)}, f32[16,128,128]{...) custom-call(s32[1]{0:T(128)} %bitcast.parity_ref, bf16[432,256]{1,0:T(8,128)(2,1)S(1)} %slice.36.misc_ref, ...), custom_call_target="tpu_custom_call" | custom-call | flops 4600000 | tf_op jit(solution)/shard_map/pallas_call | solution.py:663
  41.4 9.9 %collective-permute-done.3.refs_0_ = bf16[1536,256]{1,0:T(8,128)(2,1)S(1)} collective-permute-done((bf16[1536,256]{1,0:T(8,128)(2,1)S(1)}, bf16[1536,256]{1,0:T(8,128)(2,1)S(1)}, u32[]{:S(2)}, u32[]{:S(2)}) %collective-permute-start.3) | collective-permute-done | bytes 786464 | tf_op jit(solution)/shard_map/ppermute | solution.py:867
  53.7 6.6 %shard_map.322 = (f32[256,512]{1,0:T(8,128)S(1)}, bf16[256,512]{1,0:T(8,128)(2,1)S(1)}, bf16[2,256,768]{2,1,0:T(8,128)(2,1)S(1)}, bf16[2,4,512,128]{3,2,1,0:T(8,128)(2,1)S(1)}, bf16[256,512]{1,0:T(8,128)(2,1)S(1)}) custom-call(bf16[2,3,256,256]{3,2,1,0:T(8,128)(2,1)S(1)} %bitcast.87, bf16[2,256,256]{2,1,0:T(8,128)(2,1)S(1)} %copy-done.15, ...), custom_call_target="tpu_custom_call" | custom-call | flops 4600000 | tf_op jit(solution)/shard_map/pallas_call | solution.py:663
  63.6 3.7 %shard_map.323 = (f32[256,512]{1,0:T(8,128)S(1)}, bf16[256,512]{1,0:T(8,128)(2,1)S(1)}, bf16[256,2048]{1,0:T(8,128)(2,1)S(1)}, bf16[256,2048]{1,0:T(8,128)(2,1)S(1)}) custom-call(bf16[2,256,1024]{2,1,0:T(8,128)(2,1)S(1)} %copy-done.7, bf16[2,1024,256]{2,1,0:T(8,128)(2,1)S(1)} %copy-done.9, bf16[1536,256]{1,0:T(8,128)(2,1)S(1)} %slice.46.refs_2_.refs_9_, ...), custom_call_target="tpu_custom_call" | custom-call | flops 4600000 | tf_op jit(solution)/shard_map/pallas_call | solution.py:663
  68.1 3.5 %collective-permute-done.1.refs_0_ = bf16[1536,256]{1,0:T(8,128)(2,1)} collective-permute-done((bf16[1536,256]{1,0:T(8,128)(2,1)}, bf16[1536,256]{1,0:T(8,128)(2,1)}, u32[]{:S(2)}, u32[]{:S(2)}) %collective-permute-start.1) | collective-permute-done | bytes 786464 | tf_op jit(solution)/shard_map/ppermute | solution.py:867
  72.9 2.1 %collective-permute-done.9.refs_6_.refs_13_ = bf16[1536,256]{1,0:T(8,128)(2,1)} collective-permute-done((bf16[1536,256]{1,0:T(8,128)(2,1)}, bf16[1536,256]{1,0:T(8,128)(2,1)}, u32[]{:S(2)}, u32[]{:S(2)}) %collective-permute-start.9) | collective-permute-done | bytes 786464 | tf_op jit(solution)/shard_map/ppermute | solution.py:41
  78.5 5.1 %shard_map.325 = (f32[256,512]{1,0:T(8,128)S(1)}, bf16[256,512]{1,0:T(8,128)(2,1)S(1)}, bf16[2,256,768]{2,1,0:T(8,128)(2,1)S(1)}, bf16[2,4,512,128]{3,2,1,0:T(8,128)(2,1)S(1)}, bf16[256,512]{1,0:T(8,128)(2,1)S(1)}) custom-call(bf16[2,3,256,256]{3,2,1,0:T(8,128)(2,1)S(1)} %bitcast.88, bf16[2,256,256]{2,1,0:T(8,128)(2,1)S(1)} %copy-done.15, ...), custom_call_target="tpu_custom_call" | custom-call | flops 4600000 | tf_op jit(solution)/shard_map/pallas_call | solution.py:663
  83.8 13.9 %shard_map.326 = (bf16[196,256]{1,0:T(8,128)(2,1)}, bf16[2048,256]{1,0:T(8,128)(2,1)S(1)}, bf16[2048,256]{1,0:T(8,128)(2,1)S(1)}, f32[8,256]{1,0:T(8,128)S(1)}, ...) custom-call(bf16[2,256,1024]{2,1,0:T(8,128)(2,1)S(1)} %copy-done.8, ...), custom_call_target="tpu_custom_call" | custom-call | flops 13800000 | tf_op jit(solution)/shard_map/pallas_call | solution.py:663
  98.0 14.8 %shard_map.327 = (bf16[2048,256]{1,0:T(8,128)(2,1)S(1)}, bf16[2048,256]{1,0:T(8,128)(2,1)S(1)}, f32[8,256]{1,0:T(8,128)S(1)}, f32[8,256]{1,0:T(8,128)S(1)}, bf16...) custom-call(bf16[2,256,1024]{2,1,0:T(8,128)(2,1)S(1)} %copy-done.8, ...), custom_call_target="tpu_custom_call" | custom-call | flops 13800000 | tf_op jit(solution)/shard_map/pallas_call | solution.py:663
  117.4 1.7 collective-permute-start.44
  120.5 1.7 collective-permute-start.13
  124.0 1.6 collective-permute-start.45
  129.5 1.8 collective-permute-done.52
  137.7 2.0 collective-permute-start.47
  140.6 2.4 %collective-permute-start.16 = (bf16[200,256]{1,0:T(8,128)(2,1)S(1)}, bf16[200,256]{1,0:T(8,128)(2,1)S(1)}, u32[]{:S(2)}, u32[]{:S(2)}) collective-permute-start(bf16[200,256]{1,0:T(8,128)(2,1)S(1)} %get-tuple-element.158), channel_id=1, source_target_pairs={{0,8},{8,16},{16,24},{24,28},{28,20},{20,12},{12,4},{4,0},{1,9},{9... | collective-permute-start | bytes 307208 | tf_op jit(solution)/shard_map/ppermute | solution.py:800
  143.2 1.8 collective-permute-done.54
  145.4 1.6 collective-permute-start.55
  150.8 1.8 collective-permute-start.56
  160.6 2.0 collective-permute-start.26
  163.2 1.9 collective-permute-start.59
  168.8 2.1 %collective-permute-start.61 = (bf16[200,256]{1,0:T(8,128)(2,1)S(1)}, bf16[200,256]{1,0:T(8,128)(2,1)S(1)}, u32[]{:S(2)}, u32[]{:S(2)}) collective-permute-start(bf16[200,256]{1,0:T(8,128)(2,1)S(1)} %collective-permute-done.59.refs_20_), channel_id=1, source_target_pairs={{8,0},{16,8},{24,16},{28,24},{20,28},{12,20},{4,12},{0,4},{9,1},{1... | collective-permute-start | bytes 307208 | tf_op jit(solution)/shard_map/ppermute | solution.py:814
  174.1 1.9 collective-permute-start.63
  179.8 2.0 collective-permute-start.65
  185.0 1.9 collective-permute-start.67
  189.6 1.9 collective-permute-start.69
  194.3 1.9 collective-permute-start.71
  199.0 1.9 collective-permute-done.39.refs_15_
  201.5 3.9 %shard_map.330 = (f32[2,3,256,256]{3,2,1,0:T(8,128)}, f32[2,2,256]{2,1,0:T(2,128)}, f32[2,256,256]{2,1,0:T(8,128)}, f32[2,256]{1,0:T(2,128)}, f32[2,256,1024]{2,...) custom-call(s32[16]{0:T(128)S(1)} %stack.67.refs_0_, ...), custom_call_target="tpu_custom_call" | custom-call | flops 4600000 | tf_op jit(solution)/shard_map/pallas_call | solution.py:663
  (264 shorter events, 70.4 us)
Async XLA Ops:
  5.7 47.9 %collective-permute-start.5 = (bf16[6144,256]{1,0:T(8,128)(2,1)}, bf16[6144,256]{1,0:T(8,128)(2,1)S(1)}, u32[]{:S(2)}, u32[]{:S(2)}) collective-permute-start(bf16[6144,256]{1,0:T(8,128)(2,1)} %get-tuple-element.77), channel_id=1, source_target_pairs={{0,2},{2,0},{1,3},{3,1},{4,6},{6,4},{5,7},{7,5},{8,10},{10,8},{9,1... | collective-permute-start | bytes 9437192 | tf_op jit(solution)/shard_map/ppermute | solution.py:41
  6.2 25.7 %collective-permute-start.2 = (bf16[1968,256]{1,0:T(8,128)(2,1)}, bf16[1968,256]{1,0:T(8,128)(2,1)S(1)}, u32[]{:S(2)}, u32[]{:S(2)}) collective-permute-start(bf16[1968,256]{1,0:T(8,128)(2,1)} %get-tuple-element.75), channel_id=1, source_target_pairs={{0,1},{1,0},{2,3},{3,2},{4,5},{5,4},{6,7},{7,6},{8,9},{9,8},{10,11... | collective-permute-start | bytes 3022856 | tf_op jit(solution)/shard_map/ppermute | solution.py:41
  32.0 19.3 %collective-permute-start.3 = (bf16[1536,256]{1,0:T(8,128)(2,1)S(1)}, bf16[1536,256]{1,0:T(8,128)(2,1)S(1)}, u32[]{:S(2)}, u32[]{:S(2)}) collective-permute-start(bf16[1536,256]{1,0:T(8,128)(2,1)S(1)} %slice.46.refs_2_.refs_9_), channel_id=1, source_target_pairs={{0,4},{4,0},{8,12},{12,8},{16,20},{20,16},{24,28},{28,24},{1,5},{5... | collective-permute-start | bytes 2359304 | tf_op jit(solution)/shard_map/ppermute | solution.py:867
  33.8 19.1 %collective-permute-start = (bf16[1536,256]{1,0:T(8,128)(2,1)}, bf16[1536,256]{1,0:T(8,128)(2,1)}, u32[]{:S(2)}, u32[]{:S(2)}) collective-permute-start(bf16[1536,256]{1,0:T(8,128)(2,1)} %get-tuple-element.74._), channel_id=1, source_target_pairs={{0,1},{1,0},{2,3},{3,2},{4,5},{5,4},{6,7},{7,6},{8,9},{9,8},{10,11... | collective-permute-start | bytes 2359304 | tf_op jit(solution)/shard_map/ppermute | solution.py:41
  36.4 17.0 %collective-permute-start.6 = (bf16[1536,256]{1,0:T(8,128)(2,1)S(1)}, bf16[1536,256]{1,0:T(8,128)(2,1)S(1)}, u32[]{:S(2)}, u32[]{:S(2)}) collective-permute-start(bf16[1536,256]{1,0:T(8,128)(2,1)S(1)} %slice.46.refs_2_.refs_9_), channel_id=1, source_target_pairs={{0,2},{2,0},{1,3},{3,1},{4,6},{6,4},{5,7},{7,5},{8,10},{10,8},{9,1... | collective-permute-start | bytes 2359304 | tf_op jit(solution)/shard_map/ppermute | solution.py:41
  52.9 18.7 %collective-permute-start.1 = (bf16[1536,256]{1,0:T(8,128)(2,1)}, bf16[1536,256]{1,0:T(8,128)(2,1)}, u32[]{:S(2)}, u32[]{:S(2)}) collective-permute-start(bf16[1536,256]{1,0:T(8,128)(2,1)} %collective-permute-done.refs_11_.refs_2_.refs_9_), channel_id=1, source_target_pairs={{0,4},{4,0},{8,12},{12,8},{16,20},{20,16},{24,28},{28,24},{1,5},{5... | collective-permute-start | bytes 2359304 | tf_op jit(solution)/shard_map/ppermute | solution.py:867
  53.4 19.5 %collective-permute-start.8 = (bf16[1536,256]{1,0:T(8,128)(2,1)}, bf16[1536,256]{1,0:T(8,128)(2,1)}, u32[]{:S(2)}, u32[]{:S(2)}) collective-permute-start(bf16[1536,256]{1,0:T(8,128)(2,1)} %collective-permute-done.refs_11_.refs_2_.refs_9_), channel_id=1, source_target_pairs={{0,2},{2,0},{1,3},{3,1},{4,6},{6,4},{5,7},{7,5},{8,10},{10,8},{9,1... | collective-permute-start | bytes 2359304 | tf_op jit(solution)/shard_map/ppermute | solution.py:41
  97.7 19.0 %collective-permute-start.41 = (bf16[2048,256]{1,0:T(8,128)(2,1)S(1)}, bf16[2048,256]{1,0:T(8,128)(2,1)S(1)}, u32[]{:S(2)}, u32[]{:S(2)}) collective-permute-start(bf16[2048,256]{1,0:T(8,128)(2,1)S(1)} %get-tuple-element.113), channel_id=1, source_target_pairs={{0,2},{2,0},{1,3},{3,1},{4,6},{6,4},{5,7},{7,5},{8,10},{10,8},{9,1... | collective-permute-start | bytes 3145736 | tf_op jit(solution)/shard_map/ppermute | solution.py:41
  112.7 7.0 %collective-permute-start.10 = (bf16[2048,256]{1,0:T(8,128)(2,1)S(1)}, bf16[2048,256]{1,0:T(8,128)(2,1)S(1)}, u32[]{:S(2)}, u32[]{:S(2)}) collective-permute-start(bf16[2048,256]{1,0:T(8,128)(2,1)S(1)} %get-tuple-element.101), channel_id=1, source_target_pairs={{0,2},{2,0},{1,3},{3,1},{4,6},{6,4},{5,7},{7,5},{8,10},{10,8},{9,1... | collective-permute-start | bytes 3145736 | tf_op jit(solution)/shard_map/ppermute | solution.py:41
  120.5 5.6 %collective-permute-start.13 = (bf16[200,256]{1,0:T(8,128)(2,1)S(1)}, bf16[200,256]{1,0:T(8,128)(2,1)S(1)}, u32[]{:S(2)}, u32[]{:S(2)}) collective-permute-start(bf16[200,256]{1,0:T(8,128)(2,1)S(1)} %get-tuple-element.109), channel_id=1, source_target_pairs={{0,8},{8,16},{16,24},{24,28},{28,20},{20,12},{12,4},{4,0},{1,9},{9... | collective-permute-start | bytes 307208 | tf_op jit(solution)/shard_map/ppermute | solution.py:800
  124.0 5.5 %collective-permute-start.45 = (bf16[200,256]{1,0:T(8,128)(2,1)S(1)}, bf16[200,256]{1,0:T(8,128)(2,1)S(1)}, u32[]{:S(2)}, u32[]{:S(2)}) collective-permute-start(bf16[200,256]{1,0:T(8,128)(2,1)S(1)} %get-tuple-element.148), channel_id=1, source_target_pairs={{0,8},{8,16},{16,24},{24,28},{28,20},{20,12},{12,4},{4,0},{1,9},{9... | collective-permute-start | bytes 307208 | tf_op jit(solution)/shard_map/ppermute | solution.py:800
  125.6 5.7 %collective-permute-start.52 = (bf16[200,256]{1,0:T(8,128)(2,1)S(1)}, bf16[200,256]{1,0:T(8,128)(2,1)S(1)}, u32[]{:S(2)}, u32[]{:S(2)}) collective-permute-start(bf16[200,256]{1,0:T(8,128)(2,1)S(1)} %get-tuple-element.147), channel_id=1, source_target_pairs={{8,0},{16,8},{24,16},{28,24},{20,28},{12,20},{4,12},{0,4},{9,1},{1... | collective-permute-start | bytes 307208 | tf_op jit(solution)/shard_map/ppermute | solution.py:800
  127.1 6.3 %collective-permute-start.14 = (bf16[200,256]{1,0:T(8,128)(2,1)S(1)}, bf16[200,256]{1,0:T(8,128)(2,1)S(1)}, u32[]{:S(2)}, u32[]{:S(2)}) collective-permute-start(bf16[200,256]{1,0:T(8,128)(2,1)S(1)} %get-tuple-element.162), channel_id=1, source_target_pairs={{0,8},{8,16},{16,24},{24,28},{28,20},{20,12},{12,4},{4,0},{1,9},{9... | collective-permute-start | bytes 307208 | tf_op jit(solution)/shard_map/ppermute | solution.py:800
  128.7 5.5 %collective-permute-start.21 = (bf16[200,256]{1,0:T(8,128)(2,1)S(1)}, bf16[200,256]{1,0:T(8,128)(2,1)S(1)}, u32[]{:S(2)}, u32[]{:S(2)}) collective-permute-start(bf16[200,256]{1,0:T(8,128)(2,1)S(1)} %get-tuple-element.161), channel_id=1, source_target_pairs={{8,0},{16,8},{24,16},{28,24},{20,28},{12,20},{4,12},{0,4},{9,1},{1... | collective-permute-start | bytes 307208 | tf_op jit(solution)/shard_map/ppermute | solution.py:800
  134.3 5.5 %collective-permute-start.15 = (bf16[200,256]{1,0:T(8,128)(2,1)S(1)}, bf16[200,256]{1,0:T(8,128)(2,1)S(1)}, u32[]{:S(2)}, u32[]{:S(2)}) collective-permute-start(bf16[200,256]{1,0:T(8,128)(2,1)S(1)} %get-tuple-element.160), channel_id=1, source_target_pairs={{0,8},{8,16},{16,24},{24,28},{28,20},{20,12},{12,4},{4,0},{1,9},{9... | collective-permute-start | bytes 307208 | tf_op jit(solution)/shard_map/ppermute | solution.py:800
  137.7 5.5 %collective-permute-start.47 = (bf16[200,256]{1,0:T(8,128)(2,1)S(1)}, bf16[200,256]{1,0:T(8,128)(2,1)S(1)}, u32[]{:S(2)}, u32[]{:S(2)}) collective-permute-start(bf16[200,256]{1,0:T(8,128)(2,1)S(1)} %get-tuple-element.144), channel_id=1, source_target_pairs={{0,8},{8,16},{16,24},{24,28},{28,20},{20,12},{12,4},{4,0},{1,9},{9... | collective-permute-start | bytes 307208 | tf_op jit(solution)/shard_map/ppermute | solution.py:800
  140.6 6.5 %collective-permute-start.16 = (bf16[200,256]{1,0:T(8,128)(2,1)S(1)}, bf16[200,256]{1,0:T(8,128)(2,1)S(1)}, u32[]{:S(2)}, u32[]{:S(2)}) collective-permute-start(bf16[200,256]{1,0:T(8,128)(2,1)S(1)} %get-tuple-element.158), channel_id=1, source_target_pairs={{0,8},{8,16},{16,24},{24,28},{28,20},{20,12},{12,4},{4,0},{1,9},{9... | collective-permute-start | bytes 307208 | tf_op jit(solution)/shard_map/ppermute | solution.py:800
  147.7 5.6 %collective-permute-start.17 = (bf16[200,256]{1,0:T(8,128)(2,1)S(1)}, bf16[200,256]{1,0:T(8,128)(2,1)S(1)}, u32[]{:S(2)}, u32[]{:S(2)}) collective-permute-start(bf16[200,256]{1,0:T(8,128)(2,1)S(1)} %get-tuple-element.156), channel_id=1, source_target_pairs={{0,8},{8,16},{16,24},{24,28},{28,20},{20,12},{12,4},{4,0},{1,9},{9... | collective-permute-start | bytes 307208 | tf_op jit(solution)/shard_map/ppermute | solution.py:800
  148.7 5.7 %collective-permute-start.24 = (bf16[200,256]{1,0:T(8,128)(2,1)S(1)}, bf16[200,256]{1,0:T(8,128)(2,1)S(1)}, u32[]{:S(2)}, u32[]{:S(2)}) collective-permute-start(bf16[200,256]{1,0:T(8,128)(2,1)S(1)} %get-tuple-element.155), channel_id=1, source_target_pairs={{8,0},{16,8},{24,16},{28,24},{20,28},{12,20},{4,12},{0,4},{9,1},{1... | collective-permute-start | bytes 307208 | tf_op jit(solution)/shard_map/ppermute | solution.py:800
  150.3 6.1 %collective-permute-start.49 = (bf16[200,256]{1,0:T(8,128)(2,1)S(1)}, bf16[200,256]{1,0:T(8,128)(2,1)S(1)}, u32[]{:S(2)}, u32[]{:S(2)}) collective-permute-start(bf16[200,256]{1,0:T(8,128)(2,1)S(1)} %get-tuple-element.140), channel_id=1, source_target_pairs={{0,8},{8,16},{16,24},{24,28},{28,20},{20,12},{12,4},{4,0},{1,9},{9... | collective-permute-start | bytes 307208 | tf_op jit(solution)/shard_map/ppermute | solution.py:800
  150.8 5.7 %collective-permute-start.56 = (bf16[200,256]{1,0:T(8,128)(2,1)S(1)}, bf16[200,256]{1,0:T(8,128)(2,1)S(1)}, u32[]{:S(2)}, u32[]{:S(2)}) collective-permute-start(bf16[200,256]{1,0:T(8,128)(2,1)S(1)} %get-tuple-element.139), channel_id=1, source_target_pairs={{8,0},{16,8},{24,16},{28,24},{20,28},{12,20},{4,12},{0,4},{9,1},{1... | collective-permute-start | bytes 307208 | tf_op jit(solution)/shard_map/ppermute | solution.py:800
  155.1 5.4 %collective-permute-start.25 = (bf16[200,256]{1,0:T(8,128)(2,1)S(1)}, bf16[200,256]{1,0:T(8,128)(2,1)S(1)}, u32[]{:S(2)}, u32[]{:S(2)}) collective-permute-start(bf16[200,256]{1,0:T(8,128)(2,1)S(1)} %get-tuple-element.153), channel_id=1, source_target_pairs={{8,0},{16,8},{24,16},{28,24},{20,28},{12,20},{4,12},{0,4},{9,1},{1... | collective-permute-start | bytes 307208 | tf_op jit(solution)/shard_map/ppermute | solution.py:800
  156.5 6.1 %collective-permute-start.50 = (bf16[200,256]{1,0:T(8,128)(2,1)S(1)}, bf16[200,256]{1,0:T(8,128)(2,1)S(1)}, u32[]{:S(2)}, u32[]{:S(2)}) collective-permute-start(bf16[200,256]{1,0:T(8,128)(2,1)S(1)} %get-tuple-element.138), channel_id=1, source_target_pairs={{0,8},{8,16},{16,24},{24,28},{28,20},{20,12},{12,4},{4,0},{1,9},{9... | collective-permute-start | bytes 307208 | tf_op jit(solution)/shard_map/ppermute | solution.py:800
  157.2 5.8 %collective-permute-start.57 = (bf16[200,256]{1,0:T(8,128)(2,1)S(1)}, bf16[200,256]{1,0:T(8,128)(2,1)S(1)}, u32[]{:S(2)}, u32[]{:S(2)}) collective-permute-start(bf16[200,256]{1,0:T(8,128)(2,1)S(1)} %get-tuple-element.137), channel_id=1, source_target_pairs={{8,0},{16,8},{24,16},{28,24},{20,28},{12,20},{4,12},{0,4},{9,1},{1... | collective-permute-start | bytes 307208 | tf_op jit(solution)/shard_map/ppermute | solution.py:800
  163.1 5.7 %collective-permute-start.58 = (bf16[200,256]{1,0:T(8,128)(2,1)S(1)}, bf16[200,256]{1,0:T(8,128)(2,1)S(1)}, u32[]{:S(2)}, u32[]{:S(2)}) collective-permute-start(bf16[200,256]{1,0:T(8,128)(2,1)S(1)} %get-tuple-element.136.refs_17_), channel_id=1, source_target_pairs={{0,8},{8,16},{16,24},{24,28},{28,20},{20,12},{12,4},{4,0},{1,9},{9... | collective-permute-start | bytes 307208 | tf_op jit(solution)/shard_map/ppermute | solution.py:814
  163.2 5.5 %collective-permute-start.59 = (bf16[200,256]{1,0:T(8,128)(2,1)S(1)}, bf16[200,256]{1,0:T(8,128)(2,1)S(1)}, u32[]{:S(2)}, u32[]{:S(2)}) collective-permute-start(bf16[200,256]{1,0:T(8,128)(2,1)S(1)} %get-tuple-element.135.refs_18_), channel_id=1, source_target_pairs={{8,0},{16,8},{24,16},{28,24},{20,28},{12,20},{4,12},{0,4},{9,1},{1... | collective-permute-start | bytes 307208 | tf_op jit(solution)/shard_map/ppermute | solution.py:814
  166.3 5.8 %collective-permute-start.28 = (bf16[200,256]{1,0:T(8,128)(2,1)S(1)}, bf16[200,256]{1,0:T(8,128)(2,1)S(1)}, u32[]{:S(2)}, u32[]{:S(2)}) collective-permute-start(bf16[200,256]{1,0:T(8,128)(2,1)S(1)} %get-tuple-element.149.refs_2_), channel_id=1, source_target_pairs={{8,0},{16,8},{24,16},{28,24},{20,28},{12,20},{4,12},{0,4},{9,1},{1... | collective-permute-start | bytes 307208 | tf_op jit(solution)/shard_map/ppermute | solution.py:814
  168.8 5.3 %collective-permute-start.61 = (bf16[200,256]{1,0:T(8,128)(2,1)S(1)}, bf16[200,256]{1,0:T(8,128)(2,1)S(1)}, u32[]{:S(2)}, u32[]{:S(2)}) collective-permute-start(bf16[200,256]{1,0:T(8,128)(2,1)S(1)} %collective-permute-done.59.refs_20_), channel_id=1, source_target_pairs={{8,0},{16,8},{24,16},{28,24},{20,28},{12,20},{4,12},{0,4},{9,1},{1... | collective-permute-start | bytes 307208 | tf_op jit(solution)/shard_map/ppermute | solution.py:814
  174.0 5.8 %collective-permute-start.62 = (bf16[200,256]{1,0:T(8,128)(2,1)S(1)}, bf16[200,256]{1,0:T(8,128)(2,1)S(1)}, u32[]{:S(2)}, u32[]{:S(2)}) collective-permute-start(bf16[200,256]{1,0:T(8,128)(2,1)S(1)} %collective-permute-done.60.refs_21_), channel_id=1, source_target_pairs={{0,8},{8,16},{16,24},{24,28},{28,20},{20,12},{12,4},{4,0},{1,9},{9... | collective-permute-start | bytes 307208 | tf_op jit(solution)/shard_map/ppermute | solution.py:814
  174.1 5.7 %collective-permute-start.63 = (bf16[200,256]{1,0:T(8,128)(2,1)S(1)}, bf16[200,256]{1,0:T(8,128)(2,1)S(1)}, u32[]{:S(2)}, u32[]{:S(2)}) collective-permute-start(bf16[200,256]{1,0:T(8,128)(2,1)S(1)} %collective-permute-done.61.refs_22_), channel_id=1, source_target_pairs={{8,0},{16,8},{24,16},{28,24},{20,28},{12,20},{4,12},{0,4},{9,1},{1... | collective-permute-start | bytes 307208 | tf_op jit(solution)/shard_map/ppermute | solution.py:814
  176.2 5.7 %collective-permute-start.31 = (bf16[200,256]{1,0:T(8,128)(2,1)S(1)}, bf16[200,256]{1,0:T(8,128)(2,1)S(1)}, u32[]{:S(2)}, u32[]{:S(2)}) collective-permute-start(bf16[200,256]{1,0:T(8,128)(2,1)S(1)} %collective-permute-done.29.refs_5_), channel_id=1, source_target_pairs={{0,8},{8,16},{16,24},{24,28},{28,20},{20,12},{12,4},{4,0},{1,9},{9... | collective-permute-start | bytes 307208 | tf_op jit(solution)/shard_map/ppermute | solution.py:814
  177.2 5.6 %collective-permute-start.32 = (bf16[200,256]{1,0:T(8,128)(2,1)S(1)}, bf16[200,256]{1,0:T(8,128)(2,1)S(1)}, u32[]{:S(2)}, u32[]{:S(2)}) collective-permute-start(bf16[200,256]{1,0:T(8,128)(2,1)S(1)} %collective-permute-done.30.refs_6_), channel_id=1, source_target_pairs={{8,0},{16,8},{24,16},{28,24},{20,28},{12,20},{4,12},{0,4},{9,1},{1... | collective-permute-start | bytes 307208 | tf_op jit(solution)/shard_map/ppermute | solution.py:814
  (93 other events, 811.8 us)

commit v5 on v4

--- a/solution.py
+++ b/solution.py
@@ -538,7 +538,7 @@
     grad_input, grad_gain, grad_shift = norm_back(
         grad_normed, mid_ref[...], small_ref[GAIN_TWO : GAIN_TWO + 1]
     )
-    grad_mid_ref[...] = clear_padding(grad + grad_input)
+    grad_mid_ref[...] = grad + grad_input
     down_bias = jnp.sum(near.astype(F32), 0, keepdims=True)
     for small in small_outs:
         small[0:1, :] = down_bias
@@ -599,7 +599,7 @@
     grad_input, grad_gain, grad_shift = norm_back(
         grad_normed, x_ref[...], small_ref[GAIN_ONE : GAIN_ONE + 1]
     )
-    total = clear_padding(grad_mid + grad_input)
+    total = grad_mid + grad_input
     scratch[...] = total
     if layer % 2 == 1:
         unroll_rows(scratch, grad_ref)

time: 210 us -> 210 us (level)
  no operation moved by 1% of the time
where the time goes in v5:
time: 210 us; the launch traced here: 206 us
  starting transfers between devices  67.6 us (32%)
  waiting for transfers between devices  64.9 us (31%)
  Pallas kernels  58.2 us (28%)
  local copies, waits for them, and re-layouts  10.5 us (5%)
  matrix products  2.18 us (1%)
    pallas_call x13, Pallas kernels, call(): pl.pallas_call(kernel, out_shape=[jax.ShapeDtypeStruct(shape, kind) for s...  58.2 us
    ppermute x28, starting transfers between devices, ring_sum(): one, two = (lax.ppermute(one, 'dp', onward), lax.ppermute(two, 'dp', back))  29.8 us
    ppermute x28, starting transfers between devices, ring_gather(): one, two = (lax.ppermute(one, 'dp', onward), lax.ppermute(two, 'dp', back))  28.4 us
    ppermute x14, waiting for transfers between devices, swap(): return lax.ppermute(values, axis, [(0, 1), (1, 0)])  27 us
    ppermute x28, waiting for transfers between devices, ring_sum(): one, two = (lax.ppermute(one, 'dp', onward), lax.ppermute(two, 'dp', back))  15.3 us
    ppermute x2, waiting for transfers between devices, block(): from_dp = lax.ppermute(pack, 'dp', neighbours)  13.5 us
    ppermute x28, waiting for transfers between devices, ring_gather(): one, two = (lax.ppermute(one, 'dp', onward), lax.ppermute(two, 'dp', back))  9.21 us
    unnamed x106, local copies, waits for them, and re-layouts  9.15 us
  transfers between devices with their start and end apart: 72, of which 44 were waited for; matrix products, arithmetic and copies ran while one was open for 2% of the time, Pallas kernels for 15%

profile of v5, /device:TPU:0, one launch (start us, length us, event | category | flops | bytes accessed | tf_op | source)
XLA Modules:
  0.0 205.8 jit_solution(11098056516504289921)
XLA Ops:
  0.7 5.0 %shard_map.318 = (bf16[1968,256]{1,0:T(8,128)(2,1)}, bf16[1536,256]{1,0:T(8,128)(2,1)}, bf16[6144,256]{1,0:T(8,128)(2,1)}) custom-call(s32[1]{0:T(128)} %bitcast.parity_ref, bf16[2,3,256,256]{3,2,1,0:T(8,128)(2,1)} %bitcast.86, bf16[2,256,256]{2,1,0:T(8,128)(2,1)} %refs_8_.3, bf16[2,256,1024]{2,1,0:T(8,128)(2,1)} %refs_0_.5, bf16[2,1024,256]{2,1,0:T(8,128)(2,1)} %refs_1_.9, ...), custom_call_target="tpu_custom_call" | custom-call | flops 3450000 | tf_op jit(solution)/shard_map/pallas_call | solution.py:663
  6.2 2.6 %collective-permute-start.2 = (bf16[1968,256]{1,0:T(8,128)(2,1)}, bf16[1968,256]{1,0:T(8,128)(2,1)S(1)}, u32[]{:S(2)}, u32[]{:S(2)}) collective-permute-start(bf16[1968,256]{1,0:T(8,128)(2,1)} %get-tuple-element.75), channel_id=1, source_target_pairs={{0,1},{1,0},{2,3},{3,2},{4,5},{5,4},{6,7},{7,6},{8,9},{9,8},{10,11... | collective-permute-start | bytes 3022856 | tf_op jit(solution)/shard_map/ppermute | solution.py:41
  8.8 23.1 %collective-permute-done.2 = bf16[1968,256]{1,0:T(8,128)(2,1)S(1)} collective-permute-done((bf16[1968,256]{1,0:T(8,128)(2,1)}, bf16[1968,256]{1,0:T(8,128)(2,1)S(1)}, u32[]{:S(2)}, u32[]{:S(2)}) %collective-permute-start.2) | collective-permute-done | bytes 1007648 | tf_op jit(solution)/shard_map/ppermute | solution.py:41
  32.0 1.8 collective-permute-start.3
  37.0 3.6 %shard_map.320 = (f32[256,512]{1,0:T(8,128)S(1)}, f32[256,512]{1,0:T(8,128)S(1)}, f32[16,512]{1,0:T(8,128)S(1)}, f32[16,512]{1,0:T(8,128)S(1)}, f32[16,128,128]{...) custom-call(s32[1]{0:T(128)} %bitcast.parity_ref, bf16[432,256]{1,0:T(8,128)(2,1)S(1)} %slice.36.misc_ref, ...), custom_call_target="tpu_custom_call" | custom-call | flops 4600000 | tf_op jit(solution)/shard_map/pallas_call | solution.py:663
  41.4 9.9 %collective-permute-done.3.refs_0_ = bf16[1536,256]{1,0:T(8,128)(2,1)S(1)} collective-permute-done((bf16[1536,256]{1,0:T(8,128)(2,1)S(1)}, bf16[1536,256]{1,0:T(8,128)(2,1)S(1)}, u32[]{:S(2)}, u32[]{:S(2)}) %collective-permute-start.3) | collective-permute-done | bytes 786464 | tf_op jit(solution)/shard_map/ppermute | solution.py:867
  53.7 6.6 %shard_map.322 = (f32[256,512]{1,0:T(8,128)S(1)}, bf16[256,512]{1,0:T(8,128)(2,1)S(1)}, bf16[2,256,768]{2,1,0:T(8,128)(2,1)S(1)}, bf16[2,4,512,128]{3,2,1,0:T(8,128)(2,1)S(1)}, bf16[256,512]{1,0:T(8,128)(2,1)S(1)}) custom-call(bf16[2,3,256,256]{3,2,1,0:T(8,128)(2,1)S(1)} %bitcast.87, bf16[2,256,256]{2,1,0:T(8,128)(2,1)S(1)} %copy-done.15, ...), custom_call_target="tpu_custom_call" | custom-call | flops 4600000 | tf_op jit(solution)/shard_map/pallas_call | solution.py:663
  63.6 3.7 %shard_map.323 = (f32[256,512]{1,0:T(8,128)S(1)}, bf16[256,512]{1,0:T(8,128)(2,1)S(1)}, bf16[256,2048]{1,0:T(8,128)(2,1)S(1)}, bf16[256,2048]{1,0:T(8,128)(2,1)S(1)}) custom-call(bf16[2,256,1024]{2,1,0:T(8,128)(2,1)S(1)} %copy-done.7, bf16[2,1024,256]{2,1,0:T(8,128)(2,1)S(1)} %copy-done.9, bf16[1536,256]{1,0:T(8,128)(2,1)S(1)} %slice.46.refs_2_.refs_9_, ...), custom_call_target="tpu_custom_call" | custom-call | flops 4600000 | tf_op jit(solution)/shard_map/pallas_call | solution.py:663
  68.1 3.5 %collective-permute-done.1.refs_0_ = bf16[1536,256]{1,0:T(8,128)(2,1)} collective-permute-done((bf16[1536,256]{1,0:T(8,128)(2,1)}, bf16[1536,256]{1,0:T(8,128)(2,1)}, u32[]{:S(2)}, u32[]{:S(2)}) %collective-permute-start.1) | collective-permute-done | bytes 786464 | tf_op jit(solution)/shard_map/ppermute | solution.py:867
  72.9 2.1 %collective-permute-done.9.refs_6_.refs_13_ = bf16[1536,256]{1,0:T(8,128)(2,1)} collective-permute-done((bf16[1536,256]{1,0:T(8,128)(2,1)}, bf16[1536,256]{1,0:T(8,128)(2,1)}, u32[]{:S(2)}, u32[]{:S(2)}) %collective-permute-start.9) | collective-permute-done | bytes 786464 | tf_op jit(solution)/shard_map/ppermute | solution.py:41
  78.5 5.1 %shard_map.325 = (f32[256,512]{1,0:T(8,128)S(1)}, bf16[256,512]{1,0:T(8,128)(2,1)S(1)}, bf16[2,256,768]{2,1,0:T(8,128)(2,1)S(1)}, bf16[2,4,512,128]{3,2,1,0:T(8,128)(2,1)S(1)}, bf16[256,512]{1,0:T(8,128)(2,1)S(1)}) custom-call(bf16[2,3,256,256]{3,2,1,0:T(8,128)(2,1)S(1)} %bitcast.88, bf16[2,256,256]{2,1,0:T(8,128)(2,1)S(1)} %copy-done.15, ...), custom_call_target="tpu_custom_call" | custom-call | flops 4600000 | tf_op jit(solution)/shard_map/pallas_call | solution.py:663
  83.8 14.2 %shard_map.326 = (bf16[196,256]{1,0:T(8,128)(2,1)}, bf16[2048,256]{1,0:T(8,128)(2,1)S(1)}, bf16[2048,256]{1,0:T(8,128)(2,1)S(1)}, f32[8,256]{1,0:T(8,128)S(1)}, ...) custom-call(bf16[2,256,1024]{2,1,0:T(8,128)(2,1)S(1)} %copy-done.8, ...), custom_call_target="tpu_custom_call" | custom-call | flops 13800000 | tf_op jit(solution)/shard_map/pallas_call | solution.py:663
  98.3 14.6 %shard_map.327 = (bf16[2048,256]{1,0:T(8,128)(2,1)S(1)}, bf16[2048,256]{1,0:T(8,128)(2,1)S(1)}, f32[8,256]{1,0:T(8,128)S(1)}, f32[8,256]{1,0:T(8,128)S(1)}, bf16...) custom-call(bf16[2,256,1024]{2,1,0:T(8,128)(2,1)S(1)} %copy-done.8, ...), custom_call_target="tpu_custom_call" | custom-call | flops 13800000 | tf_op jit(solution)/shard_map/pallas_call | solution.py:663
  117.6 1.7 collective-permute-start.44
  120.7 1.7 collective-permute-start.13
  129.7 1.8 collective-permute-done.52
  137.9 2.0 collective-permute-start.47
  140.7 2.4 %collective-permute-start.16 = (bf16[200,256]{1,0:T(8,128)(2,1)S(1)}, bf16[200,256]{1,0:T(8,128)(2,1)S(1)}, u32[]{:S(2)}, u32[]{:S(2)}) collective-permute-start(bf16[200,256]{1,0:T(8,128)(2,1)S(1)} %get-tuple-element.158), channel_id=1, source_target_pairs={{0,8},{8,16},{16,24},{24,28},{28,20},{20,12},{12,4},{4,0},{1,9},{9... | collective-permute-start | bytes 307208 | tf_op jit(solution)/shard_map/ppermute | solution.py:800
  143.3 1.8 collective-permute-done.54
  145.6 1.6 collective-permute-start.55
  151.0 1.8 collective-permute-start.56
  160.8 2.0 collective-permute-start.26
  163.4 1.9 collective-permute-start.59
  166.4 1.6 collective-permute-start.28
  169.0 2.1 %collective-permute-start.61 = (bf16[200,256]{1,0:T(8,128)(2,1)S(1)}, bf16[200,256]{1,0:T(8,128)(2,1)S(1)}, u32[]{:S(2)}, u32[]{:S(2)}) collective-permute-start(bf16[200,256]{1,0:T(8,128)(2,1)S(1)} %collective-permute-done.59.refs_20_), channel_id=1, source_target_pairs={{8,0},{16,8},{24,16},{28,24},{20,28},{12,20},{4,12},{0,4},{9,1},{1... | collective-permute-start | bytes 307208 | tf_op jit(solution)/shard_map/ppermute | solution.py:814
  174.2 2.0 collective-permute-start.63
  180.0 2.0 collective-permute-start.65
  185.1 1.8 collective-permute-start.67
  189.8 1.8 collective-permute-start.69
  194.4 1.8 collective-permute-start.71
  199.1 1.9 collective-permute-done.39.refs_15_
  201.6 3.9 %shard_map.330 = (f32[2,3,256,256]{3,2,1,0:T(8,128)}, f32[2,2,256]{2,1,0:T(2,128)}, f32[2,256,256]{2,1,0:T(8,128)}, f32[2,256]{1,0:T(2,128)}, f32[2,256,1024]{2,...) custom-call(s32[16]{0:T(128)S(1)} %stack.67.refs_0_, ...), custom_call_target="tpu_custom_call" | custom-call | flops 4600000 | tf_op jit(solution)/shard_map/pallas_call | solution.py:663
  (264 shorter events, 70.7 us)
Async XLA Ops:
  5.7 47.9 %collective-permute-start.5 = (bf16[6144,256]{1,0:T(8,128)(2,1)}, bf16[6144,256]{1,0:T(8,128)(2,1)S(1)}, u32[]{:S(2)}, u32[]{:S(2)}) collective-permute-start(bf16[6144,256]{1,0:T(8,128)(2,1)} %get-tuple-element.77), channel_id=1, source_target_pairs={{0,2},{2,0},{1,3},{3,1},{4,6},{6,4},{5,7},{7,5},{8,10},{10,8},{9,1... | collective-permute-start | bytes 9437192 | tf_op jit(solution)/shard_map/ppermute | solution.py:41
  6.2 25.7 %collective-permute-start.2 = (bf16[1968,256]{1,0:T(8,128)(2,1)}, bf16[1968,256]{1,0:T(8,128)(2,1)S(1)}, u32[]{:S(2)}, u32[]{:S(2)}) collective-permute-start(bf16[1968,256]{1,0:T(8,128)(2,1)} %get-tuple-element.75), channel_id=1, source_target_pairs={{0,1},{1,0},{2,3},{3,2},{4,5},{5,4},{6,7},{7,6},{8,9},{9,8},{10,11... | collective-permute-start | bytes 3022856 | tf_op jit(solution)/shard_map/ppermute | solution.py:41
  32.0 19.3 %collective-permute-start.3 = (bf16[1536,256]{1,0:T(8,128)(2,1)S(1)}, bf16[1536,256]{1,0:T(8,128)(2,1)S(1)}, u32[]{:S(2)}, u32[]{:S(2)}) collective-permute-start(bf16[1536,256]{1,0:T(8,128)(2,1)S(1)} %slice.46.refs_2_.refs_9_), channel_id=1, source_target_pairs={{0,4},{4,0},{8,12},{12,8},{16,20},{20,16},{24,28},{28,24},{1,5},{5... | collective-permute-start | bytes 2359304 | tf_op jit(solution)/shard_map/ppermute | solution.py:867
  33.8 19.1 %collective-permute-start = (bf16[1536,256]{1,0:T(8,128)(2,1)}, bf16[1536,256]{1,0:T(8,128)(2,1)}, u32[]{:S(2)}, u32[]{:S(2)}) collective-permute-start(bf16[1536,256]{1,0:T(8,128)(2,1)} %get-tuple-element.74._), channel_id=1, source_target_pairs={{0,1},{1,0},{2,3},{3,2},{4,5},{5,4},{6,7},{7,6},{8,9},{9,8},{10,11... | collective-permute-start | bytes 2359304 | tf_op jit(solution)/shard_map/ppermute | solution.py:41
  36.4 17.0 %collective-permute-start.6 = (bf16[1536,256]{1,0:T(8,128)(2,1)S(1)}, bf16[1536,256]{1,0:T(8,128)(2,1)S(1)}, u32[]{:S(2)}, u32[]{:S(2)}) collective-permute-start(bf16[1536,256]{1,0:T(8,128)(2,1)S(1)} %slice.46.refs_2_.refs_9_), channel_id=1, source_target_pairs={{0,2},{2,0},{1,3},{3,1},{4,6},{6,4},{5,7},{7,5},{8,10},{10,8},{9,1... | collective-permute-start | bytes 2359304 | tf_op jit(solution)/shard_map/ppermute | solution.py:41
  52.9 18.7 %collective-permute-start.1 = (bf16[1536,256]{1,0:T(8,128)(2,1)}, bf16[1536,256]{1,0:T(8,128)(2,1)}, u32[]{:S(2)}, u32[]{:S(2)}) collective-permute-start(bf16[1536,256]{1,0:T(8,128)(2,1)} %collective-permute-done.refs_11_.refs_2_.refs_9_), channel_id=1, source_target_pairs={{0,4},{4,0},{8,12},{12,8},{16,20},{20,16},{24,28},{28,24},{1,5},{5... | collective-permute-start | bytes 2359304 | tf_op jit(solution)/shard_map/ppermute | solution.py:867
  53.4 19.5 %collective-permute-start.8 = (bf16[1536,256]{1,0:T(8,128)(2,1)}, bf16[1536,256]{1,0:T(8,128)(2,1)}, u32[]{:S(2)}, u32[]{:S(2)}) collective-permute-start(bf16[1536,256]{1,0:T(8,128)(2,1)} %collective-permute-done.refs_11_.refs_2_.refs_9_), channel_id=1, source_target_pairs={{0,2},{2,0},{1,3},{3,1},{4,6},{6,4},{5,7},{7,5},{8,10},{10,8},{9,1... | collective-permute-start | bytes 2359304 | tf_op jit(solution)/shard_map/ppermute | solution.py:41
  98.0 18.8 %collective-permute-start.41 = (bf16[2048,256]{1,0:T(8,128)(2,1)S(1)}, bf16[2048,256]{1,0:T(8,128)(2,1)S(1)}, u32[]{:S(2)}, u32[]{:S(2)}) collective-permute-start(bf16[2048,256]{1,0:T(8,128)(2,1)S(1)} %get-tuple-element.113), channel_id=1, source_target_pairs={{0,2},{2,0},{1,3},{3,1},{4,6},{6,4},{5,7},{7,5},{8,10},{10,8},{9,1... | collective-permute-start | bytes 3145736 | tf_op jit(solution)/shard_map/ppermute | solution.py:41
  112.9 7.0 %collective-permute-start.10 = (bf16[2048,256]{1,0:T(8,128)(2,1)S(1)}, bf16[2048,256]{1,0:T(8,128)(2,1)S(1)}, u32[]{:S(2)}, u32[]{:S(2)}) collective-permute-start(bf16[2048,256]{1,0:T(8,128)(2,1)S(1)} %get-tuple-element.101), channel_id=1, source_target_pairs={{0,2},{2,0},{1,3},{3,1},{4,6},{6,4},{5,7},{7,5},{8,10},{10,8},{9,1... | collective-permute-start | bytes 3145736 | tf_op jit(solution)/shard_map/ppermute | solution.py:41
  120.7 5.6 %collective-permute-start.13 = (bf16[200,256]{1,0:T(8,128)(2,1)S(1)}, bf16[200,256]{1,0:T(8,128)(2,1)S(1)}, u32[]{:S(2)}, u32[]{:S(2)}) collective-permute-start(bf16[200,256]{1,0:T(8,128)(2,1)S(1)} %get-tuple-element.109), channel_id=1, source_target_pairs={{0,8},{8,16},{16,24},{24,28},{28,20},{20,12},{12,4},{4,0},{1,9},{9... | collective-permute-start | bytes 307208 | tf_op jit(solution)/shard_map/ppermute | solution.py:800
  124.2 5.5 %collective-permute-start.45 = (bf16[200,256]{1,0:T(8,128)(2,1)S(1)}, bf16[200,256]{1,0:T(8,128)(2,1)S(1)}, u32[]{:S(2)}, u32[]{:S(2)}) collective-permute-start(bf16[200,256]{1,0:T(8,128)(2,1)S(1)} %get-tuple-element.148), channel_id=1, source_target_pairs={{0,8},{8,16},{16,24},{24,28},{28,20},{20,12},{12,4},{4,0},{1,9},{9... | collective-permute-start | bytes 307208 | tf_op jit(solution)/shard_map/ppermute | solution.py:800
  125.8 5.7 %collective-permute-start.52 = (bf16[200,256]{1,0:T(8,128)(2,1)S(1)}, bf16[200,256]{1,0:T(8,128)(2,1)S(1)}, u32[]{:S(2)}, u32[]{:S(2)}) collective-permute-start(bf16[200,256]{1,0:T(8,128)(2,1)S(1)} %get-tuple-element.147), channel_id=1, source_target_pairs={{8,0},{16,8},{24,16},{28,24},{20,28},{12,20},{4,12},{0,4},{9,1},{1... | collective-permute-start | bytes 307208 | tf_op jit(solution)/shard_map/ppermute | solution.py:800
  127.3 6.3 %collective-permute-start.14 = (bf16[200,256]{1,0:T(8,128)(2,1)S(1)}, bf16[200,256]{1,0:T(8,128)(2,1)S(1)}, u32[]{:S(2)}, u32[]{:S(2)}) collective-permute-start(bf16[200,256]{1,0:T(8,128)(2,1)S(1)} %get-tuple-element.162), channel_id=1, source_target_pairs={{0,8},{8,16},{16,24},{24,28},{28,20},{20,12},{12,4},{4,0},{1,9},{9... | collective-permute-start | bytes 307208 | tf_op jit(solution)/shard_map/ppermute | solution.py:800
  128.9 5.5 %collective-permute-start.21 = (bf16[200,256]{1,0:T(8,128)(2,1)S(1)}, bf16[200,256]{1,0:T(8,128)(2,1)S(1)}, u32[]{:S(2)}, u32[]{:S(2)}) collective-permute-start(bf16[200,256]{1,0:T(8,128)(2,1)S(1)} %get-tuple-element.161), channel_id=1, source_target_pairs={{8,0},{16,8},{24,16},{28,24},{20,28},{12,20},{4,12},{0,4},{9,1},{1... | collective-permute-start | bytes 307208 | tf_op jit(solution)/shard_map/ppermute | solution.py:800
  134.4 5.5 %collective-permute-start.15 = (bf16[200,256]{1,0:T(8,128)(2,1)S(1)}, bf16[200,256]{1,0:T(8,128)(2,1)S(1)}, u32[]{:S(2)}, u32[]{:S(2)}) collective-permute-start(bf16[200,256]{1,0:T(8,128)(2,1)S(1)} %get-tuple-element.160), channel_id=1, source_target_pairs={{0,8},{8,16},{16,24},{24,28},{28,20},{20,12},{12,4},{4,0},{1,9},{9... | collective-permute-start | bytes 307208 | tf_op jit(solution)/shard_map/ppermute | solution.py:800
  137.9 5.5 %collective-permute-start.47 = (bf16[200,256]{1,0:T(8,128)(2,1)S(1)}, bf16[200,256]{1,0:T(8,128)(2,1)S(1)}, u32[]{:S(2)}, u32[]{:S(2)}) collective-permute-start(bf16[200,256]{1,0:T(8,128)(2,1)S(1)} %get-tuple-element.144), channel_id=1, source_target_pairs={{0,8},{8,16},{16,24},{24,28},{28,20},{20,12},{12,4},{4,0},{1,9},{9... | collective-permute-start | bytes 307208 | tf_op jit(solution)/shard_map/ppermute | solution.py:800
  140.7 6.5 %collective-permute-start.16 = (bf16[200,256]{1,0:T(8,128)(2,1)S(1)}, bf16[200,256]{1,0:T(8,128)(2,1)S(1)}, u32[]{:S(2)}, u32[]{:S(2)}) collective-permute-start(bf16[200,256]{1,0:T(8,128)(2,1)S(1)} %get-tuple-element.158), channel_id=1, source_target_pairs={{0,8},{8,16},{16,24},{24,28},{28,20},{20,12},{12,4},{4,0},{1,9},{9... | collective-permute-start | bytes 307208 | tf_op jit(solution)/shard_map/ppermute | solution.py:800
  147.9 5.6 %collective-permute-start.17 = (bf16[200,256]{1,0:T(8,128)(2,1)S(1)}, bf16[200,256]{1,0:T(8,128)(2,1)S(1)}, u32[]{:S(2)}, u32[]{:S(2)}) collective-permute-start(bf16[200,256]{1,0:T(8,128)(2,1)S(1)} %get-tuple-element.156), channel_id=1, source_target_pairs={{0,8},{8,16},{16,24},{24,28},{28,20},{20,12},{12,4},{4,0},{1,9},{9... | collective-permute-start | bytes 307208 | tf_op jit(solution)/shard_map/ppermute | solution.py:800
  148.9 5.6 %collective-permute-start.24 = (bf16[200,256]{1,0:T(8,128)(2,1)S(1)}, bf16[200,256]{1,0:T(8,128)(2,1)S(1)}, u32[]{:S(2)}, u32[]{:S(2)}) collective-permute-start(bf16[200,256]{1,0:T(8,128)(2,1)S(1)} %get-tuple-element.155), channel_id=1, source_target_pairs={{8,0},{16,8},{24,16},{28,24},{20,28},{12,20},{4,12},{0,4},{9,1},{1... | collective-permute-start | bytes 307208 | tf_op jit(solution)/shard_map/ppermute | solution.py:800
  150.5 6.1 %collective-permute-start.49 = (bf16[200,256]{1,0:T(8,128)(2,1)S(1)}, bf16[200,256]{1,0:T(8,128)(2,1)S(1)}, u32[]{:S(2)}, u32[]{:S(2)}) collective-permute-start(bf16[200,256]{1,0:T(8,128)(2,1)S(1)} %get-tuple-element.140), channel_id=1, source_target_pairs={{0,8},{8,16},{16,24},{24,28},{28,20},{20,12},{12,4},{4,0},{1,9},{9... | collective-permute-start | bytes 307208 | tf_op jit(solution)/shard_map/ppermute | solution.py:800
  151.0 5.6 %collective-permute-start.56 = (bf16[200,256]{1,0:T(8,128)(2,1)S(1)}, bf16[200,256]{1,0:T(8,128)(2,1)S(1)}, u32[]{:S(2)}, u32[]{:S(2)}) collective-permute-start(bf16[200,256]{1,0:T(8,128)(2,1)S(1)} %get-tuple-element.139), channel_id=1, source_target_pairs={{8,0},{16,8},{24,16},{28,24},{20,28},{12,20},{4,12},{0,4},{9,1},{1... | collective-permute-start | bytes 307208 | tf_op jit(solution)/shard_map/ppermute | solution.py:800
  155.3 5.4 %collective-permute-start.25 = (bf16[200,256]{1,0:T(8,128)(2,1)S(1)}, bf16[200,256]{1,0:T(8,128)(2,1)S(1)}, u32[]{:S(2)}, u32[]{:S(2)}) collective-permute-start(bf16[200,256]{1,0:T(8,128)(2,1)S(1)} %get-tuple-element.153), channel_id=1, source_target_pairs={{8,0},{16,8},{24,16},{28,24},{20,28},{12,20},{4,12},{0,4},{9,1},{1... | collective-permute-start | bytes 307208 | tf_op jit(solution)/shard_map/ppermute | solution.py:800
  156.6 6.2 %collective-permute-start.50 = (bf16[200,256]{1,0:T(8,128)(2,1)S(1)}, bf16[200,256]{1,0:T(8,128)(2,1)S(1)}, u32[]{:S(2)}, u32[]{:S(2)}) collective-permute-start(bf16[200,256]{1,0:T(8,128)(2,1)S(1)} %get-tuple-element.138), channel_id=1, source_target_pairs={{0,8},{8,16},{16,24},{24,28},{28,20},{20,12},{12,4},{4,0},{1,9},{9... | collective-permute-start | bytes 307208 | tf_op jit(solution)/shard_map/ppermute | solution.py:800
  157.4 5.8 %collective-permute-start.57 = (bf16[200,256]{1,0:T(8,128)(2,1)S(1)}, bf16[200,256]{1,0:T(8,128)(2,1)S(1)}, u32[]{:S(2)}, u32[]{:S(2)}) collective-permute-start(bf16[200,256]{1,0:T(8,128)(2,1)S(1)} %get-tuple-element.137), channel_id=1, source_target_pairs={{8,0},{16,8},{24,16},{28,24},{20,28},{12,20},{4,12},{0,4},{9,1},{1... | collective-permute-start | bytes 307208 | tf_op jit(solution)/shard_map/ppermute | solution.py:800
  163.2 5.7 %collective-permute-start.58 = (bf16[200,256]{1,0:T(8,128)(2,1)S(1)}, bf16[200,256]{1,0:T(8,128)(2,1)S(1)}, u32[]{:S(2)}, u32[]{:S(2)}) collective-permute-start(bf16[200,256]{1,0:T(8,128)(2,1)S(1)} %get-tuple-element.136.refs_17_), channel_id=1, source_target_pairs={{0,8},{8,16},{16,24},{24,28},{28,20},{20,12},{12,4},{4,0},{1,9},{9... | collective-permute-start | bytes 307208 | tf_op jit(solution)/shard_map/ppermute | solution.py:814
  163.4 5.5 %collective-permute-start.59 = (bf16[200,256]{1,0:T(8,128)(2,1)S(1)}, bf16[200,256]{1,0:T(8,128)(2,1)S(1)}, u32[]{:S(2)}, u32[]{:S(2)}) collective-permute-start(bf16[200,256]{1,0:T(8,128)(2,1)S(1)} %get-tuple-element.135.refs_18_), channel_id=1, source_target_pairs={{8,0},{16,8},{24,16},{28,24},{20,28},{12,20},{4,12},{0,4},{9,1},{1... | collective-permute-start | bytes 307208 | tf_op jit(solution)/shard_map/ppermute | solution.py:814
  166.0 5.3 %collective-permute-start.27 = (bf16[200,256]{1,0:T(8,128)(2,1)S(1)}, bf16[200,256]{1,0:T(8,128)(2,1)S(1)}, u32[]{:S(2)}, u32[]{:S(2)}) collective-permute-start(bf16[200,256]{1,0:T(8,128)(2,1)S(1)} %get-tuple-element.150.refs_1_), channel_id=1, source_target_pairs={{0,8},{8,16},{16,24},{24,28},{28,20},{20,12},{12,4},{4,0},{1,9},{9... | collective-permute-start | bytes 307208 | tf_op jit(solution)/shard_map/ppermute | solution.py:814
  166.4 5.8 %collective-permute-start.28 = (bf16[200,256]{1,0:T(8,128)(2,1)S(1)}, bf16[200,256]{1,0:T(8,128)(2,1)S(1)}, u32[]{:S(2)}, u32[]{:S(2)}) collective-permute-start(bf16[200,256]{1,0:T(8,128)(2,1)S(1)} %get-tuple-element.149.refs_2_), channel_id=1, source_target_pairs={{8,0},{16,8},{24,16},{28,24},{20,28},{12,20},{4,12},{0,4},{9,1},{1... | collective-permute-start | bytes 307208 | tf_op jit(solution)/shard_map/ppermute | solution.py:814
  174.2 5.8 %collective-permute-start.62 = (bf16[200,256]{1,0:T(8,128)(2,1)S(1)}, bf16[200,256]{1,0:T(8,128)(2,1)S(1)}, u32[]{:S(2)}, u32[]{:S(2)}) collective-permute-start(bf16[200,256]{1,0:T(8,128)(2,1)S(1)} %collective-permute-done.60.refs_21_), channel_id=1, source_target_pairs={{0,8},{8,16},{16,24},{24,28},{28,20},{20,12},{12,4},{4,0},{1,9},{9... | collective-permute-start | bytes 307208 | tf_op jit(solution)/shard_map/ppermute | solution.py:814
  174.2 5.8 %collective-permute-start.63 = (bf16[200,256]{1,0:T(8,128)(2,1)S(1)}, bf16[200,256]{1,0:T(8,128)(2,1)S(1)}, u32[]{:S(2)}, u32[]{:S(2)}) collective-permute-start(bf16[200,256]{1,0:T(8,128)(2,1)S(1)} %collective-permute-done.61.refs_22_), channel_id=1, source_target_pairs={{8,0},{16,8},{24,16},{28,24},{20,28},{12,20},{4,12},{0,4},{9,1},{1... | collective-permute-start | bytes 307208 | tf_op jit(solution)/shard_map/ppermute | solution.py:814
  176.3 5.8 %collective-permute-start.31 = (bf16[200,256]{1,0:T(8,128)(2,1)S(1)}, bf16[200,256]{1,0:T(8,128)(2,1)S(1)}, u32[]{:S(2)}, u32[]{:S(2)}) collective-permute-start(bf16[200,256]{1,0:T(8,128)(2,1)S(1)} %collective-permute-done.29.refs_5_), channel_id=1, source_target_pairs={{0,8},{8,16},{16,24},{24,28},{28,20},{20,12},{12,4},{4,0},{1,9},{9... | collective-permute-start | bytes 307208 | tf_op jit(solution)/shard_map/ppermute | solution.py:814
  177.4 5.5 %collective-permute-start.32 = (bf16[200,256]{1,0:T(8,128)(2,1)S(1)}, bf16[200,256]{1,0:T(8,128)(2,1)S(1)}, u32[]{:S(2)}, u32[]{:S(2)}) collective-permute-start(bf16[200,256]{1,0:T(8,128)(2,1)S(1)} %collective-permute-done.30.refs_6_), channel_id=1, source_target_pairs={{8,0},{16,8},{24,16},{28,24},{20,28},{12,20},{4,12},{0,4},{9,1},{1... | collective-permute-start | bytes 307208 | tf_op jit(solution)/shard_map/ppermute | solution.py:814
  (93 other events, 815.4 us)
